TPU v7x, 32 devices: a whole 2x2x4 slice. The times are simulated.
32 devices in a mesh: member: 4 (over z), lat: 8 (over y, x, core).
Axes of the slice: x: 2, y: 2, z: 4, core: 2. Of those that a mesh axis runs over, the one named last changes fastest.
Arguments:
- grid_input: bfloat16 [4, 384, 768, 256], P('member', 'lat'), may hold values from -6 to 6
- saved_mixed: bfloat16 [4, 384, 768, 256], P('member', 'lat'), may hold values from -6 to 6
- target: bfloat16 [384, 768, 256], P('lat'), may hold values from -6 to 6
- land_weight: int32 [384, 768], P('lat'), may hold values from 0 to 3
- mix_weight: bfloat16 [256, 256], replicated, may hold values from -0.375 to 0.375
- degree_gain: float32 [384], replicated, may hold values from 0.3 to 3
- up_weight: bfloat16 [256, 512], replicated, may hold values from -0.375 to 0.375
- down_weight: bfloat16 [512, 256], replicated, may hold values from -0.25 to 0.25
Outputs:
- grad_input: bfloat16 [4, 384, 768, 256], P('member', 'lat')
All inputs are finite; a program needn't handle non-finite values.
Results may differ from a plain program's by a relative error of at most 0.015.
Values may be sent and summed in bfloat16 or wider, within the bound.
No kernel may reach another device: no remote copies, remote signals or barrier semaphores. Data moves between devices by JAX's collectives and lax.ppermute only.
A program may use at most 320 MiB of HBM per device.

v0:
```python
import math

import jax
import jax.numpy as jnp
from jax import lax
from jax.sharding import PartitionSpec as P

kappa_gelu = 0.7978845608
cubic_gelu = 0.044715
smooth_square = 0.25


def gelu_parts(inputs):
    tanh_part = jnp.tanh(kappa_gelu * (inputs + cubic_gelu * inputs * inputs * inputs))
    values = 0.5 * inputs * (1.0 + tanh_part)
    slopes = 0.5 * (1.0 + tanh_part) + 0.5 * inputs * (1.0 - tanh_part * tanh_part) * kappa_gelu * (
        1.0 + 3.0 * cubic_gelu * inputs * inputs
    )
    return (values, slopes)


def slope_abs(difference):
    return difference * lax.rsqrt(difference * difference + smooth_square)


def member_term(own_values, everyone, target, weights):
    member_count = everyone.shape[0]
    total = jnp.zeros(own_values.shape, jnp.float32)
    for slot in range(member_count):
        total = total + slope_abs(own_values - everyone[slot].astype(jnp.float32))
    direct = slope_abs(own_values - target.astype(jnp.float32))
    return (weights * (direct / member_count - total / (member_count * member_count))).astype(
        jnp.bfloat16
    )


def fourier_tables(lon_count, mode_count):
    positions = jnp.arange(lon_count)
    orders = jnp.arange(mode_count)
    phase = positions[:, None] * orders[None, :] % lon_count
    angle_grid = phase.astype(jnp.float32) * (2.0 * math.pi / lon_count)
    cosine = jnp.cos(angle_grid)
    sine = jnp.sin(angle_grid)
    factor = jnp.where(orders == 0, 1.0, 2.0).astype(jnp.float32)
    synth_table = jnp.concatenate(
        [cosine * factor[None, :], -sine * factor[None, :]], axis=1
    ).astype(jnp.bfloat16)
    analysis_table = jnp.concatenate([cosine.T, -sine.T], axis=0).astype(jnp.bfloat16)
    return (synth_table, analysis_table)


def legendre_table(orders, lat_count, degree_count):
    angles = (jnp.arange(lat_count).astype(jnp.float32) + 0.5) * (math.pi / lat_count)
    cosine = jnp.cos(angles)
    sine = jnp.sin(angles)
    order_f = orders.astype(jnp.float32)[:, None]
    factor_index = jnp.arange(1, lat_count + 1).astype(jnp.float32)
    ratios = jnp.log((2.0 * factor_index - 1.0) / (2.0 * factor_index))
    partial_log = jnp.sum(jnp.where(factor_index[None, :] <= order_f, ratios[None, :], 0.0), axis=1)
    start_log = (
        0.5 * jnp.log(order_f + 0.5) + 0.5 * partial_log[:, None] + order_f * jnp.log(sine)[None, :]
    )
    zeros_start = jnp.zeros((orders.shape[0], lat_count), jnp.float32)

    def advance(state, degree):
        older, newer, log_scale = state
        degree_f = degree.astype(jnp.float32)
        alpha_rec = jnp.sqrt(
            jnp.maximum(4.0 * degree_f * degree_f - 1.0, 1.0)
            / jnp.maximum(degree_f * degree_f - order_f * order_f, 1.0)
        )
        below = degree_f - 1.0
        beta_rec = jnp.sqrt(
            jnp.maximum(below * below - order_f * order_f, 0.0)
            / jnp.maximum(4.0 * below * below - 1.0, 1.0)
        )
        recurred = alpha_rec * (cosine[None, :] * newer - beta_rec * older)
        fresh = jnp.where(degree_f < order_f, 0.0, jnp.where(degree_f == order_f, 1.0, recurred))
        output = fresh * jnp.exp(log_scale)
        norm_value = jnp.where(degree_f < order_f, 1.0, jnp.maximum(jnp.abs(fresh), jnp.abs(newer)))
        return ((newer / norm_value, fresh / norm_value, log_scale + jnp.log(norm_value)), output)

    block_size = math.gcd(degree_count, 32)

    def advance_block(state, block_start):
        rows_out = []
        for offset in range(block_size):
            state, output = advance(state, block_start + offset)
            rows_out.append(output)
        return (state, jnp.stack(rows_out))

    start_state = (zeros_start, zeros_start, start_log)
    block_starts = jnp.arange(degree_count // block_size) * block_size
    final_state, table_blocks = lax.scan(advance_block, start_state, block_starts)
    return table_blocks.reshape(degree_count, orders.shape[0], lat_count)


def shards(
    grid_input, saved_mixed, target, land_weight, mix_weight, degree_gain, up_weight, down_weight
):
    rows_lat = grid_input.shape[1]
    lon_count = grid_input.shape[2]
    channel_count = grid_input.shape[3]
    total_lat = degree_gain.shape[0]
    mode_count = lon_count // 2
    local_modes = mode_count // lax.axis_size("lat")
    flat_saved = saved_mixed.reshape(rows_lat * lon_count, channel_count)
    hidden_pre = jnp.dot(flat_saved, up_weight, preferred_element_type=jnp.float32)
    values, slopes = gelu_parts(hidden_pre)
    activation = values.astype(jnp.bfloat16)
    branch_out = jnp.dot(activation, down_weight, preferred_element_type=jnp.float32)
    member_out = (grid_input.reshape(branch_out.shape).astype(jnp.float32) + branch_out).astype(
        jnp.bfloat16
    )
    member_out = member_out.reshape(rows_lat, lon_count, channel_count)
    lat_start = lax.axis_index("lat") * rows_lat
    local_angles = ((lat_start + jnp.arange(rows_lat)).astype(jnp.float32) + 0.5) * (
        math.pi / total_lat
    )
    weights = (jnp.sin(local_angles)[:, None] * land_weight.astype(jnp.float32))[:, :, None]
    everyone = lax.all_gather(member_out[None], "member", axis=0, tiled=True)
    cotangent = member_term(member_out.astype(jnp.float32), everyone, target, weights)
    act_grad = jnp.dot(
        cotangent.reshape(rows_lat * lon_count, channel_count),
        down_weight.T,
        preferred_element_type=jnp.float32,
    )
    pre_grad = (act_grad * slopes).astype(jnp.bfloat16)
    mixed_grad = jnp.dot(pre_grad, up_weight.T, preferred_element_type=jnp.float32).astype(
        jnp.bfloat16
    )
    mixed_grad = mixed_grad.reshape(rows_lat, lon_count, channel_count)
    synth_table, analysis_table = fourier_tables(lon_count, mode_count)
    wave_grad = jnp.einsum(
        "jnc,nk->jkc", mixed_grad, synth_table, preferred_element_type=jnp.float32
    ).astype(jnp.bfloat16)
    wave_grad = wave_grad.reshape(rows_lat, 2, mode_count, channel_count)
    wave_all = lax.all_to_all(wave_grad, "lat", split_axis=2, concat_axis=0, tiled=True)
    local_orders = lax.axis_index("lat") * local_modes + jnp.arange(local_modes)
    legendre = legendre_table(local_orders, total_lat, total_lat).astype(jnp.bfloat16)
    all_angles = (jnp.arange(total_lat).astype(jnp.float32) + 0.5) * (math.pi / total_lat)
    quad_weight = jnp.sin(all_angles) * (math.pi / total_lat)
    degree_grad = jnp.einsum(
        "lmj,jpmc->lpmc", legendre, wave_all, preferred_element_type=jnp.float32
    )
    gained = (degree_grad * degree_gain[:, None, None, None]).astype(jnp.bfloat16)
    coeff_grad = jnp.einsum(
        "lpmd,cd->lpmc", gained, mix_weight, preferred_element_type=jnp.float32
    ).astype(jnp.bfloat16)
    lat_grad = (
        jnp.einsum("lmj,lpmc->jpmc", legendre, coeff_grad, preferred_element_type=jnp.float32)
        * quad_weight[:, None, None, None]
    )
    lat_grad = lat_grad.astype(jnp.bfloat16)
    returned = lax.all_to_all(lat_grad, "lat", split_axis=0, concat_axis=2, tiled=True)
    spatial = jnp.einsum(
        "jkc,kn->jnc",
        returned.reshape(rows_lat, 2 * mode_count, channel_count),
        analysis_table,
        preferred_element_type=jnp.float32,
    ) * (1.0 / lon_count)
    grad_input = (cotangent.astype(jnp.float32) + spatial).astype(jnp.bfloat16)
    return grad_input[None]


def solution(mesh):
    in_specs = (
        P("member", "lat", None, None),
        P("member", "lat", None, None),
        P("lat", None, None),
        P("lat", None),
        P(),
        P(),
        P(),
        P(),
    )
    out_specs = P("member", "lat", None, None)
    return jax.shard_map(shards, mesh=mesh, in_specs=in_specs, out_specs=out_specs, check_vma=False)
```

profile of v0, /device:TPU:0, one launch (start us, length us, event | category | flops | bytes accessed | tf_op | source)
XLA Modules:
  0.0 2303.3 jit_solution(13692154080503595529)
XLA Ops:
  6.5 0.9 copy-done
  7.5 32.2 %fusion.73 = f32[36864,512]{1,0:T(8,128)} fusion(bf16[36864,256]{1,0:T(8,128)(2,1)} %bitcast.708, bf16[256,512]{1,0:T(8,128)(2,1)S(1)} %copy-done), kind=kOutput, calls=%fused_computation.359 | convolution fusion | flops 9663676416 | bytes 94633984 | tf_op jit(solution)/shard_map/dot_general | solution.py:108
  39.7 43.3 %fusion.18 = bf16[36864,256]{1,0:T(8,128)(2,1)} fusion(bf16[512,256]{1,0:T(8,128)(2,1)S(1)} %copy-done.8, bf16[36864,256]{1,0:T(8,128)(2,1)} %bitcast.714, f32[36864,512]{1,0:T(8,128)} %fusion.73), kind=kOutput, calls=%fused_computation.286 | convolution fusion | flops 9861857280 | bytes 113508352 | tf_op jit(solution)/shard_map/dot_general | solution.py:111
  83.2 0.5 iota_multiply_fusion
  84.0 0.7 multiply_add_fusion.1
  84.8 5.8 multiply_convert_fusion.6
  90.6 1244.4 %all-gather.2.cloned.1.call-done = bf16[4,48,768,256]{3,2,1,0:T(8,128)(2,1)} async-done(((bf16[1,48,768,256]{3,2,1,0:T(8,128)(2,1)}), bf16[4,48,768,256]{3,2,1,0:T(8,128)(2,1)}) %all-gather.2.cloned.1.call-update) | async-done | bytes 75497488 | tf_op jit(solution)/shard_map/all_gather | solution.py:121
  1335.0 51.6 %multiply_convert_fusion.3 = bf16[48,768,256]{2,1,0:T(8,128)(2,1)} fusion(bf16[48,768,256]{2,1,0:T(8,128)(2,1)} %bitcast.704, bf16[48,768,256]{2,1,0:T(8,128)(2,1)} %param.12, bf16[4,48,768,256]{3,2,1,0:T(8,128)(2,1)} %all-gather.2.cloned.1.call-done, f32[48,768]{1,0:T(8,128)S(1)} %convert_multiply_fusion.1), kind=kLoop, calls=%fused_computation.291 | loop fusion | flops 320864256 | bytes 132268032 | tf_op jit(solution)/shard_map/convert_element_type | solution.py:32
  1386.6 57.9 %convolution_convert_fusion = bf16[36864,256]{1,0:T(8,128)(2,1)} fusion(bf16[256,512]{1,0:T(8,128)(2,1)S(1)} %copy-done, f32[36864,512]{1,0:T(8,128)} %fusion.73, bf16[36864,256]{1,0:T(8,128)(2,1)} %bitcast.709, bf16[512,256]{1,0:T(8,128)(2,1)S(1)} %copy-done.8), kind=kOutput, calls=%fused_computation.285 | convolution fusion | flops 19695403008 | bytes 113770496 | tf_op jit(solution)/shard_map/dot_general | solution.py:129
  1444.5 24.5 %convolution_convert_fusion.1 = bf16[768,48,256]{2,0,1:T(8,128)(2,1)} fusion(bf16[48,768,256]{2,1,0:T(8,128)(2,1)} %bitcast.715, bf16[768,384]{0,1:T(8,128)(2,1)S(1)} %copy-done.6, bf16[768,384]{0,1:T(8,128)(2,1)S(1)} %copy-done.5), kind=kOutput, calls=%fused_computation.307 | convolution fusion | flops 14507311104 | bytes 38928384 | tf_op jit(solution)/shard_map/jnc,nk->jkc/dot_general | solution.py:134
  1469.0 34.8 %copy.22 = bf16[48,2,384,256]{3,1,0,2:T(2,128)(2,1)} copy(bf16[48,2,384,256]{3,2,1,0:T(8,128)(2,1)} %bitcast.711) | data formatting | bytes 37748736 | tf_op jit(solution)/shard_map/reshape | solution.py:137
  1503.9 6.2 all-to-all-start
  1510.1 347.0 %while.23 = (s32[]{:T(128)}, f32[48,384]{1,0:T(8,128)S(1)}, f32[48,384]{1,0:T(8,128)S(1)}, f32[48,384]{1,0:T(8,128)S(1)}, bf16[12,32,48,384]{3,2,1,0:T(8,128)(2,...) while((s32[]{:T(128)}, f32[48,384]{1,0:T(8,128)S(1)}, ...), condition=%wide.region_2.3_spmd.clone.clone.clone.clone, body=%wide.region_1.2_spmd.clone.clone.clone.clone.sunk | while | flops 11725857 | bytes 20309012 | solution.py:94
  1510.2 0.7 dynamic_slice.13
  1513.2 0.2 bitcast_dynamic-update-slice_fusion.68
  1514.8 0.3 bitcast_dynamic-update-slice_fusion.69
  1537.9 1.1 bitcast_dynamic-update-slice_fusion.98
  1539.1 0.7 dynamic_slice.13
  1542.1 0.2 bitcast_dynamic-update-slice_fusion.68
  1543.7 0.3 bitcast_dynamic-update-slice_fusion.69
  1566.8 1.2 bitcast_dynamic-update-slice_fusion.98
  1568.0 0.7 dynamic_slice.13
  1572.6 0.3 bitcast_dynamic-update-slice_fusion.69
  1595.7 1.1 bitcast_dynamic-update-slice_fusion.98
  1596.9 0.7 dynamic_slice.13
  1601.4 0.3 bitcast_dynamic-update-slice_fusion.69
  1624.6 1.2 bitcast_dynamic-update-slice_fusion.98
  1625.8 0.7 dynamic_slice.13
  1628.8 0.2 bitcast_dynamic-update-slice_fusion.68
  1630.4 0.3 bitcast_dynamic-update-slice_fusion.69
  1653.5 1.1 bitcast_dynamic-update-slice_fusion.98
  1654.7 0.7 dynamic_slice.13
  1659.3 0.3 bitcast_dynamic-update-slice_fusion.69
  1682.4 1.2 bitcast_dynamic-update-slice_fusion.98
  1683.7 0.7 dynamic_slice.13
  1686.7 0.2 bitcast_dynamic-update-slice_fusion.68
  1688.3 0.3 bitcast_dynamic-update-slice_fusion.69
  1711.4 1.2 bitcast_dynamic-update-slice_fusion.98
  1712.6 0.7 dynamic_slice.13
  1717.2 0.3 bitcast_dynamic-update-slice_fusion.69
  1740.3 1.1 bitcast_dynamic-update-slice_fusion.98
  1741.5 0.7 dynamic_slice.13
  1746.1 0.3 bitcast_dynamic-update-slice_fusion.69
  1769.2 1.1 bitcast_dynamic-update-slice_fusion.98
  1770.4 0.7 dynamic_slice.13
  1775.0 0.3 bitcast_dynamic-update-slice_fusion.69
  1798.1 1.2 bitcast_dynamic-update-slice_fusion.98
  1799.3 0.7 dynamic_slice.13
  1803.9 0.3 bitcast_dynamic-update-slice_fusion.69
  1827.1 1.1 bitcast_dynamic-update-slice_fusion.98
  1828.2 0.7 dynamic_slice.13
  1832.8 0.3 bitcast_dynamic-update-slice_fusion.69
  1856.0 1.2 bitcast_dynamic-update-slice_fusion.98
  1857.2 17.3 copy.23
  1874.5 6.9 copy.24
  1881.3 75.9 %fusion.25 = f32[48,2,256,384]{3,2,1,0:T(8,128)} fusion(bf16[384,2,48,256]{3,2,1,0:T(8,128)(2,1)} %bitcast.707, bf16[384,48,384,1]{2,1,0,3:T(8,128)(2,1)} %bitcast.712), kind=kOutput, calls=%fused_computation.300 | convolution fusion | flops 7247757312 | bytes 70778880 | tf_op jit(solution)/shard_map/lmj,jpmc->lpmc/dot_general | solution.py:143
  1957.3 34.1 %fusion.23 = bf16[384,2,48,256]{0,3,1,2:T(8,128)(2,1)} fusion(f32[384]{0:T(512)S(1)} %fusion.59, bf16[384,48,384,1]{2,1,0,3:T(8,128)(2,1)} %bitcast.713, f32[48,2,256,384]{3,2,1,0:T(8,128)} %fusion.25, f32[384]{0:T(512)S(1)} %copy-done.10, bf16[256,256]{1,0:T(8,128)(2,1)S(1)} %copy-done.9), kind=kOutput, calls=%fused_computation.294 | convolution fusion | flops 12126781440 | bytes 70913024 | tf_op jit(solution)/shard_map/lmj,lpmc->jpmc/dot_general | solution.py:151
  1991.4 46.7 %copy.30 = bf16[384,2,48,256]{3,1,2,0:T(2,128)(2,1)} copy(bf16[384,2,48,256]{0,3,1,2:T(8,128)(2,1)} %fusion.23) | data formatting | bytes 37748736 | tf_op jit(solution)/shard_map/convert_element_type | solution.py:154
  2038.1 5.9 all-to-all-start.1
  2044.0 5.0 negate_convert_fusion
  2049.1 201.4 %all-to-all-done.1 = bf16[384,2,48,256]{3,1,2,0:T(2,128)(2,1)} async-done(((bf16[384,2,48,256]{3,1,2,0:T(2,128)(2,1)}), bf16[384,2,48,256]{3,1,2,0:T(2,128)(2,1)}, u32[]{:S(2)}, u32[]{:S(2)}) %all-to-all-start.1) | async-done | bytes 18874400 | tf_op jit(solution)/shard_map/all_to_all | solution.py:155
  2250.4 12.8 copy.31
  2263.2 6.8 copy.32
  2270.1 25.9 %fusion.24 = bf16[1,48,768,256]{3,2,1,0:T(8,128)(2,1)} fusion(bf16[48,768,256]{2,1,0:T(8,128)(2,1)} %multiply_convert_fusion.3, bf16[48,768,256]{2,1,0:T(8,128)(2,1)} %bitcast.710, bf16[384,768]{0,1:T(8,128)(2,1)S(1)} %get-tuple-element.755, bf16[384,768]{0,1:T(8,128)(2,1)S(1)} %get-tuple-element.756), kind=kOutput, calls=%fused_computation.295 | convolution fusion | flops 14535622656 | bytes 57802752 | tf_op jit(solution)/shard_map/jkc,kn->jnc/dot_general | solution.py:156
  (1199 shorter events, 63.9 us)
Async XLA Ops:
  6.5 1.0 copy-start
  6.5 1328.4 %all-gather.2.cloned.1.call-start = ((), (), s32[]{:S(2)}) async-start(), calls=%async_computation.2 | async-start | bytes 94371840 | tf_op jit(solution)/shard_map/all_gather | solution.py:121
  7.5 32.2 %copy-start.8 = (bf16[512,256]{1,0:T(8,128)(2,1)S(1)}, bf16[512,256]{1,0:T(8,128)(2,1)}, u32[]{:S(2)}) copy-start(bf16[512,256]{1,0:T(8,128)(2,1)} %param.17) | copy-start | bytes 786436
  83.0 1.6 copy-start.7
  1386.6 57.9 %copy-start.5 = (bf16[768,384]{0,1:T(8,128)(2,1)S(1)}, bf16[768,384]{0,1:T(8,128)(2,1)}, u32[]{:S(2)}) copy-start(bf16[768,384]{0,1:T(8,128)(2,1)} %get-tuple-element.753) | copy-start | bytes 1769476
  1386.6 57.9 %copy-start.6 = (bf16[768,384]{0,1:T(8,128)(2,1)S(1)}, bf16[768,384]{0,1:T(8,128)(2,1)}, u32[]{:S(2)}) copy-start(bf16[768,384]{0,1:T(8,128)(2,1)} %get-tuple-element.754) | copy-start | bytes 1769476
  1503.9 6.2 copy-start.2
  1503.9 6.2 copy-start.3
  1503.9 6.3 copy-start.4
  1503.9 6.3 copy-start.11
  1503.9 353.3 %all-to-all-start = ((bf16[48,2,384,256]{3,1,0,2:T(2,128)(2,1)}), bf16[48,2,384,256]{3,1,0,2:T(2,128)(2,1)}, u32[]{:S(2)}, u32[]{:S(2)}) async-start(bf16[48,2,384,256]{3,1,0,2:T(2,128)(2,1)} %copy.22), calls=%async_computation | async-start | bytes 37748736 | tf_op jit(solution)/shard_map/all_to_all | solution.py:138
  1881.3 76.0 %copy-start.9 = (bf16[256,256]{1,0:T(8,128)(2,1)S(1)}, bf16[256,256]{1,0:T(8,128)(2,1)}, u32[]{:S(2)}) copy-start(bf16[256,256]{1,0:T(8,128)(2,1)} %param.14) | copy-start | bytes 393220
  1881.3 76.0 %copy-start.10 = (f32[384]{0:T(512)S(1)}, f32[384]{0:T(512)}, u32[]{:S(2)}) copy-start(f32[384]{0:T(512)} %param.15) | copy-start | bytes 4612
  2038.1 212.3 %all-to-all-start.1 = ((bf16[384,2,48,256]{3,1,2,0:T(2,128)(2,1)}), bf16[384,2,48,256]{3,1,2,0:T(2,128)(2,1)}, u32[]{:S(2)}, u32[]{:S(2)}) async-start(bf16[384,2,48,256]{3,1,2,0:T(2,128)(2,1)} %copy.30), calls=%async_computation.1 | async-start | bytes 37748736 | tf_op jit(solution)/shard_map/all_to_all | solution.py:155
  2270.1 25.9 %copy-start.1 = (bf16[256,512]{1,0:T(8,128)(2,1)S(1)}, bf16[256,512]{1,0:T(8,128)(2,1)}, u32[]{:S(2)}) copy-start(bf16[256,512]{1,0:T(8,128)(2,1)} %param.16) | copy-start | bytes 786436
Sparse Core Ops, SparseCore 0:
  83.2 1251.7 all-gather.1
where the time goes:
time: 2320 us; the launch traced here: 2300 us
  waiting for transfers between devices  1450 us (62%)
  matrix products  294 us (13%)
  loops' own time  258 us (11%)
  local copies, waits for them, and re-layouts  148 us (6%)
  other arithmetic  132 us (6%)
    all_gather x1, waiting for transfers between devices, shards(): everyone = lax.all_gather(member_out[None], 'member', axis=0, tiled=True)  1240 us
    another operation x1, loops' own time, legendre_table(): lax.scan(advance_block, start_state, block_starts)  258 us
    all_to_all x1, waiting for transfers between devices, shards(): lax.all_to_all(lat_grad, 'lat', split_axis=0, concat_axis=2, tiled=True)  201 us
    dot_general x1, matrix products, shards(): jnp.einsum('lmj,jpmc->lpmc', legendre, wave_all, preferred_element_type=j...  75.9 us
    dot_general x1, matrix products, shards(): jnp.dot(pre_grad, up_weight.T, preferred_element_type=jnp.float32)  57.9 us
    while x372, other arithmetic  54.4 us
    convert_element_type x1, other arithmetic, member_term(): (weights * (direct / member_count - total / (member_count * member_count)...  51.6 us
    convert_element_type x1, local copies, waits for them, and re-layouts, shards(): lat_grad = lat_grad.astype(jnp.bfloat16)  46.7 us
  transfers between devices with their start and end apart: 3, of which 2 were waited for; matrix products, arithmetic and copies ran while one was open for 4% of the time, Pallas kernels for 0%

commit v1 on v0

v1 whole, which is shorter than its diff:
```python
import functools
import math

import jax
import jax.numpy as jnp
from jax import lax
from jax.experimental import pallas as pl
from jax.experimental.pallas import tpu as pltpu
from jax.sharding import PartitionSpec as P

kappa_gelu = 0.7978845608
cubic_gelu = 0.044715
smooth_square = 0.25
F32 = jnp.float32
BF16 = jnp.bfloat16
PARAMS = pltpu.CompilerParams(vmem_limit_bytes=48 * 1024 * 1024)


TOKEN = jax.ShapeDtypeStruct((8, 128), F32)
TOKEN_IN = pl.BlockSpec(memory_space=pl.ANY)
TOKEN_OUT = pl.BlockSpec((8, 128), lambda *_: (0, 0))


def put_token(token_ref):
    token_ref[...] = jnp.zeros_like(token_ref)


def dot(a, b):
    return jnp.dot(a, b, preferred_element_type=F32)


def slope_abs(difference):
    return difference * lax.rsqrt(difference * difference + smooth_square)


def fourier_tables(lon_count, mode_count):
    row = jnp.arange(2 * mode_count)
    part = row // mode_count
    orders = row % mode_count
    positions = jnp.arange(lon_count)
    phase = orders[:, None] * positions[None, :] % lon_count
    angle_grid = phase.astype(F32) * (2.0 * math.pi / lon_count)
    values = jnp.where(part[:, None] == 0, jnp.cos(angle_grid), -jnp.sin(angle_grid))
    factor = jnp.where(orders == 0, 1.0, 2.0).astype(F32)
    synth = (values * factor[:, None]).astype(BF16)
    return synth, values.T.astype(BF16)


def legendre_kernel(
    start_ref, cosine_ref, order_ref, _, out_ref, token_ref, older_ref, newer_ref, log_ref, rows_ref
):
    put_token(token_ref)
    block = out_ref.shape[1]
    order = order_ref[...]
    cosine = cosine_ref[...]

    @pl.when(pl.program_id(0) == 0)
    def _():
        older_ref[...] = jnp.zeros_like(older_ref)
        newer_ref[...] = jnp.zeros_like(newer_ref)
        log_ref[...] = start_ref[...]

    for offset in range(block):
        degree = (pl.program_id(0) * block + offset).astype(F32)
        below = degree - 1.0
        alpha = jnp.sqrt(
            jnp.maximum(4.0 * degree * degree - 1.0, 1.0)
            / jnp.maximum(degree * degree - order * order, 1.0)
        )
        beta = jnp.sqrt(
            jnp.maximum(below * below - order * order, 0.0)
            / jnp.maximum(4.0 * below * below - 1.0, 1.0)
        )
        newer = newer_ref[...]
        log_scale = log_ref[...]
        recurred = alpha * (cosine * newer - beta * older_ref[...])
        fresh = jnp.where(degree < order, 0.0, jnp.where(degree == order, 1.0, recurred))
        rows_ref[:, offset, :] = fresh * jnp.exp(log_scale)
        norm = jnp.where(degree < order, 1.0, jnp.maximum(jnp.abs(fresh), jnp.abs(newer)))
        older_ref[...] = newer / norm
        newer_ref[...] = fresh / norm
        log_ref[...] = log_scale + jnp.log(norm)
    out_ref[...] = rows_ref[...].astype(BF16)


def legendre_table(token, orders, angles, degree_count):
    lat_count = angles.shape[0]
    order_count = orders.shape[0]
    order_f = orders.astype(F32)[:, None]
    factor_index = jnp.arange(1, lat_count + 1).astype(F32)
    ratios = jnp.log((2.0 * factor_index - 1.0) / (2.0 * factor_index))
    partial_log = jnp.sum(jnp.where(factor_index[None, :] <= order_f, ratios[None, :], 0.0), axis=1)
    start_log = (
        0.5 * jnp.log(order_f + 0.5)
        + 0.5 * partial_log[:, None]
        + order_f * jnp.log(jnp.sin(angles))[None, :]
    )
    block = math.gcd(degree_count, 16)
    state = pltpu.VMEM((order_count, lat_count), F32)
    return pl.pallas_call(
        legendre_kernel,
        grid=(degree_count // block,),
        in_specs=[
            pl.BlockSpec((order_count, lat_count), lambda i: (0, 0)),
            pl.BlockSpec((1, lat_count), lambda i: (0, 0)),
            pl.BlockSpec((order_count, 1), lambda i: (0, 0)),
            TOKEN_IN,
        ],
        out_specs=[
            pl.BlockSpec((order_count, block, lat_count), lambda i: (0, i, 0)),
            TOKEN_OUT,
        ],
        out_shape=[
            jax.ShapeDtypeStruct((order_count, degree_count, lat_count), BF16),
            TOKEN,
        ],
        scratch_shapes=[state, state, state, pltpu.VMEM((order_count, block, lat_count), F32)],
        compiler_params=PARAMS,
        cost_estimate=pl.CostEstimate(
            flops=40 * order_count * degree_count * lat_count,
            bytes_accessed=2 * order_count * degree_count * lat_count,
            transcendentals=4 * order_count * degree_count * lat_count,
        ),
    )(start_log, jnp.cos(angles)[None, :], order_f, token)


def share_of(me_ref, piece, members, share):
    return pl.ds(pl.multiple_of(lax.rem(me_ref[0] + piece, members) * share, share), share)


def forward_kernel(me_ref, saved_ref, grid_ref, up_ref, down_ref, _, *out_refs):
    put_token(out_refs[-1])
    out_refs = out_refs[:-1]
    members = len(out_refs)
    share = out_refs[0].shape[1]
    for piece in range(members):
        place = share_of(me_ref, piece, members, share)
        v = dot(saved_ref[0, place, :], up_ref[...])
        tanh_part = jnp.tanh(kappa_gelu * (v + cubic_gelu * v * v * v))
        activation = (0.5 * v * (1.0 + tanh_part)).astype(BF16)
        total = grid_ref[0, place, :].astype(F32) + dot(activation, down_ref[...])
        out_refs[piece][0] = total.astype(BF16)


def forward_rows(token, first, rows, members, me, saved, grid_input, up_weight, down_weight):
    _, lon, channels = saved.shape
    hidden = up_weight.shape[1]
    share = lon // members
    row_spec = pl.BlockSpec((1, lon, channels), lambda i, q: (first + i, 0, 0))
    piece_spec = pl.BlockSpec((1, share, channels), lambda i, q: (i, 0, 0))
    return pl.pallas_call(
        forward_kernel,
        grid_spec=pltpu.PrefetchScalarGridSpec(
            num_scalar_prefetch=1,
            grid=(rows,),
            in_specs=[
                row_spec,
                row_spec,
                pl.BlockSpec((channels, hidden), lambda i, q: (0, 0)),
                pl.BlockSpec((hidden, channels), lambda i, q: (0, 0)),
                TOKEN_IN,
            ],
            out_specs=[piece_spec] * members + [TOKEN_OUT],
        ),
        out_shape=[jax.ShapeDtypeStruct((rows, share, channels), BF16)] * members + [TOKEN],
        compiler_params=PARAMS,
        cost_estimate=pl.CostEstimate(
            flops=4 * rows * lon * channels * hidden,
            bytes_accessed=6 * rows * lon * channels,
            transcendentals=rows * lon * hidden,
        ),
    )(me, saved, grid_input, up_weight, down_weight, token)


def cotangent_kernel(first, members, me_ref, target_ref, weight_ref, _, *refs):
    put_token(refs[-1])
    row = first + pl.program_id(0)
    weight_block = weight_ref[...]
    lane = lax.broadcasted_iota(jnp.int32, weight_block.shape, 1)
    weight = jnp.sum(jnp.where(lane == row, weight_block, 0.0), axis=1, keepdims=True)
    target = target_ref[0].astype(F32)
    values = [refs[e][0].astype(F32) for e in range(members)]
    pairs = {}
    for e in range(members):
        for f in range(e + 1, members):
            pairs[e, f] = slope_abs(values[e] - values[f])
    for e in range(members):
        total = None
        for f in range(members):
            if f == e:
                continue
            term = pairs[e, f] if e < f else -pairs[f, e]
            total = term if total is None else total + term
        direct = slope_abs(values[e] - target)
        refs[members + e][0] = (
            weight * (direct * (1.0 / members) - total * (1.0 / (members * members)))
        ).astype(BF16)


def cotangent_rows(token, first, me, pieces, target, weights):
    members = len(pieces)
    rows, share, channels = pieces[0].shape
    piece_spec = pl.BlockSpec((1, share, channels), lambda i, q: (i, 0, 0))
    return pl.pallas_call(
        functools.partial(cotangent_kernel, first, members),
        grid_spec=pltpu.PrefetchScalarGridSpec(
            num_scalar_prefetch=1,
            grid=(rows,),
            in_specs=[
                pl.BlockSpec((1, share, channels), lambda i, q: (first + i, q[0], 0)),
                pl.BlockSpec((share, weights.shape[1]), lambda i, q: (q[0], 0)),
                TOKEN_IN,
            ]
            + [piece_spec] * members,
            out_specs=[piece_spec] * members + [TOKEN_OUT],
        ),
        out_shape=[jax.ShapeDtypeStruct(pieces[0].shape, BF16)] * members + [TOKEN],
        compiler_params=PARAMS,
        cost_estimate=pl.CostEstimate(
            flops=80 * rows * share * channels,
            bytes_accessed=(4 * members + 2) * rows * share * channels,
            transcendentals=10 * rows * share * channels,
        ),
    )(me, target, weights, token, *pieces)


def backward_kernel(me_ref, saved_ref, up_ref, down_t_ref, up_t_ref, synth_ref, _, __, *refs):
    members = len(refs) - 4
    out_ref, token_ref, mixed_ref, waves_ref = refs[members:]
    put_token(token_ref)
    lon, channels = mixed_ref.shape
    share = lon // members
    for piece in range(members):
        place = share_of(me_ref, piece, members, share)
        v = dot(saved_ref[0, place, :], up_ref[...])
        square = v * v
        t = jnp.tanh(kappa_gelu * (v + cubic_gelu * square * v))
        slopes = 0.5 * (1.0 + t) + 0.5 * v * (1.0 - t * t) * kappa_gelu * (
            1.0 + 3.0 * cubic_gelu * square
        )
        act_grad = dot(refs[piece][0], down_t_ref[...])
        pre_grad = (act_grad * slopes).astype(BF16)
        mixed_ref[place, :] = dot(pre_grad, up_t_ref[...]).astype(BF16)
    wave = dot(synth_ref[...], mixed_ref[...])
    modes = wave.shape[0] // 2
    row = pl.program_id(0)
    waves_ref[:, row, :channels] = wave[:modes]
    waves_ref[:, row, channels:] = wave[modes:]

    @pl.when(row == pl.num_programs(0) - 1)
    def _():
        out_ref[...] = waves_ref[...].astype(BF16).reshape(out_ref.shape)


def backward_rows(token, ahead, first, groups, me, cot, saved, up_weight, down_t, up_t, synth):
    members = len(cot)
    rows, share, channels = cot[0].shape
    lon = saved.shape[1]
    hidden = up_weight.shape[1]
    modes = synth.shape[0] // 2
    whole = lambda a: pl.BlockSpec(a.shape, lambda i, q: (0, 0))
    piece_spec = pl.BlockSpec((1, share, channels), lambda i, q: (i, 0, 0))
    out_shape = (groups, modes // groups, rows, 2 * channels)
    return pl.pallas_call(
        backward_kernel,
        grid_spec=pltpu.PrefetchScalarGridSpec(
            num_scalar_prefetch=1,
            grid=(rows,),
            in_specs=[
                pl.BlockSpec((1, lon, channels), lambda i, q: (first + i, 0, 0)),
                whole(up_weight),
                whole(down_t),
                whole(up_t),
                whole(synth),
                TOKEN_IN,
                TOKEN_IN,
            ]
            + [piece_spec] * members,
            out_specs=[pl.BlockSpec(out_shape, lambda i, q: (0, 0, 0, 0)), TOKEN_OUT],
            scratch_shapes=[
                pltpu.VMEM((lon, channels), BF16),
                pltpu.VMEM((modes, rows, 2 * channels), F32),
            ],
        ),
        out_shape=[jax.ShapeDtypeStruct(out_shape, BF16), TOKEN],
        compiler_params=PARAMS,
        cost_estimate=pl.CostEstimate(
            flops=rows * lon * channels * (6 * hidden + 4 * modes),
            bytes_accessed=6 * rows * lon * channels,
            transcendentals=rows * lon * hidden,
        ),
    )(me, saved, up_weight, down_t, up_t, synth, token, ahead, *cot)


def spectral_kernel(parts, table_ref, gain_ref, mix_t_ref, _, *refs):
    out_ref, token_ref = refs[parts:]
    put_token(token_ref)
    channels = mix_t_ref.shape[0]
    batch, columns = refs[0].shape[1], refs[0].shape[-1]
    for m in range(batch):
        pieces = [refs[p][:, m].astype(F32).reshape(-1, columns) for p in range(parts)]
        wave = jnp.concatenate(pieces, axis=0).astype(BF16)
        gained = (dot(table_ref[m], wave) * gain_ref[...]).astype(BF16)
        out_ref[m, :, :channels] = dot(gained[:, :channels], mix_t_ref[...]).astype(BF16)
        out_ref[m, :, channels:] = dot(gained[:, channels:], mix_t_ref[...]).astype(BF16)


def spectral(token, table, gain, mix_t, waves):
    parts = len(waves)
    groups, modes, rows, columns = waves[0].shape
    degrees, lats = table.shape[1:]
    batch = math.gcd(modes, 4)
    return pl.pallas_call(
        functools.partial(spectral_kernel, parts),
        grid=(modes // batch,),
        in_specs=[
            pl.BlockSpec((batch, degrees, lats), lambda m: (m, 0, 0)),
            pl.BlockSpec(gain.shape, lambda m: (0, 0)),
            pl.BlockSpec(mix_t.shape, lambda m: (0, 0)),
            TOKEN_IN,
        ]
        + [pl.BlockSpec((groups, batch, rows, columns), lambda m: (0, m, 0, 0))] * parts,
        out_specs=[pl.BlockSpec((batch, degrees, columns), lambda m: (m, 0, 0)), TOKEN_OUT],
        out_shape=[jax.ShapeDtypeStruct((modes, degrees, columns), BF16), TOKEN],
        compiler_params=PARAMS,
        cost_estimate=pl.CostEstimate(
            flops=modes * columns * degrees * (2 * lats + columns),
            bytes_accessed=modes * (2 * lats * degrees + 2 * columns * (lats + degrees)),
            transcendentals=0,
        ),
    )(table, gain, mix_t, token, *waves)


def latitude_kernel(joined, table_ref, quad_ref, coeff_ref, _, out_ref, token_ref):
    put_token(token_ref)
    groups, batch, rows, columns = out_ref.shape
    for m in range(batch):
        lat = lax.dot_general(
            table_ref[m], coeff_ref[m], (((0,), (0,)), ((), ())), preferred_element_type=F32
        )
        lat = (lat * quad_ref[...]).reshape(joined, groups, rows // joined, columns)
        out_ref[:, m] = jnp.concatenate([lat[p] for p in range(joined)], axis=1).astype(BF16)


def latitude_rows(token, index, joined, groups, table, quad, coeff):
    modes, degrees, columns = coeff.shape
    lats = quad.shape[0]
    batch = math.gcd(modes, 4)
    out_shape = (groups, modes, lats // groups, columns)
    return pl.pallas_call(
        functools.partial(latitude_kernel, joined),
        grid=(modes // batch,),
        in_specs=[
            pl.BlockSpec((batch, degrees, lats), lambda m: (m, 0, index)),
            pl.BlockSpec(quad.shape, lambda m: (0, 0)),
            pl.BlockSpec((batch, degrees, columns), lambda m: (m, 0, 0)),
            TOKEN_IN,
        ],
        out_specs=[
            pl.BlockSpec((groups, batch, lats // groups, columns), lambda m: (0, m, 0, 0)),
            TOKEN_OUT,
        ],
        out_shape=[jax.ShapeDtypeStruct(out_shape, BF16), TOKEN],
        compiler_params=PARAMS,
        cost_estimate=pl.CostEstimate(
            flops=2 * modes * columns * degrees * lats,
            bytes_accessed=2 * modes * (lats * degrees + columns * (lats + degrees)),
            transcendentals=0,
        ),
    )(table, quad, coeff, token)


def output_kernel(joined, members, scale, me_ref, wave_ref, analysis_ref, _, *refs):
    out_ref, token_ref, waves_ref = refs[-3:]
    put_token(token_ref)
    rows, share = wave_ref.shape[2] // joined, refs[0].shape[1]
    channels = out_ref.shape[-1]
    row = pl.program_id(0)

    @pl.when(row == 0)
    def _():
        waves_ref[...] = wave_ref[...].astype(F32).reshape(waves_ref.shape)

    wave = jnp.concatenate(
        [waves_ref[:, row, :channels].astype(BF16), waves_ref[:, row, channels:].astype(BF16)],
        axis=0,
    )
    for piece in range(members):
        place = share_of(me_ref, piece, members, share)
        spatial = dot(analysis_ref[place, :], wave)
        cot = refs[piece][0]
        for part in range(1, joined):
            cot = jnp.where(row >= part * rows, refs[part * members + piece][0], cot)
        out_ref[0, 0, place, :] = (cot.astype(F32) + spatial * scale).astype(BF16)


def output_rows(token, index, shape, me, wave, cots, analysis, held):
    groups, modes, rows, columns = wave.shape
    joined, members = len(cots), len(cots[0])
    each, share, channels = cots[0][0].shape
    lon = shape[2]
    in_specs = [
        pl.BlockSpec(wave.shape, lambda i, q: (0, 0, 0, 0)),
        pl.BlockSpec(analysis.shape, lambda i, q: (0, 0)),
        TOKEN_IN,
    ]
    operands = [me, wave, analysis, token]
    for part, cot in enumerate(cots):
        place = lambda i, q, part=part: (jnp.clip(i - part * each, 0, each - 1), 0, 0)
        in_specs += [pl.BlockSpec((1, share, channels), place)] * members
        operands += cot
    aliases = {}
    if held is not None:
        in_specs.append(pl.BlockSpec(memory_space=pl.ANY))
        aliases = {len(operands): 0}
        operands.append(held)
    return pl.pallas_call(
        functools.partial(output_kernel, joined, members, 1.0 / lon),
        grid_spec=pltpu.PrefetchScalarGridSpec(
            num_scalar_prefetch=1,
            grid=(rows,),
            in_specs=in_specs,
            out_specs=[
                pl.BlockSpec((1, 1, lon, channels), lambda i, q: (0, index * rows + i, 0, 0)),
                TOKEN_OUT,
            ],
            scratch_shapes=[pltpu.VMEM((groups * modes, rows, columns), F32)],
        ),
        out_shape=[jax.ShapeDtypeStruct(shape, BF16), TOKEN],
        input_output_aliases=aliases,
        compiler_params=PARAMS,
        cost_estimate=pl.CostEstimate(
            flops=2 * rows * lon * groups * modes * columns,
            bytes_accessed=6 * rows * lon * channels,
            transcendentals=0,
        ),
    )(*operands)


def shift(pieces, step):
    members = len(pieces)
    moved = [pieces[0]]
    for piece in range(1, members):
        pairs = [(e, (e + step * piece) % members) for e in range(members)]
        moved.append(lax.ppermute(pieces[piece], "member", pairs))
    return moved


def kernel_order(parts):
    order = [("forward", 0), ("forward", 1), ("table", 0), ("forward", 2)]
    for part in range(parts + 1):
        order += [("cotangent", part), ("backward", part - 1), ("forward", part + 3)]
    return [(kind, part) for kind, part in order if 0 <= part < parts]


def shards(
    grid_input, saved_mixed, target, land_weight, mix_weight, degree_gain, up_weight, down_weight
):
    rows_lat, lon_count, channel_count = grid_input.shape[1:]
    total_lat = degree_gain.shape[0]
    mode_count = lon_count // 2
    members = lax.axis_size("member")
    groups = lax.axis_size("lat")
    local_modes = mode_count // groups
    parts = math.gcd(rows_lat, 6)
    rows = rows_lat // parts
    starts = [part * rows for part in range(parts)]

    grid_rows = grid_input[0]
    saved_rows = saved_mixed[0]
    down_t = down_weight.T
    up_t = up_weight.T
    synth, analysis = fourier_tables(lon_count, mode_count)
    lat_start = lax.axis_index("lat") * rows_lat
    local_angles = ((lat_start + jnp.arange(rows_lat)).astype(F32) + 0.5) * (math.pi / total_lat)
    weights = (jnp.sin(local_angles)[:, None] * land_weight.astype(F32)).T
    me = lax.axis_index("member").astype(jnp.int32).reshape(1)

    lats = jnp.arange(total_lat).reshape(groups, parts, rows).swapaxes(0, 1).reshape(-1)
    angles = (lats.astype(F32) + 0.5) * (math.pi / total_lat)
    quad_weight = (jnp.sin(angles) * (math.pi / total_lat))[:, None]
    local_orders = lax.axis_index("lat") * local_modes + jnp.arange(local_modes)

    joined = 2 if parts % 2 == 0 else 1
    token = jnp.zeros(TOKEN.shape, F32)
    values, cots, waves = {}, {}, {}
    table = None
    for kind, part in kernel_order(parts):
        if kind == "table":
            table, token = legendre_table(token, local_orders, angles, total_lat)
        elif kind == "forward":
            *pieces, token = forward_rows(
                token, starts[part], rows, members, me, saved_rows, grid_rows, up_weight, down_weight
            )
            values[part] = shift(pieces, 1)
        elif kind == "cotangent":
            *pieces, token = cotangent_rows(token, starts[part], me, values[part], target, weights)
            cots[part] = shift(pieces, -1)
        else:
            wave, token = backward_rows(
                token,
                waves.get(part - 1, token),
                starts[part],
                groups,
                me,
                cots[part],
                saved_rows,
                up_weight,
                down_t,
                up_t,
                synth,
            )
            waves[part] = lax.all_to_all(wave, "lat", 0, 0, tiled=True)
    waves = [waves[part] for part in range(parts)]
    coeff, token = spectral(token, table, degree_gain[:, None], mix_weight.T, waves)
    result = None
    steps = parts // joined
    lat_waves = {}
    for step in range(steps + 1):
        if step < steps:
            quad = lax.slice_in_dim(quad_weight, step * total_lat // steps, (step + 1) * total_lat // steps)
            wave, token = latitude_rows(token, step, joined, groups, table, quad, coeff)
            lat_waves[step] = lax.all_to_all(wave, "lat", 0, 0, tiled=True)
        if step > 0:
            result, token = output_rows(
                token,
                step - 1,
                grid_input.shape,
                me,
                lat_waves[step - 1],
                [cots[part] for part in range((step - 1) * joined, step * joined)],
                analysis,
                result,
            )
    return result


def solution(mesh):
    in_specs = (
        P("member", "lat", None, None),
        P("member", "lat", None, None),
        P("lat", None, None),
        P("lat", None),
        P(),
        P(),
        P(),
        P(),
    )
    out_specs = P("member", "lat", None, None)
    return jax.shard_map(shards, mesh=mesh, in_specs=in_specs, out_specs=out_specs, check_vma=False)
```

time: 2320 us -> 1390 us (0.60)
  waiting for transfers between devices: 1450 us -> 678 us
  Pallas kernels: 0 us -> 416 us
  matrix products: 294 us -> 0 us
  loops' own time: 258 us -> 0 us
  starting transfers between devices: 12.1 us -> 172 us
  other arithmetic: 132 us -> 23 us
  local copies, waits for them, and re-layouts: 148 us -> 85.8 us
    all_gather x1 -> x0, waiting for transfers between devices: 1240 us -> none  [shards(): everyone = lax.all_gather(member_out[None], 'member', axis=0, tiled=True)]
    ppermute x0 -> x36, waiting for transfers between devices: none -> 513 us  [shift(): moved.append(lax.ppermute(pieces[piece], 'member', pairs))]
    pallas_call x0 -> x26, Pallas kernels: none -> 416 us  [the longest x6 133 us: backward_rows(): pl.pallas_call(backward_kernel, grid_spec=pltpu.PrefetchScalarGridSpec(nu...]
    dot_general x7 -> x0, matrix products: 294 us -> none  [the longest x1 75.9 us: shards(): jnp.einsum('lmj,jpmc->lpmc', legendre, wave_all, preferred_element_type=j...]
    another operation x1 -> x0, loops' own time: 258 us -> none  [legendre_table(): lax.scan(advance_block, start_state, block_starts)]
    ppermute x0 -> x36, starting transfers between devices: none -> 130 us  [shift(): moved.append(lax.ppermute(pieces[piece], 'member', pairs))]
    unnamed x24 -> x236, local copies, waits for them, and re-layouts: 0.99 us -> 85.3 us
    while x372 -> x0, other arithmetic: 54.4 us -> none
  transfers between devices with their start and end apart: 3 -> 45, of which waited for: 2 -> 21; matrix products, arithmetic and copies ran while one was open for 4% -> 2% of each run, Pallas kernels for 0% -> 15%
where the time goes in v1:
time: 1390 us; the launch traced here: 1380 us
  waiting for transfers between devices  678 us (49%)
  Pallas kernels  416 us (30%)
  starting transfers between devices  172 us (12%)
  local copies, waits for them, and re-layouts  85.8 us (6%)
  other arithmetic  23 us (2%)
    ppermute x36, waiting for transfers between devices, shift(): moved.append(lax.ppermute(pieces[piece], 'member', pairs))  513 us
    pallas_call x6, Pallas kernels, backward_rows(): pl.pallas_call(backward_kernel, grid_spec=pltpu.PrefetchScalarGridSpec(nu...  133 us
    ppermute x36, starting transfers between devices, shift(): moved.append(lax.ppermute(pieces[piece], 'member', pairs))  130 us
    all_to_all x3, waiting for transfers between devices, shards(): lat_waves[step] = lax.all_to_all(wave, 'lat', 0, 0, tiled=True)  127 us
    unnamed x236, local copies, waits for them, and re-layouts  85.3 us
    pallas_call x3, Pallas kernels, output_rows(): pl.pallas_call(functools.partial(output_kernel, joined, members, 1.0 / lo...  72.2 us
    pallas_call x6, Pallas kernels, forward_rows(): pl.pallas_call(forward_kernel, grid_spec=pltpu.PrefetchScalarGridSpec(num...  54.2 us
    pallas_call x6, Pallas kernels, cotangent_rows(): pl.pallas_call(functools.partial(cotangent_kernel, first, members), grid_...  47.7 us
  transfers between devices with their start and end apart: 45, of which 21 were waited for; matrix products, arithmetic and copies ran while one was open for 2% of the time, Pallas kernels for 15%

profile of v1, /device:TPU:0, one launch (start us, length us, event | category | flops | bytes accessed | tf_op | source)
XLA Modules:
  0.0 1375.4 jit_solution(1865262355529573896)
XLA Ops:
  1.9 9.6 shard_map.82
  11.5 3.0 collective-permute-start
  18.4 9.3 shard_map.83
  30.5 36.6 %shard_map.84 = (bf16[48,384,384]{2,1,0:T(8,128)(2,1)}, f32[8,128]{1,0:T(8,128)S(1)}) custom-call(f32[48,384]{1,0:T(8,128)S(1)} %multiply_add_fusion.start_ref, f32[1,384]{1,0:T(1,128)S(1)} %reshape.204.cosine_ref, f32[48,1]{1,0:T(8,128)S(1)} %add_convert_fusion.order_ref, f32[8,128]{1,0:T(8,128)S(1)} %get-tuple-element.93._), custom_call_target="tpu_custom_call" | custom-call | flops 283115520 | bytes 14155776 | tf_op jit(solution)/shard_map/pallas_call | solution.py:100
  69.4 8.9 shard_map.85
  81.8 2.8 collective-permute-start.5
  84.6 8.2 shard_map.86
  92.9 45.3 %collective-permute-start.6 = (bf16[8,192,256]{2,1,0:T(8,128)(2,1)S(1)}, bf16[8,192,256]{2,1,0:T(8,128)(2,1)S(1)}, u32[]{:S(2)}, u32[]{:S(2)}) collective-permute-start(bf16[8,192,256]{2,1,0:T(8,128)(2,1)S(1)} %get-tuple-element.109), channel_id=1, source_target_pairs={{0,24},{8,0},{16,8},{24,16},{1,25},{9,1},{17,9},{25,17},{2,26},{10... | collective-permute-start | bytes 2359304 | tf_op jit(solution)/shard_map/ppermute | solution.py:445
  139.1 31.2 %collective-permute-start.8 = (bf16[8,192,256]{2,1,0:T(8,128)(2,1)S(1)}, bf16[8,192,256]{2,1,0:T(8,128)(2,1)S(1)}, u32[]{:S(2)}, u32[]{:S(2)}) collective-permute-start(bf16[8,192,256]{2,1,0:T(8,128)(2,1)S(1)} %get-tuple-element.111), channel_id=1, source_target_pairs={{0,8},{8,16},{16,24},{24,0},{1,9},{9,17},{17,25},{25,1},{2,10},{10... | collective-permute-start | bytes 2359304 | tf_op jit(solution)/shard_map/ppermute | solution.py:445
  170.2 21.3 %select_convert_fusion = (bf16[768,768]{1,0:T(8,128)(2,1)}, bf16[768,768]{1,0:T(8,128)(2,1)S(1)}) fusion(s32[768]{0:T(1024)S(1)} %fusion.14, pred[768]{0:T(1024)(128)(4,1)S(1)} %fusion.20, f32[768]{0:T(1024)S(1)} %compare_select_fusion), kind=kLoop, calls=%fused_computation.6 | loop fusion | flops 14745600 | bytes 2366208 | tf_op jit(solution)/shard_map/convert_element_type | solution.py:46
  191.6 8.8 shard_map.87
  203.6 8.0 shard_map.88
  212.6 7.2 collective-permute-done.7.refs_2_
  219.8 22.3 %shard_map.89 = (bf16[8,48,8,512]{3,2,1,0:T(8,128)(2,1)}, f32[8,128]{1,0:T(8,128)S(1)}) custom-call(s32[1]{0:T(128)} %bitcast.me_ref, bf16[48,768,256]{2,1,0:T(8,128)(2,1)} %bitcast.25, bf16[256,512]{1,0:T(8,128)(2,1)S(1)} %copy-done.1, bf16[256,512]{1,0:T(8,128)(2,1)S(1)} %bitcast.8, bf16[512,256]{1,0:T(8,128)(2,1)S(1)} %bitcast.14, ...), custom_call_target="tpu_custom_call" | custom-call | flops 7247757312 | bytes 9437184 | tf_op jit(solution)/shard_map/pallas_call | solution.py:264
  243.0 4.6 all-to-all-start
  253.3 31.4 %collective-permute-done.10.refs_2_ = bf16[8,192,256]{2,1,0:T(8,128)(2,1)S(1)} collective-permute-done((bf16[8,192,256]{2,1,0:T(8,128)(2,1)}, bf16[8,192,256]{2,1,0:T(8,128)(2,1)S(1)}, u32[]{:S(2)}, u32[]{:S(2)}) %collective-permute-start.10) | collective-permute-done | bytes 786464 | tf_op jit(solution)/shard_map/ppermute | solution.py:445
  284.7 16.8 %collective-permute-start.14 = (bf16[8,192,256]{2,1,0:T(8,128)(2,1)}, bf16[8,192,256]{2,1,0:T(8,128)(2,1)S(1)}, u32[]{:S(2)}, u32[]{:S(2)}) collective-permute-start(bf16[8,192,256]{2,1,0:T(8,128)(2,1)} %copy-done.95), channel_id=1, source_target_pairs={{0,8},{8,16},{16,24},{24,0},{1,9},{9,17},{17,25},{25,1},{2,10},{10... | collective-permute-start | bytes 2359304 | tf_op jit(solution)/shard_map/ppermute | solution.py:445
  301.4 8.8 shard_map.90
  312.1 7.9 shard_map.91
  323.7 61.8 %collective-permute-done.13.refs_2_.refs_6_ = bf16[8,192,256]{2,1,0:T(8,128)(2,1)S(1)} collective-permute-done((bf16[8,192,256]{2,1,0:T(8,128)(2,1)}, bf16[8,192,256]{2,1,0:T(8,128)(2,1)S(1)}, u32[]{:S(2)}, u32[]{:S(2)}) %collective-permute-start.13) | collective-permute-done | bytes 786464 | tf_op jit(solution)/shard_map/ppermute | solution.py:445
  391.8 22.1 %shard_map.92 = (bf16[8,48,8,512]{3,2,1,0:T(8,128)(2,1)}, f32[8,128]{1,0:T(8,128)S(1)}) custom-call(s32[1]{0:T(128)} %bitcast.me_ref, bf16[48,768,256]{2,1,0:T(8,128)(2,1)} %bitcast.27, bf16[256,512]{1,0:T(8,128)(2,1)S(1)} %copy-done.1, bf16[256,512]{1,0:T(8,128)(2,1)S(1)} %bitcast.9, bf16[512,256]{1,0:T(8,128)(2,1)S(1)} %bitcast.15, ...), custom_call_target="tpu_custom_call" | custom-call | flops 7247757312 | bytes 9437184 | tf_op jit(solution)/shard_map/pallas_call | solution.py:264
  413.9 4.4 all-to-all-start.1
  419.3 2.9 collective-permute-start.17
  424.5 16.4 %collective-permute-done.15.refs_1_ = bf16[8,192,256]{2,1,0:T(8,128)(2,1)S(1)} collective-permute-done((bf16[8,192,256]{2,1,0:T(8,128)(2,1)}, bf16[8,192,256]{2,1,0:T(8,128)(2,1)S(1)}, u32[]{:S(2)}, u32[]{:S(2)}) %collective-permute-start.15) | collective-permute-done | bytes 786464 | tf_op jit(solution)/shard_map/ppermute | solution.py:445
  440.9 8.8 shard_map.93
  450.6 23.1 %collective-permute-done.16.refs_2_ = bf16[8,192,256]{2,1,0:T(8,128)(2,1)S(1)} collective-permute-done((bf16[8,192,256]{2,1,0:T(8,128)(2,1)}, bf16[8,192,256]{2,1,0:T(8,128)(2,1)S(1)}, u32[]{:S(2)}, u32[]{:S(2)}) %collective-permute-start.16) | collective-permute-done | bytes 786464 | tf_op jit(solution)/shard_map/ppermute | solution.py:445
  474.6 7.8 shard_map.94
  486.0 3.8 collective-permute-done.18.refs_1_
  490.7 66.6 %collective-permute-done.19.refs_2_ = bf16[8,192,256]{2,1,0:T(8,128)(2,1)S(1)} collective-permute-done((bf16[8,192,256]{2,1,0:T(8,128)(2,1)}, bf16[8,192,256]{2,1,0:T(8,128)(2,1)S(1)}, u32[]{:S(2)}, u32[]{:S(2)}) %collective-permute-start.19) | collective-permute-done | bytes 786464 | tf_op jit(solution)/shard_map/ppermute | solution.py:445
  562.5 22.1 %shard_map.95 = (bf16[8,48,8,512]{3,2,1,0:T(8,128)(2,1)}, f32[8,128]{1,0:T(8,128)S(1)}) custom-call(s32[1]{0:T(128)} %bitcast.me_ref, bf16[48,768,256]{2,1,0:T(8,128)(2,1)} %bitcast.29, bf16[256,512]{1,0:T(8,128)(2,1)S(1)} %copy-done.1, bf16[256,512]{1,0:T(8,128)(2,1)S(1)} %bitcast.10, bf16[512,256]{1,0:T(8,128)(2,1)S(1)} %bitcast.16, ...), custom_call_target="tpu_custom_call" | custom-call | flops 7247757312 | bytes 9437184 | tf_op jit(solution)/shard_map/pallas_call | solution.py:264
  584.6 4.4 all-to-all-start.2
  589.2 3.7 collective-permute-start.23
  595.0 16.6 %collective-permute-done.21.refs_1_ = bf16[8,192,256]{2,1,0:T(8,128)(2,1)S(1)} collective-permute-done((bf16[8,192,256]{2,1,0:T(8,128)(2,1)}, bf16[8,192,256]{2,1,0:T(8,128)(2,1)S(1)}, u32[]{:S(2)}, u32[]{:S(2)}) %collective-permute-start.21) | collective-permute-done | bytes 786464 | tf_op jit(solution)/shard_map/ppermute | solution.py:445
  611.6 32.8 %collective-permute-done.22.refs_2_ = bf16[8,192,256]{2,1,0:T(8,128)(2,1)S(1)} collective-permute-done((bf16[8,192,256]{2,1,0:T(8,128)(2,1)}, bf16[8,192,256]{2,1,0:T(8,128)(2,1)S(1)}, u32[]{:S(2)}, u32[]{:S(2)}) %collective-permute-start.22) | collective-permute-done | bytes 786464 | tf_op jit(solution)/shard_map/ppermute | solution.py:445
  646.5 7.8 shard_map.96
  661.5 66.6 %collective-permute-done.25.refs_2_.refs_6_ = bf16[8,192,256]{2,1,0:T(8,128)(2,1)S(1)} collective-permute-done((bf16[8,192,256]{2,1,0:T(8,128)(2,1)}, bf16[8,192,256]{2,1,0:T(8,128)(2,1)S(1)}, u32[]{:S(2)}, u32[]{:S(2)}) %collective-permute-start.25) | collective-permute-done | bytes 786464 | tf_op jit(solution)/shard_map/ppermute | solution.py:445
  734.4 22.1 %shard_map.97 = (bf16[8,48,8,512]{3,2,1,0:T(8,128)(2,1)}, f32[8,128]{1,0:T(8,128)S(1)}) custom-call(s32[1]{0:T(128)} %bitcast.me_ref, bf16[48,768,256]{2,1,0:T(8,128)(2,1)} %bitcast.30, bf16[256,512]{1,0:T(8,128)(2,1)S(1)} %copy-done.1, bf16[256,512]{1,0:T(8,128)(2,1)S(1)} %bitcast.11, bf16[512,256]{1,0:T(8,128)(2,1)S(1)} %bitcast.17, ...), custom_call_target="tpu_custom_call" | custom-call | flops 7247757312 | bytes 9437184 | tf_op jit(solution)/shard_map/pallas_call | solution.py:264
  756.5 4.4 all-to-all-start.3
  761.1 3.7 collective-permute-start.29
  766.9 16.6 %collective-permute-done.27.refs_1_ = bf16[8,192,256]{2,1,0:T(8,128)(2,1)S(1)} collective-permute-done((bf16[8,192,256]{2,1,0:T(8,128)(2,1)}, bf16[8,192,256]{2,1,0:T(8,128)(2,1)S(1)}, u32[]{:S(2)}, u32[]{:S(2)}) %collective-permute-start.27) | collective-permute-done | bytes 786464 | tf_op jit(solution)/shard_map/ppermute | solution.py:445
  783.9 32.4 %collective-permute-done.28.refs_2_ = bf16[8,192,256]{2,1,0:T(8,128)(2,1)S(1)} collective-permute-done((bf16[8,192,256]{2,1,0:T(8,128)(2,1)}, bf16[8,192,256]{2,1,0:T(8,128)(2,1)S(1)}, u32[]{:S(2)}, u32[]{:S(2)}) %collective-permute-start.28) | collective-permute-done | bytes 786464 | tf_op jit(solution)/shard_map/ppermute | solution.py:445
  818.4 7.8 shard_map.98
  829.7 2.7 collective-permute-done.30.refs_1_
  833.3 66.6 %collective-permute-done.31.refs_2_ = bf16[8,192,256]{2,1,0:T(8,128)(2,1)S(1)} collective-permute-done((bf16[8,192,256]{2,1,0:T(8,128)(2,1)}, bf16[8,192,256]{2,1,0:T(8,128)(2,1)S(1)}, u32[]{:S(2)}, u32[]{:S(2)}) %collective-permute-start.31) | collective-permute-done | bytes 786464 | tf_op jit(solution)/shard_map/ppermute | solution.py:445
  906.2 22.1 %shard_map.99 = (bf16[8,48,8,512]{3,2,1,0:T(8,128)(2,1)}, f32[8,128]{1,0:T(8,128)S(1)}) custom-call(s32[1]{0:T(128)} %bitcast.me_ref, bf16[48,768,256]{2,1,0:T(8,128)(2,1)} %bitcast.31, bf16[256,512]{1,0:T(8,128)(2,1)S(1)} %copy-done.1, bf16[256,512]{1,0:T(8,128)(2,1)S(1)} %bitcast.12, bf16[512,256]{1,0:T(8,128)(2,1)S(1)} %bitcast.18, ...), custom_call_target="tpu_custom_call" | custom-call | flops 7247757312 | bytes 9437184 | tf_op jit(solution)/shard_map/pallas_call | solution.py:264
  928.3 4.5 all-to-all-start.4
  934.9 19.2 %collective-permute-done.33.refs_1_.refs_5_ = bf16[8,192,256]{2,1,0:T(8,128)(2,1)S(1)} collective-permute-done((bf16[8,192,256]{2,1,0:T(8,128)(2,1)}, bf16[8,192,256]{2,1,0:T(8,128)(2,1)S(1)}, u32[]{:S(2)}, u32[]{:S(2)}) %collective-permute-start.33) | collective-permute-done | bytes 786464 | tf_op jit(solution)/shard_map/ppermute | solution.py:445
  955.0 46.3 %collective-permute-done.34.refs_2_.refs_6_ = bf16[8,192,256]{2,1,0:T(8,128)(2,1)S(1)} collective-permute-done((bf16[8,192,256]{2,1,0:T(8,128)(2,1)}, bf16[8,192,256]{2,1,0:T(8,128)(2,1)S(1)}, u32[]{:S(2)}, u32[]{:S(2)}) %collective-permute-start.34) | collective-permute-done | bytes 786464 | tf_op jit(solution)/shard_map/ppermute | solution.py:445
  1007.6 22.1 %shard_map.100 = (bf16[8,48,8,512]{3,2,1,0:T(8,128)(2,1)}, f32[8,128]{1,0:T(8,128)S(1)}) custom-call(s32[1]{0:T(128)} %bitcast.me_ref, bf16[48,768,256]{2,1,0:T(8,128)(2,1)} %bitcast.32, bf16[256,512]{1,0:T(8,128)(2,1)S(1)} %copy-done.1, bf16[256,512]{1,0:T(8,128)(2,1)S(1)} %bitcast.13, bf16[512,256]{1,0:T(8,128)(2,1)S(1)} %bitcast.19, ...), custom_call_target="tpu_custom_call" | custom-call | flops 7247757312 | bytes 9437184 | tf_op jit(solution)/shard_map/pallas_call | solution.py:264
  1029.7 4.6 all-to-all-start.5
  1034.8 37.4 %all-to-all-done.5.refs_5_ = bf16[8,48,8,512]{3,2,1,0:T(8,128)(2,1)} async-done(((bf16[8,48,8,512]{3,2,1,0:T(8,128)(2,1)}), bf16[8,48,8,512]{3,2,1,0:T(8,128)(2,1)}, u32[]{:S(2)}, u32[]{:S(2)}) %all-to-all-start.5) | async-done | bytes 3145760 | tf_op jit(solution)/shard_map/all_to_all | solution.py:513
  1072.2 26.0 %shard_map.101 = (bf16[48,384,512]{2,1,0:T(8,128)(2,1)}, f32[8,128]{1,0:T(8,128)S(1)}) custom-call(bf16[48,384,384]{2,1,0:T(8,128)(2,1)} %get-tuple-element.94.table_ref, f32[384,1]{1,0:T(8,128)S(1)} %broadcast_in_dim.70.gain_ref, bf16[256,256]{1,0:T(8,128)(2,1)S(1)} %bitcast.20, f32[8,128]{1,0:T(8,128)S(1)} %get-tuple-element.164._, ...), custom_call_target="tpu_custom_call" | custom-call | flops 12079595520 | bytes 51904512 | tf_op jit(solution)/shard_map/pallas_call | solution.py:313
  1098.2 15.6 %shard_map.102 = (bf16[8,48,16,512]{3,2,1,0:T(8,128)(2,1)}, f32[8,128]{1,0:T(8,128)S(1)}) custom-call(bf16[48,384,384]{2,1,0:T(8,128)(2,1)} %get-tuple-element.94.table_ref, f32[128,1]{1,0:T(8,128)S(1)} %slice.28.quad_ref, bf16[48,384,512]{2,1,0:T(8,128)(2,1)} %get-tuple-element.166.coeff_ref, f32[8,128]{1,0:T(8,128)S(1)} %get-tuple-element.167._), custom_call_target="tpu_custom_call" | custom-call | flops 2415919104 | bytes 29884416 | tf_op jit(solution)/shard_map/pallas_call | solution.py:350
  1113.7 4.7 all-to-all-start.6
  1118.6 15.6 %shard_map.103 = (bf16[8,48,16,512]{3,2,1,0:T(8,128)(2,1)}, f32[8,128]{1,0:T(8,128)S(1)}) custom-call(bf16[48,384,384]{2,1,0:T(8,128)(2,1)} %get-tuple-element.94.table_ref, f32[128,1]{1,0:T(8,128)S(1)} %slice.29.quad_ref, bf16[48,384,512]{2,1,0:T(8,128)(2,1)} %get-tuple-element.166.coeff_ref, f32[8,128]{1,0:T(8,128)S(1)} %get-tuple-element.169._), custom_call_target="tpu_custom_call" | custom-call | flops 2415919104 | bytes 29884416 | tf_op jit(solution)/shard_map/pallas_call | solution.py:350
  1134.2 55.9 %all-to-all-done.6.wave_ref = bf16[8,48,16,512]{3,2,1,0:T(8,128)(2,1)} async-done(((bf16[8,48,16,512]{3,2,1,0:T(8,128)(2,1)}), bf16[8,48,16,512]{3,2,1,0:T(8,128)(2,1)}, u32[]{:S(2)}, u32[]{:S(2)}) %all-to-all-start.6) | async-done | bytes 6291488 | tf_op jit(solution)/shard_map/all_to_all | solution.py:523
  1190.1 4.9 all-to-all-start.8
  1199.6 24.0 %shard_map.104 = (bf16[1,48,768,256]{3,2,1,0:T(8,128)(2,1)}, f32[8,128]{1,0:T(8,128)S(1)}) custom-call(s32[1]{0:T(128)} %bitcast.me_ref, bf16[8,48,16,512]{3,2,1,0:T(8,128)(2,1)} %all-to-all-done.6.wave_ref, bf16[768,768]{1,0:T(8,128)(2,1)} %get-tuple-element.182.analysis_ref, f32[8,128]{1,0:T(8,128)S(1)} %get-tuple-element.170._, ...), custom_call_target="tpu_custom_call" | custom-call | flops 4831838208 | bytes 18874368 | tf_op jit(solution)/shard_map/pallas_call | solution.py:417
  1223.7 15.6 %shard_map.105 = (bf16[8,48,16,512]{3,2,1,0:T(8,128)(2,1)}, f32[8,128]{1,0:T(8,128)S(1)}) custom-call(bf16[48,384,384]{2,1,0:T(8,128)(2,1)} %get-tuple-element.94.table_ref, f32[128,1]{1,0:T(8,128)S(1)} %slice.27.quad_ref, bf16[48,384,512]{2,1,0:T(8,128)(2,1)} %get-tuple-element.166.coeff_ref, f32[8,128]{1,0:T(8,128)S(1)} %get-tuple-element.171._), custom_call_target="tpu_custom_call" | custom-call | flops 2415919104 | bytes 29884416 | tf_op jit(solution)/shard_map/pallas_call | solution.py:350
  1239.2 27.3 %all-to-all-done.8.wave_ref = bf16[8,48,16,512]{3,2,1,0:T(8,128)(2,1)} async-done(((bf16[8,48,16,512]{3,2,1,0:T(8,128)(2,1)}), bf16[8,48,16,512]{3,2,1,0:T(8,128)(2,1)}, u32[]{:S(2)}, u32[]{:S(2)}) %all-to-all-start.8) | async-done | bytes 6291488 | tf_op jit(solution)/shard_map/all_to_all | solution.py:523
  1266.6 5.0 all-to-all-start.7
  1275.1 24.1 %shard_map.106 = (bf16[1,48,768,256]{3,2,1,0:T(8,128)(2,1)}, f32[8,128]{1,0:T(8,128)S(1)}) custom-call(s32[1]{0:T(128)} %bitcast.me_ref, bf16[8,48,16,512]{3,2,1,0:T(8,128)(2,1)} %all-to-all-done.8.wave_ref, bf16[768,768]{1,0:T(8,128)(2,1)} %get-tuple-element.182.analysis_ref, f32[8,128]{1,0:T(8,128)S(1)} %get-tuple-element.174._, ...), custom_call_target="tpu_custom_call", output_to_operand_aliasing={{0}: (12, {})} | custom-call | flops 4831838208 | bytes 18874368 | tf_op jit(solution)/shard_map/pallas_call | solution.py:417
  1299.2 44.0 %all-to-all-done.7.wave_ref = bf16[8,48,16,512]{3,2,1,0:T(8,128)(2,1)} async-done(((bf16[8,48,16,512]{3,2,1,0:T(8,128)(2,1)}), bf16[8,48,16,512]{3,2,1,0:T(8,128)(2,1)}, u32[]{:S(2)}, u32[]{:S(2)}) %all-to-all-start.7) | async-done | bytes 6291488 | tf_op jit(solution)/shard_map/all_to_all | solution.py:523
  1351.2 24.1 %shard_map.107 = (bf16[1,48,768,256]{3,2,1,0:T(8,128)(2,1)}, f32[8,128]{1,0:T(8,128)}) custom-call(s32[1]{0:T(128)} %bitcast.me_ref, bf16[8,48,16,512]{3,2,1,0:T(8,128)(2,1)} %all-to-all-done.7.wave_ref, bf16[768,768]{1,0:T(8,128)(2,1)} %get-tuple-element.182.analysis_ref, f32[8,128]{1,0:T(8,128)S(1)} %get-tuple-element.176._, ...), custom_call_target="tpu_custom_call", output_to_operand_aliasing={{0}: (12, {})} | custom-call | flops 4831838208 | bytes 18874368 | tf_op jit(solution)/shard_map/pallas_call | solution.py:417
  (312 shorter events, 111.0 us)
Async XLA Ops:
  11.5 16.3 %copy-start.68 = (bf16[8,192,256]{2,1,0:T(8,128)(2,1)}, bf16[8,192,256]{2,1,0:T(8,128)(2,1)S(1)}, u32[]{:S(2)}) copy-start(bf16[8,192,256]{2,1,0:T(8,128)(2,1)S(1)} %get-tuple-element.97.refs_0_) | copy-start | bytes 2359300
  11.5 70.3 %collective-permute-start = (bf16[8,192,256]{2,1,0:T(8,128)(2,1)}, bf16[8,192,256]{2,1,0:T(8,128)(2,1)}, u32[]{:S(2)}, u32[]{:S(2)}) collective-permute-start(bf16[8,192,256]{2,1,0:T(8,128)(2,1)} %get-tuple-element.98), channel_id=1, source_target_pairs={{0,8},{8,16},{16,24},{24,0},{1,9},{9,17},{17,25},{25,1},{2,10},{10... | collective-permute-start | bytes 2359304 | tf_op jit(solution)/shard_map/ppermute | solution.py:445
  14.5 70.1 %collective-permute-start.1 = (bf16[8,192,256]{2,1,0:T(8,128)(2,1)}, bf16[8,192,256]{2,1,0:T(8,128)(2,1)}, u32[]{:S(2)}, u32[]{:S(2)}) collective-permute-start(bf16[8,192,256]{2,1,0:T(8,128)(2,1)} %get-tuple-element.99), channel_id=1, source_target_pairs={{0,16},{8,24},{16,0},{24,8},{1,17},{9,25},{17,1},{25,9},{2,18},{10... | collective-permute-start | bytes 2359304 | tf_op jit(solution)/shard_map/ppermute | solution.py:445
  17.1 67.6 %collective-permute-start.2 = (bf16[8,192,256]{2,1,0:T(8,128)(2,1)}, bf16[8,192,256]{2,1,0:T(8,128)(2,1)}, u32[]{:S(2)}, u32[]{:S(2)}) collective-permute-start(bf16[8,192,256]{2,1,0:T(8,128)(2,1)} %get-tuple-element.100), channel_id=1, source_target_pairs={{0,24},{8,0},{16,8},{24,16},{1,25},{9,1},{17,9},{25,17},{2,26},{10... | collective-permute-start | bytes 2359304 | tf_op jit(solution)/shard_map/ppermute | solution.py:445
  28.6 109.5 %collective-permute-start.3 = (bf16[8,192,256]{2,1,0:T(8,128)(2,1)}, bf16[8,192,256]{2,1,0:T(8,128)(2,1)S(1)}, u32[]{:S(2)}, u32[]{:S(2)}) collective-permute-start(bf16[8,192,256]{2,1,0:T(8,128)(2,1)} %get-tuple-element.104), channel_id=1, source_target_pairs={{0,8},{8,16},{16,24},{24,0},{1,9},{9,17},{17,25},{25,1},{2,10},{10... | collective-permute-start | bytes 2359304 | tf_op jit(solution)/shard_map/ppermute | solution.py:445
  29.3 172.9 %collective-permute-start.4 = (bf16[8,192,256]{2,1,0:T(8,128)(2,1)}, bf16[8,192,256]{2,1,0:T(8,128)(2,1)}, u32[]{:S(2)}, u32[]{:S(2)}) collective-permute-start(bf16[8,192,256]{2,1,0:T(8,128)(2,1)} %get-tuple-element.105), channel_id=1, source_target_pairs={{0,16},{8,24},{16,0},{24,8},{1,17},{9,25},{17,1},{25,9},{2,18},{10... | collective-permute-start | bytes 2359304 | tf_op jit(solution)/shard_map/ppermute | solution.py:445
  30.5 36.6 %copy-start.3 = (bf16[512,256]{1,0:T(8,128)(2,1)S(1)}, bf16[512,256]{1,0:T(8,128)(2,1)}, u32[]{:S(2)}) copy-start(bf16[512,256]{1,0:T(8,128)(2,1)} %down_ref.11) | copy-start | bytes 786436
  30.5 36.7 %copy-start.1 = (bf16[256,512]{1,0:T(8,128)(2,1)S(1)}, bf16[256,512]{1,0:T(8,128)(2,1)}, u32[]{:S(2)}) copy-start(bf16[256,512]{1,0:T(8,128)(2,1)} %up_ref.23) | copy-start | bytes 786436
  30.5 36.9 %copy-start.113 = (s32[48,768]{1,0:T(8,128)S(1)}, s32[48,768]{1,0:T(8,128)}, u32[]{:S(2)}) copy-start(s32[48,768]{1,0:T(8,128)} %param.11) | copy-start | bytes 442372
  69.3 12.5 copy-start.91
  69.3 15.3 %copy-start.69 = (bf16[8,192,256]{2,1,0:T(8,128)(2,1)S(1)}, bf16[8,192,256]{2,1,0:T(8,128)(2,1)}, u32[]{:S(2)}) copy-start(bf16[8,192,256]{2,1,0:T(8,128)(2,1)} %copy-done.68) | copy-start | bytes 2359300
  81.8 120.4 %collective-permute-start.5 = (bf16[8,192,256]{2,1,0:T(8,128)(2,1)S(1)}, bf16[8,192,256]{2,1,0:T(8,128)(2,1)S(1)}, u32[]{:S(2)}, u32[]{:S(2)}) collective-permute-start(bf16[8,192,256]{2,1,0:T(8,128)(2,1)S(1)} %copy-done.91), channel_id=1, source_target_pairs={{0,24},{8,0},{16,8},{24,16},{1,25},{9,1},{17,9},{25,17},{2,26},{10... | collective-permute-start | bytes 2359304 | tf_op jit(solution)/shard_map/ppermute | solution.py:445
  92.9 119.7 %collective-permute-start.6 = (bf16[8,192,256]{2,1,0:T(8,128)(2,1)S(1)}, bf16[8,192,256]{2,1,0:T(8,128)(2,1)S(1)}, u32[]{:S(2)}, u32[]{:S(2)}) collective-permute-start(bf16[8,192,256]{2,1,0:T(8,128)(2,1)S(1)} %get-tuple-element.109), channel_id=1, source_target_pairs={{0,24},{8,0},{16,8},{24,16},{1,25},{9,1},{17,9},{25,17},{2,26},{10... | collective-permute-start | bytes 2359304 | tf_op jit(solution)/shard_map/ppermute | solution.py:445
  138.2 81.6 %collective-permute-start.7 = (bf16[8,192,256]{2,1,0:T(8,128)(2,1)S(1)}, bf16[8,192,256]{2,1,0:T(8,128)(2,1)S(1)}, u32[]{:S(2)}, u32[]{:S(2)}) collective-permute-start(bf16[8,192,256]{2,1,0:T(8,128)(2,1)S(1)} %get-tuple-element.110), channel_id=1, source_target_pairs={{0,16},{8,24},{16,0},{24,8},{1,17},{9,25},{17,1},{25,9},{2,18},{10... | collective-permute-start | bytes 2359304 | tf_op jit(solution)/shard_map/ppermute | solution.py:445
  139.1 80.7 %collective-permute-start.8 = (bf16[8,192,256]{2,1,0:T(8,128)(2,1)S(1)}, bf16[8,192,256]{2,1,0:T(8,128)(2,1)S(1)}, u32[]{:S(2)}, u32[]{:S(2)}) collective-permute-start(bf16[8,192,256]{2,1,0:T(8,128)(2,1)S(1)} %get-tuple-element.111), channel_id=1, source_target_pairs={{0,8},{8,16},{16,24},{24,0},{1,9},{9,17},{17,25},{25,1},{2,10},{10... | collective-permute-start | bytes 2359304 | tf_op jit(solution)/shard_map/ppermute | solution.py:445
  191.6 12.1 copy-start.67
  212.6 29.5 %copy-start.95 = (bf16[8,192,256]{2,1,0:T(8,128)(2,1)}, bf16[8,192,256]{2,1,0:T(8,128)(2,1)S(1)}, u32[]{:S(2)}) copy-start(bf16[8,192,256]{2,1,0:T(8,128)(2,1)S(1)} %get-tuple-element.123) | copy-start | bytes 2359300
  212.6 29.5 %copy-start.99 = (bf16[8,192,256]{2,1,0:T(8,128)(2,1)}, bf16[8,192,256]{2,1,0:T(8,128)(2,1)S(1)}, u32[]{:S(2)}) copy-start(bf16[8,192,256]{2,1,0:T(8,128)(2,1)S(1)} %get-tuple-element.122) | copy-start | bytes 2359300
  212.6 29.5 %copy-start.102 = (bf16[8,192,256]{2,1,0:T(8,128)(2,1)}, bf16[8,192,256]{2,1,0:T(8,128)(2,1)S(1)}, u32[]{:S(2)}) copy-start(bf16[8,192,256]{2,1,0:T(8,128)(2,1)S(1)} %get-tuple-element.121) | copy-start | bytes 2359300
  212.6 29.5 %copy-start.72 = (bf16[8,192,256]{2,1,0:T(8,128)(2,1)}, bf16[8,192,256]{2,1,0:T(8,128)(2,1)S(1)}, u32[]{:S(2)}) copy-start(bf16[8,192,256]{2,1,0:T(8,128)(2,1)S(1)} %collective-permute-done.6.refs_1_) | copy-start | bytes 2359300
  219.7 22.4 %copy-start.74 = (bf16[8,192,256]{2,1,0:T(8,128)(2,1)}, bf16[8,192,256]{2,1,0:T(8,128)(2,1)S(1)}, u32[]{:S(2)}) copy-start(bf16[8,192,256]{2,1,0:T(8,128)(2,1)S(1)} %collective-permute-done.7.refs_2_) | copy-start | bytes 2359300
  219.8 22.4 %copy-start.76 = (bf16[8,192,256]{2,1,0:T(8,128)(2,1)}, bf16[8,192,256]{2,1,0:T(8,128)(2,1)S(1)}, u32[]{:S(2)}) copy-start(bf16[8,192,256]{2,1,0:T(8,128)(2,1)S(1)} %collective-permute-done.8.refs_3_) | copy-start | bytes 2359300
  243.0 144.2 %all-to-all-start = ((bf16[8,48,8,512]{3,2,1,0:T(8,128)(2,1)}), bf16[8,48,8,512]{3,2,1,0:T(8,128)(2,1)}, u32[]{:S(2)}, u32[]{:S(2)}) async-start(bf16[8,48,8,512]{3,2,1,0:T(8,128)(2,1)} %get-tuple-element.119), calls=%async_computation | async-start | bytes 6291456 | tf_op jit(solution)/shard_map/all_to_all | solution.py:513
  247.6 37.1 %collective-permute-start.10 = (bf16[8,192,256]{2,1,0:T(8,128)(2,1)}, bf16[8,192,256]{2,1,0:T(8,128)(2,1)S(1)}, u32[]{:S(2)}, u32[]{:S(2)}) collective-permute-start(bf16[8,192,256]{2,1,0:T(8,128)(2,1)} %copy-done.92), channel_id=1, source_target_pairs={{0,16},{8,24},{16,0},{24,8},{1,17},{9,25},{17,1},{25,9},{2,18},{10... | collective-permute-start | bytes 2359304 | tf_op jit(solution)/shard_map/ppermute | solution.py:445
  248.4 62.8 %collective-permute-start.11 = (bf16[8,192,256]{2,1,0:T(8,128)(2,1)}, bf16[8,192,256]{2,1,0:T(8,128)(2,1)S(1)}, u32[]{:S(2)}, u32[]{:S(2)}) collective-permute-start(bf16[8,192,256]{2,1,0:T(8,128)(2,1)} %copy-done.89), channel_id=1, source_target_pairs={{0,24},{8,0},{16,8},{24,16},{1,25},{9,1},{17,9},{25,17},{2,26},{10... | collective-permute-start | bytes 2359304 | tf_op jit(solution)/shard_map/ppermute | solution.py:445
  249.3 61.9 %collective-permute-start.9 = (bf16[8,192,256]{2,1,0:T(8,128)(2,1)S(1)}, bf16[8,192,256]{2,1,0:T(8,128)(2,1)S(1)}, u32[]{:S(2)}, u32[]{:S(2)}) collective-permute-start(bf16[8,192,256]{2,1,0:T(8,128)(2,1)S(1)} %copy-done.88), channel_id=1, source_target_pairs={{0,8},{8,16},{16,24},{24,0},{1,9},{9,17},{17,25},{25,1},{2,10},{10... | collective-permute-start | bytes 2359304 | tf_op jit(solution)/shard_map/ppermute | solution.py:445
  250.4 72.3 %collective-permute-start.12 = (bf16[8,192,256]{2,1,0:T(8,128)(2,1)}, bf16[8,192,256]{2,1,0:T(8,128)(2,1)S(1)}, u32[]{:S(2)}, u32[]{:S(2)}) collective-permute-start(bf16[8,192,256]{2,1,0:T(8,128)(2,1)} %copy-done.102), channel_id=1, source_target_pairs={{0,24},{8,0},{16,8},{24,16},{1,25},{9,1},{17,9},{25,17},{2,26},{10... | collective-permute-start | bytes 2359304 | tf_op jit(solution)/shard_map/ppermute | solution.py:445
  253.1 132.3 %collective-permute-start.13 = (bf16[8,192,256]{2,1,0:T(8,128)(2,1)}, bf16[8,192,256]{2,1,0:T(8,128)(2,1)S(1)}, u32[]{:S(2)}, u32[]{:S(2)}) collective-permute-start(bf16[8,192,256]{2,1,0:T(8,128)(2,1)} %copy-done.99), channel_id=1, source_target_pairs={{0,16},{8,24},{16,0},{24,8},{1,17},{9,25},{17,1},{25,9},{2,18},{10... | collective-permute-start | bytes 2359304 | tf_op jit(solution)/shard_map/ppermute | solution.py:445
  284.7 101.6 %collective-permute-start.14 = (bf16[8,192,256]{2,1,0:T(8,128)(2,1)}, bf16[8,192,256]{2,1,0:T(8,128)(2,1)S(1)}, u32[]{:S(2)}, u32[]{:S(2)}) collective-permute-start(bf16[8,192,256]{2,1,0:T(8,128)(2,1)} %copy-done.95), channel_id=1, source_target_pairs={{0,8},{8,16},{16,24},{24,0},{1,9},{9,17},{17,25},{25,1},{2,10},{10... | collective-permute-start | bytes 2359304 | tf_op jit(solution)/shard_map/ppermute | solution.py:445
  301.4 10.6 copy-start.65
  311.1 8.9 copy-start.83
  413.9 145.3 %all-to-all-start.1 = ((bf16[8,48,8,512]{3,2,1,0:T(8,128)(2,1)}), bf16[8,48,8,512]{3,2,1,0:T(8,128)(2,1)}, u32[]{:S(2)}, u32[]{:S(2)}) async-start(bf16[8,48,8,512]{3,2,1,0:T(8,128)(2,1)} %get-tuple-element.131), calls=%async_computation.1 | async-start | bytes 6291456 | tf_op jit(solution)/shard_map/all_to_all | solution.py:513
  418.3 22.6 %collective-permute-start.15 = (bf16[8,192,256]{2,1,0:T(8,128)(2,1)}, bf16[8,192,256]{2,1,0:T(8,128)(2,1)S(1)}, u32[]{:S(2)}, u32[]{:S(2)}) collective-permute-start(bf16[8,192,256]{2,1,0:T(8,128)(2,1)} %copy-done.85), channel_id=1, source_target_pairs={{0,8},{8,16},{16,24},{24,0},{1,9},{9,17},{17,25},{25,1},{2,10},{10... | collective-permute-start | bytes 2359304 | tf_op jit(solution)/shard_map/ppermute | solution.py:445
  418.4 55.3 %collective-permute-start.16 = (bf16[8,192,256]{2,1,0:T(8,128)(2,1)}, bf16[8,192,256]{2,1,0:T(8,128)(2,1)S(1)}, u32[]{:S(2)}, u32[]{:S(2)}) collective-permute-start(bf16[8,192,256]{2,1,0:T(8,128)(2,1)} %copy-done.79), channel_id=1, source_target_pairs={{0,16},{8,24},{16,0},{24,8},{1,17},{9,25},{17,1},{25,9},{2,18},{10... | collective-permute-start | bytes 2359304 | tf_op jit(solution)/shard_map/ppermute | solution.py:445
  419.3 54.4 %collective-permute-start.17 = (bf16[8,192,256]{2,1,0:T(8,128)(2,1)}, bf16[8,192,256]{2,1,0:T(8,128)(2,1)S(1)}, u32[]{:S(2)}, u32[]{:S(2)}) collective-permute-start(bf16[8,192,256]{2,1,0:T(8,128)(2,1)} %copy-done.78), channel_id=1, source_target_pairs={{0,24},{8,0},{16,8},{24,16},{1,25},{9,1},{17,9},{25,17},{2,26},{10... | collective-permute-start | bytes 2359304 | tf_op jit(solution)/shard_map/ppermute | solution.py:445
  422.2 67.6 %collective-permute-start.18 = (bf16[8,192,256]{2,1,0:T(8,128)(2,1)}, bf16[8,192,256]{2,1,0:T(8,128)(2,1)S(1)}, u32[]{:S(2)}, u32[]{:S(2)}) collective-permute-start(bf16[8,192,256]{2,1,0:T(8,128)(2,1)} %copy-done.96), channel_id=1, source_target_pairs={{0,24},{8,0},{16,8},{24,16},{1,25},{9,1},{17,9},{25,17},{2,26},{10... | collective-permute-start | bytes 2359304 | tf_op jit(solution)/shard_map/ppermute | solution.py:445
  423.0 134.3 %collective-permute-start.19 = (bf16[8,192,256]{2,1,0:T(8,128)(2,1)}, bf16[8,192,256]{2,1,0:T(8,128)(2,1)S(1)}, u32[]{:S(2)}, u32[]{:S(2)}) collective-permute-start(bf16[8,192,256]{2,1,0:T(8,128)(2,1)} %copy-done.94), channel_id=1, source_target_pairs={{0,16},{8,24},{16,0},{24,8},{1,17},{9,25},{17,1},{25,9},{2,18},{10... | collective-permute-start | bytes 2359304 | tf_op jit(solution)/shard_map/ppermute | solution.py:445
  440.9 117.3 %collective-permute-start.20 = (bf16[8,192,256]{2,1,0:T(8,128)(2,1)}, bf16[8,192,256]{2,1,0:T(8,128)(2,1)S(1)}, u32[]{:S(2)}, u32[]{:S(2)}) collective-permute-start(bf16[8,192,256]{2,1,0:T(8,128)(2,1)} %copy-done.93), channel_id=1, source_target_pairs={{0,8},{8,16},{16,24},{24,0},{1,9},{9,17},{17,25},{25,1},{2,10},{10... | collective-permute-start | bytes 2359304 | tf_op jit(solution)/shard_map/ppermute | solution.py:445
  440.9 33.7 %copy-start.59 = (bf16[8,192,256]{2,1,0:T(8,128)(2,1)S(1)}, bf16[8,192,256]{2,1,0:T(8,128)(2,1)}, u32[]{:S(2)}) copy-start(bf16[8,192,256]{2,1,0:T(8,128)(2,1)} %copy-done.58) | copy-start | bytes 2359300
  450.6 31.8 %copy-start.82 = (bf16[8,192,256]{2,1,0:T(8,128)(2,1)}, bf16[8,192,256]{2,1,0:T(8,128)(2,1)S(1)}, u32[]{:S(2)}) copy-start(bf16[8,192,256]{2,1,0:T(8,128)(2,1)S(1)} %get-tuple-element.151) | copy-start | bytes 2359300
  450.6 31.8 %copy-start.84 = (bf16[8,192,256]{2,1,0:T(8,128)(2,1)}, bf16[8,192,256]{2,1,0:T(8,128)(2,1)S(1)}, u32[]{:S(2)}) copy-start(bf16[8,192,256]{2,1,0:T(8,128)(2,1)S(1)} %get-tuple-element.150) | copy-start | bytes 2359300
  450.6 31.8 %copy-start.86 = (bf16[8,192,256]{2,1,0:T(8,128)(2,1)}, bf16[8,192,256]{2,1,0:T(8,128)(2,1)S(1)}, u32[]{:S(2)}) copy-start(bf16[8,192,256]{2,1,0:T(8,128)(2,1)S(1)} %get-tuple-element.149) | copy-start | bytes 2359300
  584.6 145.2 %all-to-all-start.2 = ((bf16[8,48,8,512]{3,2,1,0:T(8,128)(2,1)}), bf16[8,48,8,512]{3,2,1,0:T(8,128)(2,1)}, u32[]{:S(2)}, u32[]{:S(2)}) async-start(bf16[8,48,8,512]{3,2,1,0:T(8,128)(2,1)} %get-tuple-element.142), calls=%async_computation.2 | async-start | bytes 6291456 | tf_op jit(solution)/shard_map/all_to_all | solution.py:513
  589.1 22.6 %collective-permute-start.21 = (bf16[8,192,256]{2,1,0:T(8,128)(2,1)}, bf16[8,192,256]{2,1,0:T(8,128)(2,1)S(1)}, u32[]{:S(2)}, u32[]{:S(2)}) collective-permute-start(bf16[8,192,256]{2,1,0:T(8,128)(2,1)} %copy-done.83), channel_id=1, source_target_pairs={{0,8},{8,16},{16,24},{24,0},{1,9},{9,17},{17,25},{25,1},{2,10},{10... | collective-permute-start | bytes 2359304 | tf_op jit(solution)/shard_map/ppermute | solution.py:445
  589.1 55.3 %collective-permute-start.22 = (bf16[8,192,256]{2,1,0:T(8,128)(2,1)}, bf16[8,192,256]{2,1,0:T(8,128)(2,1)S(1)}, u32[]{:S(2)}, u32[]{:S(2)}) collective-permute-start(bf16[8,192,256]{2,1,0:T(8,128)(2,1)} %copy-done.81), channel_id=1, source_target_pairs={{0,16},{8,24},{16,0},{24,8},{1,17},{9,25},{17,1},{25,9},{2,18},{10... | collective-permute-start | bytes 2359304 | tf_op jit(solution)/shard_map/ppermute | solution.py:445
  589.2 55.3 %collective-permute-start.23 = (bf16[8,192,256]{2,1,0:T(8,128)(2,1)}, bf16[8,192,256]{2,1,0:T(8,128)(2,1)S(1)}, u32[]{:S(2)}, u32[]{:S(2)}) collective-permute-start(bf16[8,192,256]{2,1,0:T(8,128)(2,1)} %copy-done.80), channel_id=1, source_target_pairs={{0,24},{8,0},{16,8},{24,16},{1,25},{9,1},{17,9},{25,17},{2,26},{10... | collective-permute-start | bytes 2359304 | tf_op jit(solution)/shard_map/ppermute | solution.py:445
  592.9 67.6 %collective-permute-start.24 = (bf16[8,192,256]{2,1,0:T(8,128)(2,1)}, bf16[8,192,256]{2,1,0:T(8,128)(2,1)S(1)}, u32[]{:S(2)}, u32[]{:S(2)}) collective-permute-start(bf16[8,192,256]{2,1,0:T(8,128)(2,1)} %copy-done.104), channel_id=1, source_target_pairs={{0,24},{8,0},{16,8},{24,16},{1,25},{9,1},{17,9},{25,17},{2,26},{10... | collective-permute-start | bytes 2359304 | tf_op jit(solution)/shard_map/ppermute | solution.py:445
  593.6 134.5 %collective-permute-start.25 = (bf16[8,192,256]{2,1,0:T(8,128)(2,1)}, bf16[8,192,256]{2,1,0:T(8,128)(2,1)S(1)}, u32[]{:S(2)}, u32[]{:S(2)}) collective-permute-start(bf16[8,192,256]{2,1,0:T(8,128)(2,1)} %copy-done.101), channel_id=1, source_target_pairs={{0,16},{8,24},{16,0},{24,8},{1,17},{9,25},{17,1},{25,9},{2,18},{10... | collective-permute-start | bytes 2359304 | tf_op jit(solution)/shard_map/ppermute | solution.py:445
  611.6 117.3 %collective-permute-start.26 = (bf16[8,192,256]{2,1,0:T(8,128)(2,1)}, bf16[8,192,256]{2,1,0:T(8,128)(2,1)S(1)}, u32[]{:S(2)}, u32[]{:S(2)}) collective-permute-start(bf16[8,192,256]{2,1,0:T(8,128)(2,1)} %copy-done.98), channel_id=1, source_target_pairs={{0,8},{8,16},{16,24},{24,0},{1,9},{9,17},{17,25},{25,1},{2,10},{10... | collective-permute-start | bytes 2359304 | tf_op jit(solution)/shard_map/ppermute | solution.py:445
  756.5 145.2 %all-to-all-start.3 = ((bf16[8,48,8,512]{3,2,1,0:T(8,128)(2,1)}), bf16[8,48,8,512]{3,2,1,0:T(8,128)(2,1)}, u32[]{:S(2)}, u32[]{:S(2)}) async-start(bf16[8,48,8,512]{3,2,1,0:T(8,128)(2,1)} %get-tuple-element.153), calls=%async_computation.3 | async-start | bytes 6291456 | tf_op jit(solution)/shard_map/all_to_all | solution.py:513
  760.9 22.6 %collective-permute-start.27 = (bf16[8,192,256]{2,1,0:T(8,128)(2,1)}, bf16[8,192,256]{2,1,0:T(8,128)(2,1)S(1)}, u32[]{:S(2)}, u32[]{:S(2)}) collective-permute-start(bf16[8,192,256]{2,1,0:T(8,128)(2,1)} %copy-done.86), channel_id=1, source_target_pairs={{0,8},{8,16},{16,24},{24,0},{1,9},{9,17},{17,25},{25,1},{2,10},{10... | collective-permute-start | bytes 2359304 | tf_op jit(solution)/shard_map/ppermute | solution.py:445
  761.0 55.3 %collective-permute-start.28 = (bf16[8,192,256]{2,1,0:T(8,128)(2,1)}, bf16[8,192,256]{2,1,0:T(8,128)(2,1)S(1)}, u32[]{:S(2)}, u32[]{:S(2)}) collective-permute-start(bf16[8,192,256]{2,1,0:T(8,128)(2,1)} %copy-done.84), channel_id=1, source_target_pairs={{0,16},{8,24},{16,0},{24,8},{1,17},{9,25},{17,1},{25,9},{2,18},{10... | collective-permute-start | bytes 2359304 | tf_op jit(solution)/shard_map/ppermute | solution.py:445
  761.1 55.3 %collective-permute-start.29 = (bf16[8,192,256]{2,1,0:T(8,128)(2,1)}, bf16[8,192,256]{2,1,0:T(8,128)(2,1)S(1)}, u32[]{:S(2)}, u32[]{:S(2)}) collective-permute-start(bf16[8,192,256]{2,1,0:T(8,128)(2,1)} %copy-done.82), channel_id=1, source_target_pairs={{0,24},{8,0},{16,8},{24,16},{1,25},{9,1},{17,9},{25,17},{2,26},{10... | collective-permute-start | bytes 2359304 | tf_op jit(solution)/shard_map/ppermute | solution.py:445
  764.8 67.6 %collective-permute-start.30 = (bf16[8,192,256]{2,1,0:T(8,128)(2,1)}, bf16[8,192,256]{2,1,0:T(8,128)(2,1)S(1)}, u32[]{:S(2)}, u32[]{:S(2)}) collective-permute-start(bf16[8,192,256]{2,1,0:T(8,128)(2,1)} %copy-done.103), channel_id=1, source_target_pairs={{0,24},{8,0},{16,8},{24,16},{1,25},{9,1},{17,9},{25,17},{2,26},{10... | collective-permute-start | bytes 2359304 | tf_op jit(solution)/shard_map/ppermute | solution.py:445
  765.4 134.5 %collective-permute-start.31 = (bf16[8,192,256]{2,1,0:T(8,128)(2,1)}, bf16[8,192,256]{2,1,0:T(8,128)(2,1)S(1)}, u32[]{:S(2)}, u32[]{:S(2)}) collective-permute-start(bf16[8,192,256]{2,1,0:T(8,128)(2,1)} %copy-done.100), channel_id=1, source_target_pairs={{0,16},{8,24},{16,0},{24,8},{1,17},{9,25},{17,1},{25,9},{2,18},{10... | collective-permute-start | bytes 2359304 | tf_op jit(solution)/shard_map/ppermute | solution.py:445
  783.5 117.3 %collective-permute-start.32 = (bf16[8,192,256]{2,1,0:T(8,128)(2,1)}, bf16[8,192,256]{2,1,0:T(8,128)(2,1)S(1)}, u32[]{:S(2)}, u32[]{:S(2)}) collective-permute-start(bf16[8,192,256]{2,1,0:T(8,128)(2,1)} %copy-done.97), channel_id=1, source_target_pairs={{0,8},{8,16},{16,24},{24,0},{1,9},{9,17},{17,25},{25,1},{2,10},{10... | collective-permute-start | bytes 2359304 | tf_op jit(solution)/shard_map/ppermute | solution.py:445
  928.3 74.8 %all-to-all-start.4 = ((bf16[8,48,8,512]{3,2,1,0:T(8,128)(2,1)}), bf16[8,48,8,512]{3,2,1,0:T(8,128)(2,1)}, u32[]{:S(2)}, u32[]{:S(2)}) async-start(bf16[8,48,8,512]{3,2,1,0:T(8,128)(2,1)} %get-tuple-element.159), calls=%async_computation.4 | async-start | bytes 6291456 | tf_op jit(solution)/shard_map/all_to_all | solution.py:513
  932.8 21.3 %collective-permute-start.33 = (bf16[8,192,256]{2,1,0:T(8,128)(2,1)}, bf16[8,192,256]{2,1,0:T(8,128)(2,1)S(1)}, u32[]{:S(2)}, u32[]{:S(2)}) collective-permute-start(bf16[8,192,256]{2,1,0:T(8,128)(2,1)} %copy-done.107), channel_id=1, source_target_pairs={{0,24},{8,0},{16,8},{24,16},{1,25},{9,1},{17,9},{25,17},{2,26},{10... | collective-permute-start | bytes 2359304 | tf_op jit(solution)/shard_map/ppermute | solution.py:445
  932.8 68.5 %collective-permute-start.34 = (bf16[8,192,256]{2,1,0:T(8,128)(2,1)}, bf16[8,192,256]{2,1,0:T(8,128)(2,1)S(1)}, u32[]{:S(2)}, u32[]{:S(2)}) collective-permute-start(bf16[8,192,256]{2,1,0:T(8,128)(2,1)} %copy-done.106), channel_id=1, source_target_pairs={{0,16},{8,24},{16,0},{24,8},{1,17},{9,25},{17,1},{25,9},{2,18},{10... | collective-permute-start | bytes 2359304 | tf_op jit(solution)/shard_map/ppermute | solution.py:445
  932.9 69.3 %collective-permute-start.35 = (bf16[8,192,256]{2,1,0:T(8,128)(2,1)}, bf16[8,192,256]{2,1,0:T(8,128)(2,1)S(1)}, u32[]{:S(2)}, u32[]{:S(2)}) collective-permute-start(bf16[8,192,256]{2,1,0:T(8,128)(2,1)} %copy-done.105), channel_id=1, source_target_pairs={{0,8},{8,16},{16,24},{24,0},{1,9},{9,17},{17,25},{25,1},{2,10},{10... | collective-permute-start | bytes 2359304 | tf_op jit(solution)/shard_map/ppermute | solution.py:445
  1029.7 42.5 %all-to-all-start.5 = ((bf16[8,48,8,512]{3,2,1,0:T(8,128)(2,1)}), bf16[8,48,8,512]{3,2,1,0:T(8,128)(2,1)}, u32[]{:S(2)}, u32[]{:S(2)}) async-start(bf16[8,48,8,512]{3,2,1,0:T(8,128)(2,1)} %get-tuple-element.165), calls=%async_computation.5 | async-start | bytes 6291456 | tf_op jit(solution)/shard_map/all_to_all | solution.py:513
  1113.7 76.3 %all-to-all-start.6 = ((bf16[8,48,16,512]{3,2,1,0:T(8,128)(2,1)}), bf16[8,48,16,512]{3,2,1,0:T(8,128)(2,1)}, u32[]{:S(2)}, u32[]{:S(2)}) async-start(bf16[8,48,16,512]{3,2,1,0:T(8,128)(2,1)} %get-tuple-element.168), calls=%async_computation.6 | async-start | bytes 12582912 | tf_op jit(solution)/shard_map/all_to_all | solution.py:523
  1190.1 76.5 %all-to-all-start.8 = ((bf16[8,48,16,512]{3,2,1,0:T(8,128)(2,1)}), bf16[8,48,16,512]{3,2,1,0:T(8,128)(2,1)}, u32[]{:S(2)}, u32[]{:S(2)}) async-start(bf16[8,48,16,512]{3,2,1,0:T(8,128)(2,1)} %get-tuple-element.173), calls=%async_computation.8 | async-start | bytes 12582912 | tf_op jit(solution)/shard_map/all_to_all | solution.py:523
  1266.6 76.7 %all-to-all-start.7 = ((bf16[8,48,16,512]{3,2,1,0:T(8,128)(2,1)}), bf16[8,48,16,512]{3,2,1,0:T(8,128)(2,1)}, u32[]{:S(2)}, u32[]{:S(2)}) async-start(bf16[8,48,16,512]{3,2,1,0:T(8,128)(2,1)} %get-tuple-element.172), calls=%async_computation.7 | async-start | bytes 12582912 | tf_op jit(solution)/shard_map/all_to_all | solution.py:523
  (97 other events, 149.5 us)

commit v2 on v1

v2 whole, which is shorter than its diff:
```python
import functools
import math

import jax
import jax.numpy as jnp
from jax import lax
from jax.experimental import pallas as pl
from jax.experimental.pallas import tpu as pltpu
from jax.sharding import PartitionSpec as P

kappa_gelu = 0.7978845608
cubic_gelu = 0.044715
smooth_square = 0.25
F32 = jnp.float32
BF16 = jnp.bfloat16
PARAMS = pltpu.CompilerParams(vmem_limit_bytes=48 * 1024 * 1024)


TOKEN = jax.ShapeDtypeStruct((8, 128), F32)
TOKEN_IN = pl.BlockSpec(memory_space=pl.ANY)
TOKEN_OUT = pl.BlockSpec((8, 128), lambda *_: (0, 0))


def strips(rows, columns):
    lanes = math.gcd(columns // 2, 128)
    return pltpu.VMEM((columns // lanes, rows, lanes), F32)


def put_token(token_ref):
    token_ref[...] = jnp.zeros_like(token_ref)


COST = pl.CostEstimate(flops=5 * 10**10, bytes_accessed=1000, transcendentals=0)


def dot(a, b):
    return jnp.dot(a, b, preferred_element_type=F32)


def slope_abs(difference):
    return difference * lax.rsqrt(difference * difference + smooth_square)


def fourier_tables(lon_count, mode_count):
    row = jnp.arange(2 * mode_count)
    part = row // mode_count
    orders = row % mode_count
    positions = jnp.arange(lon_count)
    phase = orders[:, None] * positions[None, :] % lon_count
    angle_grid = phase.astype(F32) * (2.0 * math.pi / lon_count)
    values = jnp.where(part[:, None] == 0, jnp.cos(angle_grid), -jnp.sin(angle_grid))
    factor = jnp.where(orders == 0, 1.0, 2.0).astype(F32)
    synth = (values * factor[:, None]).astype(BF16)
    return synth, values.T.astype(BF16)


def legendre_kernel(
    start_ref, cosine_ref, order_ref, _, out_ref, token_ref, older_ref, newer_ref, log_ref, rows_ref
):
    put_token(token_ref)
    block = out_ref.shape[1]
    order = order_ref[...]
    cosine = cosine_ref[...]

    @pl.when(pl.program_id(0) == 0)
    def _():
        older_ref[...] = jnp.zeros_like(older_ref)
        newer_ref[...] = jnp.zeros_like(newer_ref)
        log_ref[...] = start_ref[...]

    for offset in range(block):
        degree = (pl.program_id(0) * block + offset).astype(F32)
        below = degree - 1.0
        alpha = jnp.sqrt(
            jnp.maximum(4.0 * degree * degree - 1.0, 1.0)
            / jnp.maximum(degree * degree - order * order, 1.0)
        )
        beta = jnp.sqrt(
            jnp.maximum(below * below - order * order, 0.0)
            / jnp.maximum(4.0 * below * below - 1.0, 1.0)
        )
        newer = newer_ref[...]
        log_scale = log_ref[...]
        recurred = alpha * (cosine * newer - beta * older_ref[...])
        fresh = jnp.where(degree < order, 0.0, jnp.where(degree == order, 1.0, recurred))
        rows_ref[:, offset, :] = fresh * jnp.exp(log_scale)
        norm = jnp.where(degree < order, 1.0, jnp.maximum(jnp.abs(fresh), jnp.abs(newer)))
        older_ref[...] = newer / norm
        newer_ref[...] = fresh / norm
        log_ref[...] = log_scale + jnp.log(norm)
    out_ref[...] = rows_ref[...].astype(BF16)


def legendre_table(token, orders, angles, degree_count):
    lat_count = angles.shape[0]
    order_count = orders.shape[0]
    order_f = orders.astype(F32)[:, None]
    factor_index = jnp.arange(1, lat_count + 1).astype(F32)
    ratios = jnp.log((2.0 * factor_index - 1.0) / (2.0 * factor_index))
    partial_log = jnp.sum(jnp.where(factor_index[None, :] <= order_f, ratios[None, :], 0.0), axis=1)
    start_log = (
        0.5 * jnp.log(order_f + 0.5)
        + 0.5 * partial_log[:, None]
        + order_f * jnp.log(jnp.sin(angles))[None, :]
    )
    block = math.gcd(degree_count, 16)
    state = pltpu.VMEM((order_count, lat_count), F32)
    return pl.pallas_call(
        legendre_kernel,
        grid=(degree_count // block,),
        in_specs=[
            pl.BlockSpec((order_count, lat_count), lambda i: (0, 0)),
            pl.BlockSpec((1, lat_count), lambda i: (0, 0)),
            pl.BlockSpec((order_count, 1), lambda i: (0, 0)),
            TOKEN_IN,
        ],
        out_specs=[
            pl.BlockSpec((order_count, block, lat_count), lambda i: (0, i, 0)),
            TOKEN_OUT,
        ],
        out_shape=[
            jax.ShapeDtypeStruct((order_count, degree_count, lat_count), BF16),
            TOKEN,
        ],
        scratch_shapes=[state, state, state, pltpu.VMEM((order_count, block, lat_count), F32)],
        compiler_params=PARAMS,
        cost_estimate=COST,
        name="legendre",
    )(start_log, jnp.cos(angles)[None, :], order_f, token)


def share_of(me_ref, piece, members, share):
    return pl.ds(pl.multiple_of(lax.rem(me_ref[0] + piece, members) * share, share), share)


def forward_row(me_ref, saved_ref, grid_ref, up_ref, down_ref, put):
    members = saved_ref.shape[1] // put.share
    for piece in range(members):
        place = share_of(me_ref, piece, members, put.share)
        v = dot(saved_ref[0, place, :], up_ref[...])
        tanh_part = jnp.tanh(kappa_gelu * (v + cubic_gelu * v * v * v))
        activation = (0.5 * v * (1.0 + tanh_part)).astype(BF16)
        total = grid_ref[0, place, :].astype(F32) + dot(activation, down_ref[...])
        put(piece, total.astype(BF16))


def cotangent_row(row, member_refs, target_ref, weight_ref, put):
    members = len(member_refs)
    weight_block = weight_ref[...]
    lane = lax.broadcasted_iota(jnp.int32, weight_block.shape, 1)
    weight = jnp.sum(jnp.where(lane == row, weight_block, 0.0), axis=1, keepdims=True)
    target = target_ref[0].astype(F32)
    values = [ref[...].reshape(target.shape).astype(F32) for ref in member_refs]
    pairs = {}
    for e in range(members):
        for f in range(e + 1, members):
            pairs[e, f] = slope_abs(values[e] - values[f])
    for e in range(members):
        total = None
        for f in range(members):
            if f == e:
                continue
            term = pairs[e, f] if e < f else -pairs[f, e]
            total = term if total is None else total + term
        direct = slope_abs(values[e] - target)
        put(
            e, (weight * (direct * (1.0 / members) - total * (1.0 / (members * members)))).astype(BF16)
        )


class Put:
    def __init__(self, refs, slot, back):
        self.refs, self.slot, self.back = refs, slot, back
        self.share = refs[0].shape[2]

    def __call__(self, piece, value):
        members = len(self.refs)
        self.refs[(members - piece) % members if self.back else piece][self.slot, 0] = value


def exchange_kernel(members, forward, cotangent, me_ref, *refs):
    refs = list(refs)
    take = lambda count: [refs.pop(0) for _ in range(count)]
    refs.pop(0)
    forward_refs = take(4) if forward is not None else None
    if cotangent is not None:
        target_ref, weight_ref = take(2)
        member_refs = take(members)
    out_refs = take(members)
    put_token(refs[0])
    if forward is not None:
        forward_row(me_ref, *forward_refs, Put(out_refs, 0, False))
    if cotangent is not None:
        put = Put(out_refs, 0 if forward is None else 1, True)
        row = cotangent + pl.program_id(0)
        cotangent_row(row, member_refs, target_ref, weight_ref, put)


def pick(slot, share, channels):
    return pl.BlockSpec((1, 1, share, channels), lambda i, q: (slot, i, 0, 0))


def exchange_rows(
    token, rows, members, me, forward, cotangent, saved, grid_input, up_weight, down_weight, target, weights, values
):
    _, lon, channels = saved.shape
    hidden = up_weight.shape[1]
    share = lon // members
    in_specs, operands = [TOKEN_IN], [me, token]
    if forward is not None:
        row_spec = pl.BlockSpec((1, lon, channels), lambda i, q: (forward + i, 0, 0))
        in_specs += [
            row_spec,
            row_spec,
            pl.BlockSpec((channels, hidden), lambda i, q: (0, 0)),
            pl.BlockSpec((hidden, channels), lambda i, q: (0, 0)),
        ]
        operands += [saved, grid_input, up_weight, down_weight]
    if cotangent is not None:
        in_specs += [
            pl.BlockSpec((1, share, channels), lambda i, q: (cotangent + i, q[0], 0)),
            pl.BlockSpec((share, weights.shape[1]), lambda i, q: (q[0], 0)),
        ]
        in_specs += [pick(slot, share, channels) for _, slot in values]
        operands += [target, weights] + [array for array, _ in values]
    slots = (forward is not None) + (cotangent is not None)
    out_shape = jax.ShapeDtypeStruct((slots, rows, share, channels), BF16)
    return pl.pallas_call(
        functools.partial(exchange_kernel, members, forward, cotangent),
        grid_spec=pltpu.PrefetchScalarGridSpec(
            num_scalar_prefetch=1,
            grid=(rows,),
            in_specs=in_specs,
            out_specs=[pl.BlockSpec((slots, 1, share, channels), lambda i, q: (0, i, 0, 0))] * members
            + [TOKEN_OUT],
        ),
        out_shape=[out_shape] * members + [TOKEN],
        compiler_params=PARAMS,
        cost_estimate=COST,
        name="exchange",
    )(*operands)


def backward_kernel(me_ref, saved_ref, up_ref, down_t_ref, up_t_ref, synth_ref, _, __, *refs):
    members = len(refs) - 4
    out_ref, token_ref, mixed_ref, waves_ref = refs[members:]
    put_token(token_ref)
    lon, channels = mixed_ref.shape
    share = lon // members
    for piece in range(members):
        place = share_of(me_ref, piece, members, share)
        v = dot(saved_ref[0, place, :], up_ref[...])
        square = v * v
        half = 0.5 + 0.5 * jnp.tanh(v * (kappa_gelu + (kappa_gelu * cubic_gelu) * square))
        inner = v * (2.0 * kappa_gelu + (6.0 * kappa_gelu * cubic_gelu) * square)
        slopes = half * (1.0 + (1.0 - half) * inner)
        act_grad = dot(refs[piece][0, 0], down_t_ref[...])
        pre_grad = (act_grad * slopes).astype(BF16)
        mixed_ref[place, :] = dot(pre_grad, up_t_ref[...]).astype(BF16)
    wave = dot(synth_ref[...], mixed_ref[...])
    modes = wave.shape[0] // 2
    row = pl.program_id(0)
    rows = out_ref.shape[2]
    place = pl.ds(row, modes, stride=rows)
    lanes = waves_ref.shape[2]
    for index in range(waves_ref.shape[0]):
        part, lane = divmod(index * lanes, channels)
        waves_ref[index, place, :] = wave[part * modes : (part + 1) * modes, lane : lane + lanes]

    @pl.when(row == rows - 1)
    def _():
        for index in range(waves_ref.shape[0]):
            block = waves_ref[index].reshape(out_ref.shape[:3] + (lanes,))
            out_ref[..., index * lanes : (index + 1) * lanes] = block.astype(BF16)


def backward_rows(token, ahead, first, groups, me, cot, saved, up_weight, down_t, up_t, synth):
    members = len(cot)
    _, rows, share, channels = cot[0][0].shape
    lon = saved.shape[1]
    modes = synth.shape[0] // 2
    whole = lambda a: pl.BlockSpec(a.shape, lambda i, q: (0, 0))
    out_shape = (groups, modes // groups, rows, 2 * channels)
    return pl.pallas_call(
        backward_kernel,
        grid_spec=pltpu.PrefetchScalarGridSpec(
            num_scalar_prefetch=1,
            grid=(rows,),
            in_specs=[
                pl.BlockSpec((1, lon, channels), lambda i, q: (first + i, 0, 0)),
                whole(up_weight),
                whole(down_t),
                whole(up_t),
                whole(synth),
                TOKEN_IN,
                TOKEN_IN,
            ]
            + [pick(slot, share, channels) for _, slot in cot],
            out_specs=[pl.BlockSpec(out_shape, lambda i, q: (0, 0, 0, 0)), TOKEN_OUT],
            scratch_shapes=[
                pltpu.VMEM((lon, channels), BF16),
                strips(modes * rows, 2 * channels),
            ],
        ),
        out_shape=[jax.ShapeDtypeStruct(out_shape, BF16), TOKEN],
        compiler_params=PARAMS,
        cost_estimate=COST,
        name="backward",
    )(me, saved, up_weight, down_t, up_t, synth, token, ahead, *[array for array, _ in cot])


def latitude(joined, table, quad, coeff, out_ref, m):
    groups, _, rows, columns = out_ref.shape
    lat = lax.dot_general(table, coeff, (((0,), (0,)), ((), ())), preferred_element_type=F32)
    lat = (lat * quad).reshape(joined, groups, rows // joined, columns)
    out_ref[:, m] = jnp.concatenate([lat[p] for p in range(joined)], axis=1).astype(BF16)


def spectral_kernel(parts, joined, table_ref, gain_ref, mix_t_ref, quad_ref, _, *refs):
    out_ref, lat_ref, token_ref = refs[parts:]
    put_token(token_ref)
    channels = mix_t_ref.shape[0]
    batch, columns = refs[0].shape[1], refs[0].shape[-1]
    first = quad_ref.shape[0]
    for m in range(batch):
        pieces = [refs[p][:, m].astype(F32).reshape(-1, columns) for p in range(parts)]
        wave = jnp.concatenate(pieces, axis=0).astype(BF16)
        gained = (dot(table_ref[m], wave) * gain_ref[...]).astype(BF16)
        coeff = jnp.concatenate(
            [
                dot(gained[:, :channels], mix_t_ref[...]).astype(BF16),
                dot(gained[:, channels:], mix_t_ref[...]).astype(BF16),
            ],
            axis=1,
        )
        out_ref[m] = coeff
        latitude(joined, table_ref[m, :, :first], quad_ref[...], coeff, lat_ref, m)


def spectral(token, joined, table, gain, mix_t, quad, waves):
    parts = len(waves)
    groups, modes, rows, columns = waves[0].shape
    degrees, lats = table.shape[1:]
    batch = math.gcd(modes, 4)
    lat_rows = joined * rows
    return pl.pallas_call(
        functools.partial(spectral_kernel, parts, joined),
        grid=(modes // batch,),
        in_specs=[
            pl.BlockSpec((batch, degrees, lats), lambda m: (m, 0, 0)),
            pl.BlockSpec(gain.shape, lambda m: (0, 0)),
            pl.BlockSpec(mix_t.shape, lambda m: (0, 0)),
            pl.BlockSpec(quad.shape, lambda m: (0, 0)),
            TOKEN_IN,
        ]
        + [pl.BlockSpec((groups, batch, rows, columns), lambda m: (0, m, 0, 0))] * parts,
        out_specs=[
            pl.BlockSpec((batch, degrees, columns), lambda m: (m, 0, 0)),
            pl.BlockSpec((groups, batch, lat_rows, columns), lambda m: (0, m, 0, 0)),
            TOKEN_OUT,
        ],
        out_shape=[
            jax.ShapeDtypeStruct((modes, degrees, columns), BF16),
            jax.ShapeDtypeStruct((groups, modes, lat_rows, columns), BF16),
            TOKEN,
        ],
        compiler_params=PARAMS,
        cost_estimate=COST,
        name="spectral",
    )(table, gain, mix_t, quad, token, *waves)


def latitude_kernel(joined, table_ref, quad_ref, coeff_ref, _, out_ref, token_ref):
    put_token(token_ref)
    for m in range(out_ref.shape[1]):
        latitude(joined, table_ref[m], quad_ref[...], coeff_ref[m], out_ref, m)


def latitude_rows(token, index, joined, groups, table, quad, coeff):
    modes, degrees, columns = coeff.shape
    lats = quad.shape[0]
    batch = math.gcd(modes, 4)
    out_shape = (groups, modes, lats // groups, columns)
    return pl.pallas_call(
        functools.partial(latitude_kernel, joined),
        grid=(modes // batch,),
        in_specs=[
            pl.BlockSpec((batch, degrees, lats), lambda m: (m, 0, index)),
            pl.BlockSpec(quad.shape, lambda m: (0, 0)),
            pl.BlockSpec((batch, degrees, columns), lambda m: (m, 0, 0)),
            TOKEN_IN,
        ],
        out_specs=[
            pl.BlockSpec((groups, batch, lats // groups, columns), lambda m: (0, m, 0, 0)),
            TOKEN_OUT,
        ],
        out_shape=[jax.ShapeDtypeStruct(out_shape, BF16), TOKEN],
        compiler_params=PARAMS,
        cost_estimate=COST,
        name="latitude",
    )(table, quad, coeff, token)


def output_kernel(joined, members, scale, me_ref, wave_ref, analysis_ref, _, *refs):
    out_ref, token_ref, waves_ref = refs[-3:]
    put_token(token_ref)
    every, share = wave_ref.shape[2], refs[0].shape[2]
    rows = every // joined
    count, _, lanes = waves_ref.shape
    channels = out_ref.shape[-1]
    row = pl.program_id(0)

    @pl.when(row == 0)
    def _():
        for index in range(count):
            block = wave_ref[..., index * lanes : (index + 1) * lanes].astype(F32)
            waves_ref[index] = block.reshape(waves_ref.shape[1:])

    at = pl.ds(row, waves_ref.shape[1] // every, stride=every)
    strip = [waves_ref[index, at, :].astype(BF16) for index in range(count)]
    half = count // 2
    wave = jnp.concatenate(
        [jnp.concatenate(strip[:half], axis=1), jnp.concatenate(strip[half:], axis=1)], axis=0
    )
    for piece in range(members):
        place = share_of(me_ref, piece, members, share)
        spatial = dot(analysis_ref[place, :], wave)
        cot = refs[piece][0, 0]
        for part in range(1, joined):
            cot = jnp.where(row >= part * rows, refs[part * members + piece][0, 0], cot)
        out_ref[0, 0, place, :] = (cot.astype(F32) + spatial * scale).astype(BF16)


def output_rows(token, index, shape, me, wave, cots, analysis, held):
    groups, modes, rows, columns = wave.shape
    joined, members = len(cots), len(cots[0])
    _, each, share, channels = cots[0][0][0].shape
    lon = shape[2]
    in_specs = [
        pl.BlockSpec(wave.shape, lambda i, q: (0, 0, 0, 0)),
        pl.BlockSpec(analysis.shape, lambda i, q: (0, 0)),
        TOKEN_IN,
    ]
    operands = [me, wave, analysis, token]
    for part, cot in enumerate(cots):
        for array, slot in cot:
            place = lambda i, q, at=part * each, slot=slot: (slot, jnp.clip(i - at, 0, each - 1), 0, 0)
            in_specs.append(pl.BlockSpec((1, 1, share, channels), place))
            operands.append(array)
    aliases = {}
    if held is not None:
        in_specs.append(pl.BlockSpec(memory_space=pl.ANY))
        aliases = {len(operands): 0}
        operands.append(held)
    return pl.pallas_call(
        functools.partial(output_kernel, joined, members, 1.0 / lon),
        grid_spec=pltpu.PrefetchScalarGridSpec(
            num_scalar_prefetch=1,
            grid=(rows,),
            in_specs=in_specs,
            out_specs=[
                pl.BlockSpec((1, 1, lon, channels), lambda i, q: (0, index * rows + i, 0, 0)),
                TOKEN_OUT,
            ],
            scratch_shapes=[strips(groups * modes * rows, columns)],
        ),
        out_shape=[jax.ShapeDtypeStruct(shape, BF16), TOKEN],
        input_output_aliases=aliases,
        compiler_params=PARAMS,
        cost_estimate=COST,
        name="output",
    )(*operands)


def shift(pieces):
    members = len(pieces)
    moved = [pieces[0]]
    for piece in range(1, members):
        pairs = [(e, (e + piece) % members) for e in range(members)]
        moved.append(lax.ppermute(pieces[piece], "member", pairs))
    return moved


def after_kernel(*_):
    pass


def after(value, other):
    return pl.pallas_call(
        after_kernel,
        in_specs=[TOKEN_IN, TOKEN_IN],
        out_specs=TOKEN_IN,
        out_shape=jax.ShapeDtypeStruct(value.shape, value.dtype),
        input_output_aliases={0: 0},
        name="after",
    )(value, other)


def kernel_order(parts, ahead):
    order = [("exchange", -ahead), ("exchange", 1 - ahead), ("table", 0)]
    for step in range(2 - ahead, parts + 2):
        order.append(("exchange", step) if step < parts else None)
        order.append(("backward", step - 2) if step >= 2 else None)
    return [entry for entry in order if entry is not None]


def shards(
    grid_input, saved_mixed, target, land_weight, mix_weight, degree_gain, up_weight, down_weight
):
    rows_lat, lon_count, channel_count = grid_input.shape[1:]
    total_lat = degree_gain.shape[0]
    mode_count = lon_count // 2
    members = lax.axis_size("member")
    groups = lax.axis_size("lat")
    local_modes = mode_count // groups
    parts = math.gcd(rows_lat, 6)
    rows = rows_lat // parts
    starts = [part * rows for part in range(parts)]

    grid_rows = grid_input[0]
    saved_rows = saved_mixed[0]
    down_t = down_weight.T
    up_t = up_weight.T
    synth, analysis = fourier_tables(lon_count, mode_count)
    lat_start = lax.axis_index("lat") * rows_lat
    local_angles = ((lat_start + jnp.arange(rows_lat)).astype(F32) + 0.5) * (math.pi / total_lat)
    weights = (jnp.sin(local_angles)[:, None] * land_weight.astype(F32)).T
    me = lax.axis_index("member").astype(jnp.int32).reshape(1)

    lats = jnp.arange(total_lat).reshape(groups, parts, rows).swapaxes(0, 1).reshape(-1)
    angles = (lats.astype(F32) + 0.5) * (math.pi / total_lat)
    quad_weight = (jnp.sin(angles) * (math.pi / total_lat))[:, None]
    local_orders = lax.axis_index("lat") * local_modes + jnp.arange(local_modes)

    joined = 2 if parts % 2 == 0 else 1
    token = jnp.zeros(TOKEN.shape, F32)
    values, cots, waves = {}, {}, {}
    table = None
    ahead = 2
    for kind, part in kernel_order(parts, ahead):
        if kind == "table":
            table, token = legendre_table(token, local_orders, angles, total_lat)
        elif kind == "exchange":
            forward = part + ahead if part + ahead < parts else None
            cotangent = part if part >= 0 else None
            *pieces, token = exchange_rows(
                token,
                rows,
                members,
                me,
                None if forward is None else starts[forward],
                None if cotangent is None else starts[cotangent],
                saved_rows,
                grid_rows,
                up_weight,
                down_weight,
                target,
                weights,
                values.get(cotangent),
            )
            moved = shift(pieces)
            values[forward] = [(array, 0) for array in moved]
            slot = 0 if forward is None else 1
            cots[cotangent] = [(moved[-piece % members], slot) for piece in range(members)]
        else:
            wave, token = backward_rows(
                token,
                waves.get(part - 2, token),
                starts[part],
                groups,
                me,
                cots[part],
                saved_rows,
                up_weight,
                down_t,
                up_t,
                synth,
            )
            if part == parts - 1 and part > 0:
                wave = after(wave, waves[part - 1])
            waves[part] = lax.all_to_all(wave, "lat", 0, 0, tiled=True)
    waves = [waves[part] for part in range(parts)]
    steps = parts // joined
    quads = [
        lax.slice_in_dim(quad_weight, step * total_lat // steps, (step + 1) * total_lat // steps)
        for step in range(steps)
    ]
    coeff, wave, token = spectral(
        token, joined, table, degree_gain[:, None], mix_weight.T, quads[0], waves
    )
    result = None
    lat_waves = {0: lax.all_to_all(wave, "lat", 0, 0, tiled=True)}
    for step in range(steps + 1):
        if 0 < step < steps:
            wave, token = latitude_rows(token, step, joined, groups, table, quads[step], coeff)
            lat_waves[step] = lax.all_to_all(wave, "lat", 0, 0, tiled=True)
        if step > 0:
            result, token = output_rows(
                token,
                step - 1,
                grid_input.shape,
                me,
                lat_waves[step - 1],
                [cots[part] for part in range((step - 1) * joined, step * joined)],
                analysis,
                result,
            )
    return result


def solution(mesh):
    in_specs = (
        P("member", "lat", None, None),
        P("member", "lat", None, None),
        P("lat", None, None),
        P("lat", None),
        P(),
        P(),
        P(),
        P(),
    )
    out_specs = P("member", "lat", None, None)
    return jax.shard_map(shards, mesh=mesh, in_specs=in_specs, out_specs=out_specs, check_vma=False)
```

time: 1390 us -> 1200 us (0.86)
  waiting for transfers between devices: 678 us -> 406 us
  starting transfers between devices: 172 us -> 363 us
  Pallas kernels: 416 us -> 364 us
  local copies, waits for them, and re-layouts: 85.8 us -> 36.2 us
    ppermute x36 -> x24, waiting for transfers between devices: 513 us -> 183 us  [shift(): moved.append(lax.ppermute(pieces[piece], 'member', pairs))]
    ppermute x36 -> x24, starting transfers between devices: 130 us -> 321 us  [shift(): moved.append(lax.ppermute(pieces[piece], 'member', pairs))]
    all_to_all x0 -> x1, waiting for transfers between devices: none -> 55.8 us  [shards(): lat_waves = {0: lax.all_to_all(wave, 'lat', 0, 0, tiled=True)}]
    unnamed x236 -> x112, local copies, waits for them, and re-layouts: 85.3 us -> 35.7 us
    all_to_all x6, waiting for transfers between devices: 37.5 us -> 85.5 us  [shards(): waves[part] = lax.all_to_all(wave, 'lat', 0, 0, tiled=True)]
    all_to_all x3 -> x2, waiting for transfers between devices: 127 us -> 82.2 us  [shards(): lat_waves[step] = lax.all_to_all(wave, 'lat', 0, 0, tiled=True)]
    pallas_call x6, Pallas kernels: 133 us -> 116 us  [backward_rows(): pl.pallas_call(backward_kernel, grid_spec=pltpu.PrefetchScalarGridSpec(nu...]
    pallas_call x3 -> x2, Pallas kernels: 46.7 us -> 31.1 us  [latitude_rows(): pl.pallas_call(functools.partial(latitude_kernel, joined), grid=(modes //...]
  transfers between devices with their start and end apart: 45 -> 33, of which waited for: 21 -> 10; matrix products, arithmetic and copies ran while one was open for 2% -> 2% of each run, Pallas kernels for 15% -> 25%
where the time goes in v2:
time: 1200 us; the launch traced here: 1190 us
  waiting for transfers between devices  406 us (34%)
  Pallas kernels  364 us (30%)
  starting transfers between devices  363 us (30%)
  local copies, waits for them, and re-layouts  36.2 us (3%)
  other arithmetic  22.1 us (2%)
    ppermute x24, starting transfers between devices, shift(): moved.append(lax.ppermute(pieces[piece], 'member', pairs))  321 us
    ppermute x24, waiting for transfers between devices, shift(): moved.append(lax.ppermute(pieces[piece], 'member', pairs))  183 us
    pallas_call x6, Pallas kernels, backward_rows(): pl.pallas_call(backward_kernel, grid_spec=pltpu.PrefetchScalarGridSpec(nu...  116 us
    pallas_call x8, Pallas kernels, exchange_rows(): pl.pallas_call(functools.partial(exchange_kernel, members, forward, cotan...  89 us
    all_to_all x6, waiting for transfers between devices, shards(): waves[part] = lax.all_to_all(wave, 'lat', 0, 0, tiled=True)  85.5 us
    all_to_all x2, waiting for transfers between devices, shards(): lat_waves[step] = lax.all_to_all(wave, 'lat', 0, 0, tiled=True)  82.2 us
    pallas_call x3, Pallas kernels, output_rows(): pl.pallas_call(functools.partial(output_kernel, joined, members, 1.0 / lo...  60 us
    all_to_all x1, waiting for transfers between devices, shards(): lat_waves = {0: lax.all_to_all(wave, 'lat', 0, 0, tiled=True)}  55.8 us
  transfers between devices with their start and end apart: 33, of which 10 were waited for; matrix products, arithmetic and copies ran while one was open for 2% of the time, Pallas kernels for 25%

profile of v2, /device:TPU:0, one launch (start us, length us, event | category | flops | bytes accessed | tf_op | source)
XLA Modules:
  0.0 1192.1 jit_solution(4912937629960215990)
XLA Ops:
  1.9 9.6 exchange.8
  12.4 3.0 collective-permute-start
  15.4 2.6 collective-permute-start.1
  19.4 9.3 exchange.9
  32.3 36.6 %legendre.1 = (bf16[48,384,384]{2,1,0:T(8,128)(2,1)}, f32[8,128]{1,0:T(8,128)S(1)}) custom-call(f32[48,384]{1,0:T(8,128)S(1)} %multiply_add_fusion.start_ref, f32[1,384]{1,0:T(1,128)S(1)} %reshape.204.cosine_ref, f32[48,1]{1,0:T(8,128)S(1)} %add_convert_fusion.order_ref, f32[8,128]{1,0:T(8,128)S(1)} %get-tuple-element.72._), custom_call_target="tpu_custom_call" | custom-call | flops 49999998976 | bytes 1000 | tf_op jit(solution)/shard_map/legendre/pallas_call | solution.py:108
  69.5 21.4 %select_convert_fusion = (bf16[768,768]{1,0:T(8,128)(2,1)}, bf16[768,768]{1,0:T(8,128)(2,1)S(1)}) fusion(s32[768]{0:T(1024)S(1)} %fusion.14, pred[768]{0:T(1024)(128)(4,1)S(1)} %fusion.20, f32[768]{0:T(1024)S(1)} %compare_select_fusion), kind=kLoop, calls=%fused_computation.6 | loop fusion | flops 14745600 | bytes 2366208 | tf_op jit(solution)/shard_map/convert_element_type | solution.py:54
  90.8 2.9 collective-permute-start.5
  93.7 13.1 %exchange.10 = (bf16[2,8,192,256]{3,2,1,0:T(8,128)(2,1)S(1)}, bf16[2,8,192,256]{3,2,1,0:T(8,128)(2,1)}, bf16[2,8,192,256]{3,2,1,0:T(8,128)(2,1)}, bf16[2,8,192,256]{3,2,1,0:T(8,128)(2,1)}, f32[8,128]{1,0:T(8,128)S(1)}) custom-call(s32[1]{0:T(128)} %bitcast.me_ref, f32[8,128]{1,0:T(8,128)S(1)} %get-tuple-element.74.refs_0_, bf16[48,768,256]{2,1,0:T(8,128)(2,1)} %bitcast.29, ...), custom_call_target="tpu_custom_call" | custom-call | flops 49999998976 | bytes 1000 | tf_op jit(solution)/shard_map/exchange/pallas_call | solution.py:228
  108.0 27.4 %collective-permute-start.6 = (bf16[2,8,192,256]{3,2,1,0:T(8,128)(2,1)}, bf16[2,8,192,256]{3,2,1,0:T(8,128)(2,1)S(1)}, u32[]{:S(2)}, u32[]{:S(2)}) collective-permute-start(bf16[2,8,192,256]{3,2,1,0:T(8,128)(2,1)} %get-tuple-element.86), channel_id=1, source_target_pairs={{0,8},{8,16},{16,24},{24,0},{1,9},{9,17},{17,25},{25,1},{2,10},{10... | collective-permute-start | bytes 4718600 | tf_op jit(solution)/shard_map/ppermute | solution.py:480
  135.4 1.9 collective-permute-start.7
  137.7 64.2 %collective-permute-done.4.refs_9_ = bf16[1,8,192,256]{3,2,1,0:T(8,128)(2,1)S(1)} collective-permute-done((bf16[1,8,192,256]{3,2,1,0:T(8,128)(2,1)}, bf16[1,8,192,256]{3,2,1,0:T(8,128)(2,1)S(1)}, u32[]{:S(2)}, u32[]{:S(2)}) %collective-permute-start.4) | collective-permute-done | bytes 786464 | tf_op jit(solution)/shard_map/ppermute | solution.py:480
  201.9 12.7 %exchange.11 = (bf16[2,8,192,256]{3,2,1,0:T(8,128)(2,1)S(1)}, bf16[2,8,192,256]{3,2,1,0:T(8,128)(2,1)}, bf16[2,8,192,256]{3,2,1,0:T(8,128)(2,1)}, bf16[2,8,192,256]{3,2,1,0:T(8,128)(2,1)}, f32[8,128]{1,0:T(8,128)S(1)}) custom-call(s32[1]{0:T(128)} %bitcast.me_ref, f32[8,128]{1,0:T(8,128)S(1)} %get-tuple-element.79.refs_0_, bf16[48,768,256]{2,1,0:T(8,128)(2,1)} %bitcast.30, ...), custom_call_target="tpu_custom_call" | custom-call | flops 49999998976 | bytes 1000 | tf_op jit(solution)/shard_map/exchange/pallas_call | solution.py:228
  215.7 18.4 %collective-permute-start.10 = (bf16[2,8,192,256]{3,2,1,0:T(8,128)(2,1)}, bf16[2,8,192,256]{3,2,1,0:T(8,128)(2,1)}, u32[]{:S(2)}, u32[]{:S(2)}) collective-permute-start(bf16[2,8,192,256]{3,2,1,0:T(8,128)(2,1)} %get-tuple-element.93), channel_id=1, source_target_pairs={{0,16},{8,24},{16,0},{24,8},{1,17},{9,25},{17,1},{25,9},{2,18},{10... | collective-permute-start | bytes 4718600 | tf_op jit(solution)/shard_map/ppermute | solution.py:480
  234.1 3.4 collective-permute-start.11
  237.5 84.5 %collective-permute-start.9 = (bf16[2,8,192,256]{3,2,1,0:T(8,128)(2,1)}, bf16[2,8,192,256]{3,2,1,0:T(8,128)(2,1)}, u32[]{:S(2)}, u32[]{:S(2)}) collective-permute-start(bf16[2,8,192,256]{3,2,1,0:T(8,128)(2,1)} %get-tuple-element.92), channel_id=1, source_target_pairs={{0,8},{8,16},{16,24},{24,0},{1,9},{9,17},{17,25},{25,1},{2,10},{10... | collective-permute-start | bytes 4718600 | tf_op jit(solution)/shard_map/ppermute | solution.py:480
  323.7 13.3 %exchange.12 = (bf16[2,8,192,256]{3,2,1,0:T(8,128)(2,1)S(1)}, bf16[2,8,192,256]{3,2,1,0:T(8,128)(2,1)}, bf16[2,8,192,256]{3,2,1,0:T(8,128)(2,1)}, bf16[2,8,192,256]{3,2,1,0:T(8,128)(2,1)}, f32[8,128]{1,0:T(8,128)S(1)}) custom-call(s32[1]{0:T(128)} %bitcast.me_ref, f32[8,128]{1,0:T(8,128)S(1)} %get-tuple-element.84.refs_0_, bf16[48,768,256]{2,1,0:T(8,128)(2,1)} %bitcast.31, ...), custom_call_target="tpu_custom_call" | custom-call | flops 49999998976 | bytes 1000 | tf_op jit(solution)/shard_map/exchange/pallas_call | solution.py:228
  338.1 33.6 %collective-permute-start.12 = (bf16[2,8,192,256]{3,2,1,0:T(8,128)(2,1)}, bf16[2,8,192,256]{3,2,1,0:T(8,128)(2,1)}, u32[]{:S(2)}, u32[]{:S(2)}) collective-permute-start(bf16[2,8,192,256]{3,2,1,0:T(8,128)(2,1)} %get-tuple-element.98), channel_id=1, source_target_pairs={{0,8},{8,16},{16,24},{24,0},{1,9},{9,17},{17,25},{25,1},{2,10},{10... | collective-permute-start | bytes 4718600 | tf_op jit(solution)/shard_map/ppermute | solution.py:480
  371.7 3.3 collective-permute-start.13
  375.0 1.4 copy-done.7
  376.4 19.2 %backward.6 = (bf16[8,48,8,512]{3,2,1,0:T(8,128)(2,1)}, f32[8,128]{1,0:T(8,128)S(1)}) custom-call(s32[1]{0:T(128)} %bitcast.me_ref, bf16[48,768,256]{2,1,0:T(8,128)(2,1)} %bitcast.32, bf16[256,512]{1,0:T(8,128)(2,1)S(1)} %copy-done.3, bf16[256,512]{1,0:T(8,128)(2,1)S(1)} %bitcast.8, bf16[512,256]{1,0:T(8,128)(2,1)S(1)} %bitcast.14, ...), custom_call_target="tpu_custom_call" | custom-call | flops 49999998976 | bytes 1000 | tf_op jit(solution)/shard_map/backward/pallas_call | solution.py:284
  395.7 4.5 all-to-all-start
  400.1 56.6 %collective-permute-done.10.refs_9_.refs_2_.refs_6_ = bf16[2,8,192,256]{3,2,1,0:T(8,128)(2,1)} collective-permute-done((bf16[2,8,192,256]{3,2,1,0:T(8,128)(2,1)}, bf16[2,8,192,256]{3,2,1,0:T(8,128)(2,1)}, u32[]{:S(2)}, u32[]{:S(2)}) %collective-permute-start.10) | collective-permute-done | bytes 1572896 | tf_op jit(solution)/shard_map/ppermute | solution.py:480
  458.0 13.3 %exchange.13 = (bf16[2,8,192,256]{3,2,1,0:T(8,128)(2,1)S(1)}, bf16[2,8,192,256]{3,2,1,0:T(8,128)(2,1)}, bf16[2,8,192,256]{3,2,1,0:T(8,128)(2,1)}, bf16[2,8,192,256]{3,2,1,0:T(8,128)(2,1)}, f32[8,128]{1,0:T(8,128)S(1)}) custom-call(s32[1]{0:T(128)} %bitcast.me_ref, f32[8,128]{1,0:T(8,128)S(1)} %get-tuple-element.90.refs_0_, bf16[48,768,256]{2,1,0:T(8,128)(2,1)} %bitcast.33, ...), custom_call_target="tpu_custom_call" | custom-call | flops 49999998976 | bytes 1000 | tf_op jit(solution)/shard_map/exchange/pallas_call | solution.py:228
  472.5 34.2 %collective-permute-start.15 = (bf16[2,8,192,256]{3,2,1,0:T(8,128)(2,1)}, bf16[2,8,192,256]{3,2,1,0:T(8,128)(2,1)}, u32[]{:S(2)}, u32[]{:S(2)}) collective-permute-start(bf16[2,8,192,256]{3,2,1,0:T(8,128)(2,1)} %get-tuple-element.105), channel_id=1, source_target_pairs={{0,8},{8,16},{16,24},{24,0},{1,9},{9,17},{17,25},{25,1},{2,10},{10... | collective-permute-start | bytes 4718600 | tf_op jit(solution)/shard_map/ppermute | solution.py:480
  506.6 1.4 copy-done.10
  508.0 19.5 %backward.7 = (bf16[8,48,8,512]{3,2,1,0:T(8,128)(2,1)}, f32[8,128]{1,0:T(8,128)S(1)}) custom-call(s32[1]{0:T(128)} %bitcast.me_ref, bf16[48,768,256]{2,1,0:T(8,128)(2,1)} %bitcast.34, bf16[256,512]{1,0:T(8,128)(2,1)S(1)} %copy-done.3, bf16[256,512]{1,0:T(8,128)(2,1)S(1)} %bitcast.9, bf16[512,256]{1,0:T(8,128)(2,1)S(1)} %bitcast.15, ...), custom_call_target="tpu_custom_call" | custom-call | flops 49999998976 | bytes 1000 | tf_op jit(solution)/shard_map/backward/pallas_call | solution.py:284
  527.5 2.4 collective-permute-start.17
  529.9 61.8 %collective-permute-done.13.refs_5_.refs_2_ = bf16[2,8,192,256]{3,2,1,0:T(8,128)(2,1)} collective-permute-done((bf16[2,8,192,256]{3,2,1,0:T(8,128)(2,1)}, bf16[2,8,192,256]{3,2,1,0:T(8,128)(2,1)}, u32[]{:S(2)}, u32[]{:S(2)}) %collective-permute-start.13) | collective-permute-done | bytes 1572896 | tf_op jit(solution)/shard_map/ppermute | solution.py:480
  592.9 9.0 exchange.14
  602.8 36.4 %collective-permute-start.18 = (bf16[1,8,192,256]{3,2,1,0:T(8,128)(2,1)}, bf16[1,8,192,256]{3,2,1,0:T(8,128)(2,1)}, u32[]{:S(2)}, u32[]{:S(2)}) collective-permute-start(bf16[1,8,192,256]{3,2,1,0:T(8,128)(2,1)} %get-tuple-element.113), channel_id=1, source_target_pairs={{0,24},{8,0},{16,8},{24,16},{1,25},{9,1},{17,9},{25,17},{2,26},{10... | collective-permute-start | bytes 2359304 | tf_op jit(solution)/shard_map/ppermute | solution.py:480
  639.2 4.6 all-to-all-start.1
  645.1 1.4 copy-done.35
  646.5 19.5 %backward.8 = (bf16[8,48,8,512]{3,2,1,0:T(8,128)(2,1)}, f32[8,128]{1,0:T(8,128)S(1)}) custom-call(s32[1]{0:T(128)} %bitcast.me_ref, bf16[48,768,256]{2,1,0:T(8,128)(2,1)} %bitcast.35, bf16[256,512]{1,0:T(8,128)(2,1)S(1)} %copy-done.3, bf16[256,512]{1,0:T(8,128)(2,1)S(1)} %bitcast.10, bf16[512,256]{1,0:T(8,128)(2,1)S(1)} %bitcast.16, ...), custom_call_target="tpu_custom_call" | custom-call | flops 49999998976 | bytes 1000 | tf_op jit(solution)/shard_map/backward/pallas_call | solution.py:284
  665.9 27.0 %collective-permute-start.20 = (bf16[1,8,192,256]{3,2,1,0:T(8,128)(2,1)}, bf16[1,8,192,256]{3,2,1,0:T(8,128)(2,1)S(1)}, u32[]{:S(2)}, u32[]{:S(2)}) collective-permute-start(bf16[1,8,192,256]{3,2,1,0:T(8,128)(2,1)} %get-tuple-element.115), channel_id=1, source_target_pairs={{0,8},{8,16},{16,24},{24,0},{1,9},{9,17},{17,25},{25,1},{2,10},{10... | collective-permute-start | bytes 2359304 | tf_op jit(solution)/shard_map/ppermute | solution.py:480
  692.9 8.8 exchange.15
  702.6 36.4 %collective-permute-start.21 = (bf16[1,8,192,256]{3,2,1,0:T(8,128)(2,1)}, bf16[1,8,192,256]{3,2,1,0:T(8,128)(2,1)S(1)}, u32[]{:S(2)}, u32[]{:S(2)}) collective-permute-start(bf16[1,8,192,256]{3,2,1,0:T(8,128)(2,1)} %get-tuple-element.119), channel_id=1, source_target_pairs={{0,24},{8,0},{16,8},{24,16},{1,25},{9,1},{17,9},{25,17},{2,26},{10... | collective-permute-start | bytes 2359304 | tf_op jit(solution)/shard_map/ppermute | solution.py:480
  739.0 4.5 all-to-all-start.2
  744.8 1.4 copy-done.39
  746.2 19.3 %backward.9 = (bf16[8,48,8,512]{3,2,1,0:T(8,128)(2,1)}, f32[8,128]{1,0:T(8,128)S(1)}) custom-call(s32[1]{0:T(128)} %bitcast.me_ref, bf16[48,768,256]{2,1,0:T(8,128)(2,1)} %bitcast.36, bf16[256,512]{1,0:T(8,128)(2,1)S(1)} %copy-done.3, bf16[256,512]{1,0:T(8,128)(2,1)S(1)} %bitcast.11, bf16[512,256]{1,0:T(8,128)(2,1)S(1)} %bitcast.17, ...), custom_call_target="tpu_custom_call" | custom-call | flops 49999998976 | bytes 1000 | tf_op jit(solution)/shard_map/backward/pallas_call | solution.py:284
  765.5 15.9 %all-to-all-done.2.__.refs_2_ = bf16[8,48,8,512]{3,2,1,0:T(8,128)(2,1)} async-done(((bf16[8,48,8,512]{3,2,1,0:T(8,128)(2,1)}), bf16[8,48,8,512]{3,2,1,0:T(8,128)(2,1)}, u32[]{:S(2)}, u32[]{:S(2)}) %all-to-all-start.2) | async-done | bytes 3145760 | tf_op jit(solution)/shard_map/all_to_all | solution.py:581
  781.4 4.5 all-to-all-start.3
  786.5 1.5 copy-done.26
  789.2 19.3 %backward.10 = (bf16[8,48,8,512]{3,2,1,0:T(8,128)(2,1)}, f32[8,128]{1,0:T(8,128)S(1)}) custom-call(s32[1]{0:T(128)} %bitcast.me_ref, bf16[48,768,256]{2,1,0:T(8,128)(2,1)} %bitcast.37, bf16[256,512]{1,0:T(8,128)(2,1)S(1)} %copy-done.3, bf16[256,512]{1,0:T(8,128)(2,1)S(1)} %bitcast.12, bf16[512,256]{1,0:T(8,128)(2,1)S(1)} %bitcast.18, ...), custom_call_target="tpu_custom_call" | custom-call | flops 49999998976 | bytes 1000 | tf_op jit(solution)/shard_map/backward/pallas_call | solution.py:284
  808.5 15.2 %all-to-all-done.3.__.refs_3_ = bf16[8,48,8,512]{3,2,1,0:T(8,128)(2,1)} async-done(((bf16[8,48,8,512]{3,2,1,0:T(8,128)(2,1)}), bf16[8,48,8,512]{3,2,1,0:T(8,128)(2,1)}, u32[]{:S(2)}, u32[]{:S(2)}) %all-to-all-start.3) | async-done | bytes 3145760 | tf_op jit(solution)/shard_map/all_to_all | solution.py:581
  823.7 4.6 all-to-all-start.4
  828.4 1.5 copy-done.27
  829.9 19.3 %backward.11 = (bf16[8,48,8,512]{3,2,1,0:T(8,128)(2,1)}, f32[8,128]{1,0:T(8,128)S(1)}) custom-call(s32[1]{0:T(128)} %bitcast.me_ref, bf16[48,768,256]{2,1,0:T(8,128)(2,1)} %bitcast.38, bf16[256,512]{1,0:T(8,128)(2,1)S(1)} %copy-done.3, bf16[256,512]{1,0:T(8,128)(2,1)S(1)} %bitcast.13, bf16[512,256]{1,0:T(8,128)(2,1)S(1)} %bitcast.19, ...), custom_call_target="tpu_custom_call" | custom-call | flops 49999998976 | bytes 1000 | tf_op jit(solution)/shard_map/backward/pallas_call | solution.py:284
  849.2 17.0 %all-to-all-done.4.__1_.refs_4_ = bf16[8,48,8,512]{3,2,1,0:T(8,128)(2,1)} async-done(((bf16[8,48,8,512]{3,2,1,0:T(8,128)(2,1)}), bf16[8,48,8,512]{3,2,1,0:T(8,128)(2,1)}, u32[]{:S(2)}, u32[]{:S(2)}) %all-to-all-start.4) | async-done | bytes 3145760 | tf_op jit(solution)/shard_map/all_to_all | solution.py:581
  866.2 4.6 all-to-all-start.5
  871.3 37.4 %all-to-all-done.5.refs_5_ = bf16[8,48,8,512]{3,2,1,0:T(8,128)(2,1)} async-done(((bf16[8,48,8,512]{3,2,1,0:T(8,128)(2,1)}), bf16[8,48,8,512]{3,2,1,0:T(8,128)(2,1)}, u32[]{:S(2)}, u32[]{:S(2)}) %all-to-all-start.5) | async-done | bytes 3145760 | tf_op jit(solution)/shard_map/all_to_all | solution.py:581
  908.7 30.9 %spectral.1 = (bf16[48,384,512]{2,1,0:T(8,128)(2,1)}, bf16[8,48,16,512]{3,2,1,0:T(8,128)(2,1)}, f32[8,128]{1,0:T(8,128)S(1)}) custom-call(bf16[48,384,384]{2,1,0:T(8,128)(2,1)} %get-tuple-element.73.table_ref, f32[384,1]{1,0:T(8,128)S(1)} %broadcast_in_dim.70.gain_ref, bf16[256,256]{1,0:T(8,128)(2,1)S(1)} %bitcast.20, f32[128,1]{1,0:T(8,128)S(1)} %slice.28.quad_ref, ...), custom_call_target="tpu_custom_call" | custom-call | flops 49999998976 | bytes 1000 | tf_op jit(solution)/shard_map/spectral/pallas_call | solution.py:346
  939.6 4.8 all-to-all-start.6
  944.6 15.6 %latitude.2 = (bf16[8,48,16,512]{3,2,1,0:T(8,128)(2,1)}, f32[8,128]{1,0:T(8,128)S(1)}) custom-call(bf16[48,384,384]{2,1,0:T(8,128)(2,1)} %get-tuple-element.73.table_ref, f32[128,1]{1,0:T(8,128)S(1)} %slice.29.quad_ref, bf16[48,384,512]{2,1,0:T(8,128)(2,1)} %get-tuple-element.125.coeff_ref, f32[8,128]{1,0:T(8,128)S(1)} %get-tuple-element.127._), custom_call_target="tpu_custom_call" | custom-call | flops 49999998976 | bytes 1000 | tf_op jit(solution)/shard_map/latitude/pallas_call | solution.py:384
  960.2 55.8 %all-to-all-done.6.wave_ref = bf16[8,48,16,512]{3,2,1,0:T(8,128)(2,1)} async-done(((bf16[8,48,16,512]{3,2,1,0:T(8,128)(2,1)}), bf16[8,48,16,512]{3,2,1,0:T(8,128)(2,1)}, u32[]{:S(2)}, u32[]{:S(2)}) %all-to-all-start.6) | async-done | bytes 6291488 | tf_op jit(solution)/shard_map/all_to_all | solution.py:592
  1016.0 5.3 all-to-all-start.8
  1022.6 1.4 copy-done.30
  1024.0 19.8 %output.3 = (bf16[1,48,768,256]{3,2,1,0:T(8,128)(2,1)}, f32[8,128]{1,0:T(8,128)S(1)}) custom-call(s32[1]{0:T(128)} %bitcast.me_ref, bf16[8,48,16,512]{3,2,1,0:T(8,128)(2,1)} %all-to-all-done.6.wave_ref, bf16[768,768]{1,0:T(8,128)(2,1)S(1)} %copy-done.20, f32[8,128]{1,0:T(8,128)S(1)} %get-tuple-element.128._, bf16[2,8,192,256]{3,2,1,0:T(8,128)(2,1)S(1)} %copy-done.30, ...), custom_call_target="tpu_custom_call" | custom-call | flops 49999998976 | bytes 1000 | tf_op jit(solution)/shard_map/output/pallas_call | solution.py:455
  1043.8 15.6 %latitude.3 = (bf16[8,48,16,512]{3,2,1,0:T(8,128)(2,1)}, f32[8,128]{1,0:T(8,128)S(1)}) custom-call(bf16[48,384,384]{2,1,0:T(8,128)(2,1)} %get-tuple-element.73.table_ref, f32[128,1]{1,0:T(8,128)S(1)} %slice.27.quad_ref, bf16[48,384,512]{2,1,0:T(8,128)(2,1)} %get-tuple-element.125.coeff_ref, f32[8,128]{1,0:T(8,128)S(1)} %get-tuple-element.129._), custom_call_target="tpu_custom_call" | custom-call | flops 49999998976 | bytes 1000 | tf_op jit(solution)/shard_map/latitude/pallas_call | solution.py:384
  1059.4 33.6 %all-to-all-done.8.wave_ref = bf16[8,48,16,512]{3,2,1,0:T(8,128)(2,1)} async-done(((bf16[8,48,16,512]{3,2,1,0:T(8,128)(2,1)}), bf16[8,48,16,512]{3,2,1,0:T(8,128)(2,1)}, u32[]{:S(2)}, u32[]{:S(2)}) %all-to-all-start.8) | async-done | bytes 6291488 | tf_op jit(solution)/shard_map/all_to_all | solution.py:596
  1092.9 4.9 all-to-all-start.7
  1099.1 1.4 copy-done.36
  1100.5 20.3 %output.4 = (bf16[1,48,768,256]{3,2,1,0:T(8,128)(2,1)}, f32[8,128]{1,0:T(8,128)S(1)}) custom-call(s32[1]{0:T(128)} %bitcast.me_ref, bf16[8,48,16,512]{3,2,1,0:T(8,128)(2,1)} %all-to-all-done.8.wave_ref, bf16[768,768]{1,0:T(8,128)(2,1)S(1)} %copy-done.21, f32[8,128]{1,0:T(8,128)S(1)} %get-tuple-element.132._, ...), custom_call_target="tpu_custom_call", output_to_operand_aliasing={{0}: (12, {})} | custom-call | flops 49999998976 | bytes 1000 | tf_op jit(solution)/shard_map/output/pallas_call | solution.py:455
  1120.8 48.6 %all-to-all-done.7.wave_ref = bf16[8,48,16,512]{3,2,1,0:T(8,128)(2,1)} async-done(((bf16[8,48,16,512]{3,2,1,0:T(8,128)(2,1)}), bf16[8,48,16,512]{3,2,1,0:T(8,128)(2,1)}, u32[]{:S(2)}, u32[]{:S(2)}) %all-to-all-start.7) | async-done | bytes 6291488 | tf_op jit(solution)/shard_map/all_to_all | solution.py:596
  1171.7 20.0 %output.5 = (bf16[1,48,768,256]{3,2,1,0:T(8,128)(2,1)}, f32[8,128]{1,0:T(8,128)}) custom-call(s32[1]{0:T(128)} %bitcast.me_ref, bf16[8,48,16,512]{3,2,1,0:T(8,128)(2,1)} %all-to-all-done.7.wave_ref, bf16[768,768]{1,0:T(8,128)(2,1)} %get-tuple-element.140.analysis_ref, f32[8,128]{1,0:T(8,128)S(1)} %get-tuple-element.134._, ...), custom_call_target="tpu_custom_call", output_to_operand_aliasing={{0}: (12, {})} | custom-call | flops 49999998976 | bytes 1000 | tf_op jit(solution)/shard_map/output/pallas_call | solution.py:455
  (160 shorter events, 29.0 us)
Async XLA Ops:
  1.9 17.5 %copy-start.1 = (bf16[512,256]{1,0:T(8,128)(2,1)S(1)}, bf16[512,256]{1,0:T(8,128)(2,1)}, u32[]{:S(2)}) copy-start(bf16[512,256]{1,0:T(8,128)(2,1)} %refs_4_.11) | copy-start | bytes 786436
  12.4 78.4 %collective-permute-start = (bf16[1,8,192,256]{3,2,1,0:T(8,128)(2,1)}, bf16[1,8,192,256]{3,2,1,0:T(8,128)(2,1)}, u32[]{:S(2)}, u32[]{:S(2)}) collective-permute-start(bf16[1,8,192,256]{3,2,1,0:T(8,128)(2,1)} %get-tuple-element.76), channel_id=1, source_target_pairs={{0,8},{8,16},{16,24},{24,0},{1,9},{9,17},{17,25},{25,1},{2,10},{10... | collective-permute-start | bytes 2359304 | tf_op jit(solution)/shard_map/ppermute | solution.py:480
  15.4 78.3 %collective-permute-start.1 = (bf16[1,8,192,256]{3,2,1,0:T(8,128)(2,1)}, bf16[1,8,192,256]{3,2,1,0:T(8,128)(2,1)}, u32[]{:S(2)}, u32[]{:S(2)}) collective-permute-start(bf16[1,8,192,256]{3,2,1,0:T(8,128)(2,1)} %get-tuple-element.77), channel_id=1, source_target_pairs={{0,16},{8,24},{16,0},{24,8},{1,17},{9,25},{17,1},{25,9},{2,18},{10... | collective-permute-start | bytes 2359304 | tf_op jit(solution)/shard_map/ppermute | solution.py:480
  18.0 75.7 %collective-permute-start.2 = (bf16[1,8,192,256]{3,2,1,0:T(8,128)(2,1)}, bf16[1,8,192,256]{3,2,1,0:T(8,128)(2,1)}, u32[]{:S(2)}, u32[]{:S(2)}) collective-permute-start(bf16[1,8,192,256]{3,2,1,0:T(8,128)(2,1)} %get-tuple-element.78), channel_id=1, source_target_pairs={{0,24},{8,0},{16,8},{24,16},{1,25},{9,1},{17,9},{25,17},{2,26},{10... | collective-permute-start | bytes 2359304 | tf_op jit(solution)/shard_map/ppermute | solution.py:480
  30.5 106.7 %collective-permute-start.3 = (bf16[1,8,192,256]{3,2,1,0:T(8,128)(2,1)}, bf16[1,8,192,256]{3,2,1,0:T(8,128)(2,1)S(1)}, u32[]{:S(2)}, u32[]{:S(2)}) collective-permute-start(bf16[1,8,192,256]{3,2,1,0:T(8,128)(2,1)} %get-tuple-element.81), channel_id=1, source_target_pairs={{0,8},{8,16},{16,24},{24,0},{1,9},{9,17},{17,25},{25,1},{2,10},{10... | collective-permute-start | bytes 2359304 | tf_op jit(solution)/shard_map/ppermute | solution.py:480
  31.2 170.7 %collective-permute-start.4 = (bf16[1,8,192,256]{3,2,1,0:T(8,128)(2,1)}, bf16[1,8,192,256]{3,2,1,0:T(8,128)(2,1)S(1)}, u32[]{:S(2)}, u32[]{:S(2)}) collective-permute-start(bf16[1,8,192,256]{3,2,1,0:T(8,128)(2,1)} %get-tuple-element.82), channel_id=1, source_target_pairs={{0,16},{8,24},{16,0},{24,8},{1,17},{9,25},{17,1},{25,9},{2,18},{10... | collective-permute-start | bytes 2359304 | tf_op jit(solution)/shard_map/ppermute | solution.py:480
  32.3 36.8 %copy-start.3 = (bf16[256,512]{1,0:T(8,128)(2,1)S(1)}, bf16[256,512]{1,0:T(8,128)(2,1)}, u32[]{:S(2)}) copy-start(bf16[256,512]{1,0:T(8,128)(2,1)} %up_ref.11) | copy-start | bytes 786436
  32.3 36.9 %copy-start.50 = (s32[48,768]{1,0:T(8,128)S(1)}, s32[48,768]{1,0:T(8,128)}, u32[]{:S(2)}) copy-start(s32[48,768]{1,0:T(8,128)} %param.11) | copy-start | bytes 442372
  69.4 21.4 %copy-start.19 = (bf16[1,8,192,256]{3,2,1,0:T(8,128)(2,1)S(1)}, bf16[1,8,192,256]{3,2,1,0:T(8,128)(2,1)}, u32[]{:S(2)}) copy-start(bf16[1,8,192,256]{3,2,1,0:T(8,128)(2,1)} %copy-done.18) | copy-start | bytes 2359300
  69.5 24.3 %copy-start.43 = (bf16[1,8,192,256]{3,2,1,0:T(8,128)(2,1)S(1)}, bf16[1,8,192,256]{3,2,1,0:T(8,128)(2,1)}, u32[]{:S(2)}) copy-start(bf16[1,8,192,256]{3,2,1,0:T(8,128)(2,1)} %copy-done.42) | copy-start | bytes 2359300
  90.8 284.2 %copy-start.22 = (bf16[768,768]{1,0:T(8,128)(2,1)}, bf16[768,768]{1,0:T(8,128)(2,1)S(1)}, u32[]{:S(2)}) copy-start(bf16[768,768]{1,0:T(8,128)(2,1)S(1)} %get-tuple-element.141.synth_ref) | copy-start | bytes 3538948
  90.8 111.0 %collective-permute-start.5 = (bf16[1,8,192,256]{3,2,1,0:T(8,128)(2,1)S(1)}, bf16[1,8,192,256]{3,2,1,0:T(8,128)(2,1)S(1)}, u32[]{:S(2)}, u32[]{:S(2)}) collective-permute-start(bf16[1,8,192,256]{3,2,1,0:T(8,128)(2,1)S(1)} %copy-done.19), channel_id=1, source_target_pairs={{0,24},{8,0},{16,8},{24,16},{1,25},{9,1},{17,9},{25,17},{2,26},{10... | collective-permute-start | bytes 2359304 | tf_op jit(solution)/shard_map/ppermute | solution.py:480
  93.7 108.2 %copy-start.41 = (bf16[1,8,192,256]{3,2,1,0:T(8,128)(2,1)S(1)}, bf16[1,8,192,256]{3,2,1,0:T(8,128)(2,1)}, u32[]{:S(2)}) copy-start(bf16[1,8,192,256]{3,2,1,0:T(8,128)(2,1)} %copy-done.40) | copy-start | bytes 2359300
  108.0 129.5 %collective-permute-start.6 = (bf16[2,8,192,256]{3,2,1,0:T(8,128)(2,1)}, bf16[2,8,192,256]{3,2,1,0:T(8,128)(2,1)S(1)}, u32[]{:S(2)}, u32[]{:S(2)}) collective-permute-start(bf16[2,8,192,256]{3,2,1,0:T(8,128)(2,1)} %get-tuple-element.86), channel_id=1, source_target_pairs={{0,8},{8,16},{16,24},{24,0},{1,9},{9,17},{17,25},{25,1},{2,10},{10... | collective-permute-start | bytes 4718600 | tf_op jit(solution)/shard_map/ppermute | solution.py:480
  135.4 186.7 %collective-permute-start.7 = (bf16[2,8,192,256]{3,2,1,0:T(8,128)(2,1)}, bf16[2,8,192,256]{3,2,1,0:T(8,128)(2,1)S(1)}, u32[]{:S(2)}, u32[]{:S(2)}) collective-permute-start(bf16[2,8,192,256]{3,2,1,0:T(8,128)(2,1)} %get-tuple-element.87), channel_id=1, source_target_pairs={{0,16},{8,24},{16,0},{24,8},{1,17},{9,25},{17,1},{25,9},{2,18},{10... | collective-permute-start | bytes 4718600 | tf_op jit(solution)/shard_map/ppermute | solution.py:480
  137.2 184.8 %collective-permute-start.8 = (bf16[2,8,192,256]{3,2,1,0:T(8,128)(2,1)}, bf16[2,8,192,256]{3,2,1,0:T(8,128)(2,1)S(1)}, u32[]{:S(2)}, u32[]{:S(2)}) collective-permute-start(bf16[2,8,192,256]{3,2,1,0:T(8,128)(2,1)} %get-tuple-element.88), channel_id=1, source_target_pairs={{0,24},{8,0},{16,8},{24,16},{1,25},{9,1},{17,9},{25,17},{2,26},{10... | collective-permute-start | bytes 4718600 | tf_op jit(solution)/shard_map/ppermute | solution.py:480
  215.7 241.0 %collective-permute-start.10 = (bf16[2,8,192,256]{3,2,1,0:T(8,128)(2,1)}, bf16[2,8,192,256]{3,2,1,0:T(8,128)(2,1)}, u32[]{:S(2)}, u32[]{:S(2)}) collective-permute-start(bf16[2,8,192,256]{3,2,1,0:T(8,128)(2,1)} %get-tuple-element.93), channel_id=1, source_target_pairs={{0,16},{8,24},{16,0},{24,8},{1,17},{9,25},{17,1},{25,9},{2,18},{10... | collective-permute-start | bytes 4718600 | tf_op jit(solution)/shard_map/ppermute | solution.py:480
  234.1 222.7 %collective-permute-start.11 = (bf16[2,8,192,256]{3,2,1,0:T(8,128)(2,1)}, bf16[2,8,192,256]{3,2,1,0:T(8,128)(2,1)S(1)}, u32[]{:S(2)}, u32[]{:S(2)}) collective-permute-start(bf16[2,8,192,256]{3,2,1,0:T(8,128)(2,1)} %get-tuple-element.94), channel_id=1, source_target_pairs={{0,24},{8,0},{16,8},{24,16},{1,25},{9,1},{17,9},{25,17},{2,26},{10... | collective-permute-start | bytes 4718600 | tf_op jit(solution)/shard_map/ppermute | solution.py:480
  237.5 84.5 %copy-start.53 = (bf16[2,8,192,256]{3,2,1,0:T(8,128)(2,1)}, bf16[2,8,192,256]{3,2,1,0:T(8,128)(2,1)S(1)}, u32[]{:S(2)}) copy-start(bf16[2,8,192,256]{3,2,1,0:T(8,128)(2,1)S(1)} %collective-permute-done.6.refs_8_.refs_3_) | copy-start | bytes 4718596
  237.5 219.3 %collective-permute-start.9 = (bf16[2,8,192,256]{3,2,1,0:T(8,128)(2,1)}, bf16[2,8,192,256]{3,2,1,0:T(8,128)(2,1)}, u32[]{:S(2)}, u32[]{:S(2)}) collective-permute-start(bf16[2,8,192,256]{3,2,1,0:T(8,128)(2,1)} %get-tuple-element.92), channel_id=1, source_target_pairs={{0,8},{8,16},{16,24},{24,0},{1,9},{9,17},{17,25},{25,1},{2,10},{10... | collective-permute-start | bytes 4718600 | tf_op jit(solution)/shard_map/ppermute | solution.py:480
  322.0 1.7 copy-start.6
  323.7 51.3 %copy-start.29 = (bf16[2,8,192,256]{3,2,1,0:T(8,128)(2,1)S(1)}, bf16[2,8,192,256]{3,2,1,0:T(8,128)(2,1)}, u32[]{:S(2)}) copy-start(bf16[2,8,192,256]{3,2,1,0:T(8,128)(2,1)} %copy-done.28) | copy-start | bytes 4718596
  338.1 189.4 %collective-permute-start.12 = (bf16[2,8,192,256]{3,2,1,0:T(8,128)(2,1)}, bf16[2,8,192,256]{3,2,1,0:T(8,128)(2,1)}, u32[]{:S(2)}, u32[]{:S(2)}) collective-permute-start(bf16[2,8,192,256]{3,2,1,0:T(8,128)(2,1)} %get-tuple-element.98), channel_id=1, source_target_pairs={{0,8},{8,16},{16,24},{24,0},{1,9},{9,17},{17,25},{25,1},{2,10},{10... | collective-permute-start | bytes 4718600 | tf_op jit(solution)/shard_map/ppermute | solution.py:480
  371.7 220.0 %collective-permute-start.13 = (bf16[2,8,192,256]{3,2,1,0:T(8,128)(2,1)}, bf16[2,8,192,256]{3,2,1,0:T(8,128)(2,1)}, u32[]{:S(2)}, u32[]{:S(2)}) collective-permute-start(bf16[2,8,192,256]{3,2,1,0:T(8,128)(2,1)} %get-tuple-element.99), channel_id=1, source_target_pairs={{0,16},{8,24},{16,0},{24,8},{1,17},{9,25},{17,1},{25,9},{2,18},{10... | collective-permute-start | bytes 4718600 | tf_op jit(solution)/shard_map/ppermute | solution.py:480
  375.0 1.4 copy-start.7
  395.7 243.5 %all-to-all-start = ((bf16[8,48,8,512]{3,2,1,0:T(8,128)(2,1)}), bf16[8,48,8,512]{3,2,1,0:T(8,128)(2,1)}, u32[]{:S(2)}, u32[]{:S(2)}) async-start(bf16[8,48,8,512]{3,2,1,0:T(8,128)(2,1)} %get-tuple-element.102), calls=%async_computation | async-start | bytes 6291456 | tf_op jit(solution)/shard_map/all_to_all | solution.py:581
  456.8 134.9 %collective-permute-start.14 = (bf16[2,8,192,256]{3,2,1,0:T(8,128)(2,1)}, bf16[2,8,192,256]{3,2,1,0:T(8,128)(2,1)S(1)}, u32[]{:S(2)}, u32[]{:S(2)}) collective-permute-start(bf16[2,8,192,256]{3,2,1,0:T(8,128)(2,1)} %get-tuple-element.100), channel_id=1, source_target_pairs={{0,24},{8,0},{16,8},{24,16},{1,25},{9,1},{17,9},{25,17},{2,26},{10... | collective-permute-start | bytes 4718600 | tf_op jit(solution)/shard_map/ppermute | solution.py:480
  458.0 48.6 %copy-start.23 = (bf16[768,768]{1,0:T(8,128)(2,1)S(1)}, bf16[768,768]{1,0:T(8,128)(2,1)}, u32[]{:S(2)}) copy-start(bf16[768,768]{1,0:T(8,128)(2,1)} %copy-done.22) | copy-start | bytes 3538948
  458.0 48.6 %copy-start.32 = (bf16[2,8,192,256]{3,2,1,0:T(8,128)(2,1)S(1)}, bf16[2,8,192,256]{3,2,1,0:T(8,128)(2,1)}, u32[]{:S(2)}) copy-start(bf16[2,8,192,256]{3,2,1,0:T(8,128)(2,1)} %copy-done.31) | copy-start | bytes 4718596
  472.5 193.5 %collective-permute-start.15 = (bf16[2,8,192,256]{3,2,1,0:T(8,128)(2,1)}, bf16[2,8,192,256]{3,2,1,0:T(8,128)(2,1)}, u32[]{:S(2)}, u32[]{:S(2)}) collective-permute-start(bf16[2,8,192,256]{3,2,1,0:T(8,128)(2,1)} %get-tuple-element.105), channel_id=1, source_target_pairs={{0,8},{8,16},{16,24},{24,0},{1,9},{9,17},{17,25},{25,1},{2,10},{10... | collective-permute-start | bytes 4718600 | tf_op jit(solution)/shard_map/ppermute | solution.py:480
  506.6 186.3 %collective-permute-start.16 = (bf16[2,8,192,256]{3,2,1,0:T(8,128)(2,1)}, bf16[2,8,192,256]{3,2,1,0:T(8,128)(2,1)}, u32[]{:S(2)}, u32[]{:S(2)}) collective-permute-start(bf16[2,8,192,256]{3,2,1,0:T(8,128)(2,1)} %get-tuple-element.106), channel_id=1, source_target_pairs={{0,16},{8,24},{16,0},{24,8},{1,17},{9,25},{17,1},{25,9},{2,18},{10... | collective-permute-start | bytes 4718600 | tf_op jit(solution)/shard_map/ppermute | solution.py:480
  506.6 1.4 copy-start.10
  508.0 84.8 %copy-start.34 = (bf16[2,8,192,256]{3,2,1,0:T(8,128)(2,1)S(1)}, bf16[2,8,192,256]{3,2,1,0:T(8,128)(2,1)}, u32[]{:S(2)}) copy-start(bf16[2,8,192,256]{3,2,1,0:T(8,128)(2,1)} %copy-done.33) | copy-start | bytes 4718596
  527.5 165.4 %collective-permute-start.17 = (bf16[2,8,192,256]{3,2,1,0:T(8,128)(2,1)}, bf16[2,8,192,256]{3,2,1,0:T(8,128)(2,1)}, u32[]{:S(2)}, u32[]{:S(2)}) collective-permute-start(bf16[2,8,192,256]{3,2,1,0:T(8,128)(2,1)} %get-tuple-element.107), channel_id=1, source_target_pairs={{0,24},{8,0},{16,8},{24,16},{1,25},{9,1},{17,9},{25,17},{2,26},{10... | collective-permute-start | bytes 4718600 | tf_op jit(solution)/shard_map/ppermute | solution.py:480
  602.8 183.1 %collective-permute-start.18 = (bf16[1,8,192,256]{3,2,1,0:T(8,128)(2,1)}, bf16[1,8,192,256]{3,2,1,0:T(8,128)(2,1)}, u32[]{:S(2)}, u32[]{:S(2)}) collective-permute-start(bf16[1,8,192,256]{3,2,1,0:T(8,128)(2,1)} %get-tuple-element.113), channel_id=1, source_target_pairs={{0,24},{8,0},{16,8},{24,16},{1,25},{9,1},{17,9},{25,17},{2,26},{10... | collective-permute-start | bytes 2359304 | tf_op jit(solution)/shard_map/ppermute | solution.py:480
  639.2 147.3 %collective-permute-start.19 = (bf16[1,8,192,256]{3,2,1,0:T(8,128)(2,1)}, bf16[1,8,192,256]{3,2,1,0:T(8,128)(2,1)}, u32[]{:S(2)}, u32[]{:S(2)}) collective-permute-start(bf16[1,8,192,256]{3,2,1,0:T(8,128)(2,1)} %get-tuple-element.114), channel_id=1, source_target_pairs={{0,16},{8,24},{16,0},{24,8},{1,17},{9,25},{17,1},{25,9},{2,18},{10... | collective-permute-start | bytes 2359304 | tf_op jit(solution)/shard_map/ppermute | solution.py:480
  639.2 4.6 copy-start.12
  639.2 99.8 %all-to-all-start.1 = ((bf16[8,48,8,512]{3,2,1,0:T(8,128)(2,1)}), bf16[8,48,8,512]{3,2,1,0:T(8,128)(2,1)}, u32[]{:S(2)}, u32[]{:S(2)}) async-start(bf16[8,48,8,512]{3,2,1,0:T(8,128)(2,1)} %get-tuple-element.109), calls=%async_computation.1 | async-start | bytes 6291456 | tf_op jit(solution)/shard_map/all_to_all | solution.py:581
  645.1 1.4 copy-start.35
  646.5 46.4 %copy-start.38 = (bf16[2,8,192,256]{3,2,1,0:T(8,128)(2,1)S(1)}, bf16[2,8,192,256]{3,2,1,0:T(8,128)(2,1)}, u32[]{:S(2)}) copy-start(bf16[2,8,192,256]{3,2,1,0:T(8,128)(2,1)} %copy-done.37) | copy-start | bytes 4718596
  665.9 120.5 %collective-permute-start.20 = (bf16[1,8,192,256]{3,2,1,0:T(8,128)(2,1)}, bf16[1,8,192,256]{3,2,1,0:T(8,128)(2,1)S(1)}, u32[]{:S(2)}, u32[]{:S(2)}) collective-permute-start(bf16[1,8,192,256]{3,2,1,0:T(8,128)(2,1)} %get-tuple-element.115), channel_id=1, source_target_pairs={{0,8},{8,16},{16,24},{24,0},{1,9},{9,17},{17,25},{25,1},{2,10},{10... | collective-permute-start | bytes 2359304 | tf_op jit(solution)/shard_map/ppermute | solution.py:480
  702.6 125.7 %collective-permute-start.21 = (bf16[1,8,192,256]{3,2,1,0:T(8,128)(2,1)}, bf16[1,8,192,256]{3,2,1,0:T(8,128)(2,1)S(1)}, u32[]{:S(2)}, u32[]{:S(2)}) collective-permute-start(bf16[1,8,192,256]{3,2,1,0:T(8,128)(2,1)} %get-tuple-element.119), channel_id=1, source_target_pairs={{0,24},{8,0},{16,8},{24,16},{1,25},{9,1},{17,9},{25,17},{2,26},{10... | collective-permute-start | bytes 2359304 | tf_op jit(solution)/shard_map/ppermute | solution.py:480
  739.0 89.3 %collective-permute-start.22 = (bf16[1,8,192,256]{3,2,1,0:T(8,128)(2,1)}, bf16[1,8,192,256]{3,2,1,0:T(8,128)(2,1)}, u32[]{:S(2)}, u32[]{:S(2)}) collective-permute-start(bf16[1,8,192,256]{3,2,1,0:T(8,128)(2,1)} %get-tuple-element.120), channel_id=1, source_target_pairs={{0,16},{8,24},{16,0},{24,8},{1,17},{9,25},{17,1},{25,9},{2,18},{10... | collective-permute-start | bytes 2359304 | tf_op jit(solution)/shard_map/ppermute | solution.py:480
  739.0 42.4 %all-to-all-start.2 = ((bf16[8,48,8,512]{3,2,1,0:T(8,128)(2,1)}), bf16[8,48,8,512]{3,2,1,0:T(8,128)(2,1)}, u32[]{:S(2)}, u32[]{:S(2)}) async-start(bf16[8,48,8,512]{3,2,1,0:T(8,128)(2,1)} %get-tuple-element.111), calls=%async_computation.2 | async-start | bytes 6291456 | tf_op jit(solution)/shard_map/all_to_all | solution.py:581
  744.8 1.4 copy-start.39
  781.4 42.4 %all-to-all-start.3 = ((bf16[8,48,8,512]{3,2,1,0:T(8,128)(2,1)}), bf16[8,48,8,512]{3,2,1,0:T(8,128)(2,1)}, u32[]{:S(2)}, u32[]{:S(2)}) async-start(bf16[8,48,8,512]{3,2,1,0:T(8,128)(2,1)} %get-tuple-element.117), calls=%async_computation.3 | async-start | bytes 6291456 | tf_op jit(solution)/shard_map/all_to_all | solution.py:581
  785.8 42.5 %collective-permute-start.23 = (bf16[1,8,192,256]{3,2,1,0:T(8,128)(2,1)S(1)}, bf16[1,8,192,256]{3,2,1,0:T(8,128)(2,1)}, u32[]{:S(2)}, u32[]{:S(2)}) collective-permute-start(bf16[1,8,192,256]{3,2,1,0:T(8,128)(2,1)S(1)} %get-tuple-element.121), channel_id=1, source_target_pairs={{0,8},{8,16},{16,24},{24,0},{1,9},{9,17},{17,25},{25,1},{2,10},{10... | collective-permute-start | bytes 2359304 | tf_op jit(solution)/shard_map/ppermute | solution.py:480
  786.5 22.0 %copy-start.14 = (bf16[1,8,192,256]{3,2,1,0:T(8,128)(2,1)}, bf16[1,8,192,256]{3,2,1,0:T(8,128)(2,1)S(1)}, u32[]{:S(2)}) copy-start(bf16[1,8,192,256]{3,2,1,0:T(8,128)(2,1)S(1)} %collective-permute-done.20.refs_3_) | copy-start | bytes 2359300
  786.5 1.6 copy-start.26
  823.7 4.7 copy-start.48
  823.7 42.5 %all-to-all-start.4 = ((bf16[8,48,8,512]{3,2,1,0:T(8,128)(2,1)}), bf16[8,48,8,512]{3,2,1,0:T(8,128)(2,1)}, u32[]{:S(2)}, u32[]{:S(2)}) async-start(bf16[8,48,8,512]{3,2,1,0:T(8,128)(2,1)} %get-tuple-element.123), calls=%async_computation.4 | async-start | bytes 6291456 | tf_op jit(solution)/shard_map/all_to_all | solution.py:581
  828.3 20.9 %copy-start.16 = (bf16[1,8,192,256]{3,2,1,0:T(8,128)(2,1)}, bf16[1,8,192,256]{3,2,1,0:T(8,128)(2,1)S(1)}, u32[]{:S(2)}) copy-start(bf16[1,8,192,256]{3,2,1,0:T(8,128)(2,1)S(1)} %collective-permute-done.21.refs_1_.refs_5_) | copy-start | bytes 2359300
  828.4 1.5 copy-start.27
  866.2 4.8 copy-start.52
  866.2 4.9 copy-start.51
  866.2 42.5 %all-to-all-start.5 = ((bf16[8,48,8,512]{3,2,1,0:T(8,128)(2,1)}), bf16[8,48,8,512]{3,2,1,0:T(8,128)(2,1)}, u32[]{:S(2)}, u32[]{:S(2)}) async-start(bf16[8,48,8,512]{3,2,1,0:T(8,128)(2,1)} %after.1), calls=%async_computation.5 | async-start | bytes 6291456 | tf_op jit(solution)/shard_map/all_to_all | solution.py:581
  939.6 76.4 %all-to-all-start.6 = ((bf16[8,48,16,512]{3,2,1,0:T(8,128)(2,1)}), bf16[8,48,16,512]{3,2,1,0:T(8,128)(2,1)}, u32[]{:S(2)}, u32[]{:S(2)}) async-start(bf16[8,48,16,512]{3,2,1,0:T(8,128)(2,1)} %get-tuple-element.126), calls=%async_computation.6 | async-start | bytes 12582912 | tf_op jit(solution)/shard_map/all_to_all | solution.py:592
  1016.0 5.3 copy-start.5
  1016.0 5.3 copy-start.8
  1016.0 76.9 %all-to-all-start.8 = ((bf16[8,48,16,512]{3,2,1,0:T(8,128)(2,1)}), bf16[8,48,16,512]{3,2,1,0:T(8,128)(2,1)}, u32[]{:S(2)}, u32[]{:S(2)}) async-start(bf16[8,48,16,512]{3,2,1,0:T(8,128)(2,1)} %get-tuple-element.131), calls=%async_computation.8 | async-start | bytes 12582912 | tf_op jit(solution)/shard_map/all_to_all | solution.py:596
  1092.9 4.9 copy-start.13
  1092.9 76.5 %all-to-all-start.7 = ((bf16[8,48,16,512]{3,2,1,0:T(8,128)(2,1)}), bf16[8,48,16,512]{3,2,1,0:T(8,128)(2,1)}, u32[]{:S(2)}, u32[]{:S(2)}) async-start(bf16[8,48,16,512]{3,2,1,0:T(8,128)(2,1)} %get-tuple-element.130), calls=%async_computation.7 | async-start | bytes 12582912 | tf_op jit(solution)/shard_map/all_to_all | solution.py:596
  1100.5 68.9 %copy-start.15 = (bf16[1,8,192,256]{3,2,1,0:T(8,128)(2,1)S(1)}, bf16[1,8,192,256]{3,2,1,0:T(8,128)(2,1)}, u32[]{:S(2)}) copy-start(bf16[1,8,192,256]{3,2,1,0:T(8,128)(2,1)} %copy-done.14) | copy-start | bytes 2359300
  1100.5 68.9 %copy-start.17 = (bf16[1,8,192,256]{3,2,1,0:T(8,128)(2,1)S(1)}, bf16[1,8,192,256]{3,2,1,0:T(8,128)(2,1)}, u32[]{:S(2)}) copy-start(bf16[1,8,192,256]{3,2,1,0:T(8,128)(2,1)} %copy-done.16) | copy-start | bytes 2359300
  (23 other events, 25.9 us)

commit v3 on v2

--- a/solution.py
+++ b/solution.py
@@ -242,19 +242,21 @@
 
 
 def backward_kernel(me_ref, saved_ref, up_ref, down_t_ref, up_t_ref, synth_ref, _, __, *refs):
-    members = len(refs) - 4
-    out_ref, token_ref, mixed_ref, waves_ref = refs[members:]
+    members = len(refs) - 5
+    out_ref, token_ref, cot_ref, mixed_ref, waves_ref = refs[members:]
     put_token(token_ref)
     lon, channels = mixed_ref.shape
     share = lon // members
     for piece in range(members):
-        place = share_of(me_ref, piece, members, share)
+        cot_ref[share_of(me_ref, piece, members, share), :] = refs[piece][0, 0]
+    for start in range(0, lon, lon // 2):
+        place = pl.ds(start, lon // 2)
         v = dot(saved_ref[0, place, :], up_ref[...])
         square = v * v
         half = 0.5 + 0.5 * jnp.tanh(v * (kappa_gelu + (kappa_gelu * cubic_gelu) * square))
         inner = v * (2.0 * kappa_gelu + (6.0 * kappa_gelu * cubic_gelu) * square)
         slopes = half * (1.0 + (1.0 - half) * inner)
-        act_grad = dot(refs[piece][0, 0], down_t_ref[...])
+        act_grad = dot(cot_ref[place, :], down_t_ref[...])
         pre_grad = (act_grad * slopes).astype(BF16)
         mixed_ref[place, :] = dot(pre_grad, up_t_ref[...]).astype(BF16)
     wave = dot(synth_ref[...], mixed_ref[...])
@@ -299,6 +301,7 @@
             out_specs=[pl.BlockSpec(out_shape, lambda i, q: (0, 0, 0, 0)), TOKEN_OUT],
             scratch_shapes=[
                 pltpu.VMEM((lon, channels), BF16),
+                pltpu.VMEM((lon, channels), BF16),
                 strips(modes * rows, 2 * channels),
             ],
         ),
@@ -322,19 +325,24 @@
     channels = mix_t_ref.shape[0]
     batch, columns = refs[0].shape[1], refs[0].shape[-1]
     first = quad_ref.shape[0]
+    degrees = table_ref.shape[1]
+    gained = []
     for m in range(batch):
         pieces = [refs[p][:, m].astype(F32).reshape(-1, columns) for p in range(parts)]
         wave = jnp.concatenate(pieces, axis=0).astype(BF16)
-        gained = (dot(table_ref[m], wave) * gain_ref[...]).astype(BF16)
-        coeff = jnp.concatenate(
-            [
-                dot(gained[:, :channels], mix_t_ref[...]).astype(BF16),
-                dot(gained[:, channels:], mix_t_ref[...]).astype(BF16),
-            ],
-            axis=1,
-        )
-        out_ref[m] = coeff
-        latitude(joined, table_ref[m, :, :first], quad_ref[...], coeff, lat_ref, m)
+        gained.append((dot(table_ref[m], wave) * gain_ref[...]).astype(BF16))
+    gained = jnp.concatenate(gained, axis=0)
+    coeff = jnp.concatenate(
+        [
+            dot(gained[:, :channels], mix_t_ref[...]).astype(BF16),
+            dot(gained[:, channels:], mix_t_ref[...]).astype(BF16),
+        ],
+        axis=1,
+    )
+    for m in range(batch):
+        own = coeff[m * degrees : (m + 1) * degrees]
+        out_ref[m] = own
+        latitude(joined, table_ref[m, :, :first], quad_ref[...], own, lat_ref, m)
 
 
 def spectral(token, joined, table, gain, mix_t, quad, waves):
@@ -402,7 +410,7 @@
 
 
 def output_kernel(joined, members, scale, me_ref, wave_ref, analysis_ref, _, *refs):
-    out_ref, token_ref, waves_ref = refs[-3:]
+    out_ref, token_ref, waves_ref, spatial_ref = refs[-4:]
     put_token(token_ref)
     every, share = wave_ref.shape[2], refs[0].shape[2]
     rows = every // joined
@@ -422,13 +430,13 @@
     wave = jnp.concatenate(
         [jnp.concatenate(strip[:half], axis=1), jnp.concatenate(strip[half:], axis=1)], axis=0
     )
+    spatial_ref[...] = dot(analysis_ref[...], wave)
     for piece in range(members):
         place = share_of(me_ref, piece, members, share)
-        spatial = dot(analysis_ref[place, :], wave)
         cot = refs[piece][0, 0]
         for part in range(1, joined):
             cot = jnp.where(row >= part * rows, refs[part * members + piece][0, 0], cot)
-        out_ref[0, 0, place, :] = (cot.astype(F32) + spatial * scale).astype(BF16)
+        out_ref[0, 0, place, :] = (cot.astype(F32) + spatial_ref[place, :] * scale).astype(BF16)
 
 
 def output_rows(token, index, shape, me, wave, cots, analysis, held):
@@ -462,7 +470,7 @@
                 pl.BlockSpec((1, 1, lon, channels), lambda i, q: (0, index * rows + i, 0, 0)),
                 TOKEN_OUT,
             ],
-            scratch_shapes=[strips(groups * modes * rows, columns)],
+            scratch_shapes=[strips(groups * modes * rows, columns), pltpu.VMEM((lon, channels), F32)],
         ),
         out_shape=[jax.ShapeDtypeStruct(shape, BF16), TOKEN],
         input_output_aliases=aliases,
@@ -485,15 +493,15 @@
     pass
 
 
-def after(value, other):
+def after(values, *others):
     return pl.pallas_call(
         after_kernel,
-        in_specs=[TOKEN_IN, TOKEN_IN],
-        out_specs=TOKEN_IN,
-        out_shape=jax.ShapeDtypeStruct(value.shape, value.dtype),
-        input_output_aliases={0: 0},
+        in_specs=[TOKEN_IN] * (len(values) + len(others)),
+        out_specs=[TOKEN_IN] * len(values),
+        out_shape=[jax.ShapeDtypeStruct(value.shape, value.dtype) for value in values],
+        input_output_aliases={index: index for index in range(len(values))},
         name="after",
-    )(value, other)
+    )(*values, *others)
 
 
 def kernel_order(parts, ahead):
@@ -501,6 +509,7 @@
     for step in range(2 - ahead, parts + 2):
         order.append(("exchange", step) if step < parts else None)
         order.append(("backward", step - 2) if step >= 2 else None)
+        order.append(("gate", 0) if step == parts - 1 else None)
     return [entry for entry in order if entry is not None]
 
 
@@ -558,11 +567,19 @@
                 weights,
                 values.get(cotangent),
             )
-            moved = shift(pieces)
+            held = pieces
+            if part == parts - 1:
+                continue
+        if kind == "gate":
+            earlier = [array for array, _ in cots[parts - 2][1:]]
+            *moved, token = after(held[1:] + [token], *earlier)
+            held = held[:1] + moved
+        if kind in ("exchange", "gate"):
+            moved = shift(held)
             values[forward] = [(array, 0) for array in moved]
             slot = 0 if forward is None else 1
             cots[cotangent] = [(moved[-piece % members], slot) for piece in range(members)]
-        else:
+        if kind == "backward":
             wave, token = backward_rows(
                 token,
                 waves.get(part - 2, token),
@@ -577,7 +594,7 @@
                 synth,
             )
             if part == parts - 1 and part > 0:
-                wave = after(wave, waves[part - 1])
+                [wave] = after([wave], waves[part - 1])
             waves[part] = lax.all_to_all(wave, "lat", 0, 0, tiled=True)
     waves = [waves[part] for part in range(parts)]
     steps = parts // joined

time: 1200 us -> 1200 us (level); the launches traced: 1190 us -> 1180 us
  starting transfers between devices: 363 us -> 332 us
  waiting for transfers between devices: 406 us -> 426 us
    ppermute x24, waiting for transfers between devices: 183 us -> 237 us  [shift(): moved.append(lax.ppermute(pieces[piece], 'member', pairs))]
    ppermute x24, starting transfers between devices: 321 us -> 289 us  [shift(): moved.append(lax.ppermute(pieces[piece], 'member', pairs))]
    all_to_all x6, waiting for transfers between devices: 85.5 us -> 55 us  [shards(): waves[part] = lax.all_to_all(wave, 'lat', 0, 0, tiled=True)]
    unnamed x112 -> x126, local copies, waits for them, and re-layouts: 35.7 us -> 42.4 us
where the time goes in v3:
time: 1200 us; the launch traced here: 1180 us
  waiting for transfers between devices  426 us (36%)
  Pallas kernels  354 us (30%)
  starting transfers between devices  332 us (28%)
  local copies, waits for them, and re-layouts  43 us (4%)
  other arithmetic  22.1 us (2%)
    ppermute x24, starting transfers between devices, shift(): moved.append(lax.ppermute(pieces[piece], 'member', pairs))  289 us
    ppermute x24, waiting for transfers between devices, shift(): moved.append(lax.ppermute(pieces[piece], 'member', pairs))  237 us
    pallas_call x6, Pallas kernels, backward_rows(): pl.pallas_call(backward_kernel, grid_spec=pltpu.PrefetchScalarGridSpec(nu...  108 us
    pallas_call x8, Pallas kernels, exchange_rows(): pl.pallas_call(functools.partial(exchange_kernel, members, forward, cotan...  88.3 us
    all_to_all x2, waiting for transfers between devices, shards(): lat_waves[step] = lax.all_to_all(wave, 'lat', 0, 0, tiled=True)  78 us
    pallas_call x3, Pallas kernels, output_rows(): pl.pallas_call(functools.partial(output_kernel, joined, members, 1.0 / lo...  64 us
    all_to_all x1, waiting for transfers between devices, shards(): lat_waves = {0: lax.all_to_all(wave, 'lat', 0, 0, tiled=True)}  55.8 us
    all_to_all x6, waiting for transfers between devices, shards(): waves[part] = lax.all_to_all(wave, 'lat', 0, 0, tiled=True)  55 us
  transfers between devices with their start and end apart: 33, of which 10 were waited for; matrix products, arithmetic and copies ran while one was open for 2% of the time, Pallas kernels for 25%

profile of v3, /device:TPU:0, one launch (start us, length us, event | category | flops | bytes accessed | tf_op | source)
XLA Modules:
  0.0 1177.5 jit_solution(18072965254770536554)
XLA Ops:
  1.9 9.6 exchange.8
  12.4 3.0 collective-permute-start
  15.4 2.6 collective-permute-start.1
  19.4 9.3 exchange.9
  32.3 36.6 %legendre.1 = (bf16[48,384,384]{2,1,0:T(8,128)(2,1)}, f32[8,128]{1,0:T(8,128)S(1)}) custom-call(f32[48,384]{1,0:T(8,128)S(1)} %multiply_add_fusion.start_ref, f32[1,384]{1,0:T(1,128)S(1)} %reshape.204.cosine_ref, f32[48,1]{1,0:T(8,128)S(1)} %add_convert_fusion.order_ref, f32[8,128]{1,0:T(8,128)S(1)} %get-tuple-element.76._), custom_call_target="tpu_custom_call" | custom-call | flops 49999998976 | bytes 1000 | tf_op jit(solution)/shard_map/legendre/pallas_call | solution.py:108
  69.5 21.4 %select_convert_fusion = (bf16[768,768]{1,0:T(8,128)(2,1)}, bf16[768,768]{1,0:T(8,128)(2,1)S(1)}) fusion(s32[768]{0:T(1024)S(1)} %fusion.14, pred[768]{0:T(1024)(128)(4,1)S(1)} %fusion.20, f32[768]{0:T(1024)S(1)} %compare_select_fusion), kind=kLoop, calls=%fused_computation.6 | loop fusion | flops 14745600 | bytes 2366208 | tf_op jit(solution)/shard_map/convert_element_type | solution.py:54
  90.8 2.9 collective-permute-start.5
  93.7 13.0 %exchange.10 = (bf16[2,8,192,256]{3,2,1,0:T(8,128)(2,1)S(1)}, bf16[2,8,192,256]{3,2,1,0:T(8,128)(2,1)}, bf16[2,8,192,256]{3,2,1,0:T(8,128)(2,1)}, bf16[2,8,192,256]{3,2,1,0:T(8,128)(2,1)}, f32[8,128]{1,0:T(8,128)S(1)}) custom-call(s32[1]{0:T(128)} %bitcast.me_ref, f32[8,128]{1,0:T(8,128)S(1)} %get-tuple-element.78.refs_0_, bf16[48,768,256]{2,1,0:T(8,128)(2,1)} %bitcast.29, ...), custom_call_target="tpu_custom_call" | custom-call | flops 49999998976 | bytes 1000 | tf_op jit(solution)/shard_map/exchange/pallas_call | solution.py:228
  107.9 27.4 %collective-permute-start.6 = (bf16[2,8,192,256]{3,2,1,0:T(8,128)(2,1)}, bf16[2,8,192,256]{3,2,1,0:T(8,128)(2,1)S(1)}, u32[]{:S(2)}, u32[]{:S(2)}) collective-permute-start(bf16[2,8,192,256]{3,2,1,0:T(8,128)(2,1)} %get-tuple-element.90), channel_id=1, source_target_pairs={{0,8},{8,16},{16,24},{24,0},{1,9},{9,17},{17,25},{25,1},{2,10},{10... | collective-permute-start | bytes 4718600 | tf_op jit(solution)/shard_map/ppermute | solution.py:488
  135.2 1.8 collective-permute-start.7
  137.6 64.4 %collective-permute-done.4.refs_9_ = bf16[1,8,192,256]{3,2,1,0:T(8,128)(2,1)S(1)} collective-permute-done((bf16[1,8,192,256]{3,2,1,0:T(8,128)(2,1)}, bf16[1,8,192,256]{3,2,1,0:T(8,128)(2,1)S(1)}, u32[]{:S(2)}, u32[]{:S(2)}) %collective-permute-start.4) | collective-permute-done | bytes 786464 | tf_op jit(solution)/shard_map/ppermute | solution.py:488
  203.1 12.7 %exchange.11 = (bf16[2,8,192,256]{3,2,1,0:T(8,128)(2,1)S(1)}, bf16[2,8,192,256]{3,2,1,0:T(8,128)(2,1)}, bf16[2,8,192,256]{3,2,1,0:T(8,128)(2,1)}, bf16[2,8,192,256]{3,2,1,0:T(8,128)(2,1)}, f32[8,128]{1,0:T(8,128)S(1)}) custom-call(s32[1]{0:T(128)} %bitcast.me_ref, f32[8,128]{1,0:T(8,128)S(1)} %get-tuple-element.83.refs_0_, bf16[48,768,256]{2,1,0:T(8,128)(2,1)} %bitcast.30, ...), custom_call_target="tpu_custom_call" | custom-call | flops 49999998976 | bytes 1000 | tf_op jit(solution)/shard_map/exchange/pallas_call | solution.py:228
  216.9 18.3 %collective-permute-start.10 = (bf16[2,8,192,256]{3,2,1,0:T(8,128)(2,1)}, bf16[2,8,192,256]{3,2,1,0:T(8,128)(2,1)}, u32[]{:S(2)}, u32[]{:S(2)}) collective-permute-start(bf16[2,8,192,256]{3,2,1,0:T(8,128)(2,1)} %get-tuple-element.97), channel_id=1, source_target_pairs={{0,16},{8,24},{16,0},{24,8},{1,17},{9,25},{17,1},{25,9},{2,18},{10... | collective-permute-start | bytes 4718600 | tf_op jit(solution)/shard_map/ppermute | solution.py:488
  235.2 3.4 collective-permute-start.11
  238.6 83.4 %collective-permute-start.9 = (bf16[2,8,192,256]{3,2,1,0:T(8,128)(2,1)}, bf16[2,8,192,256]{3,2,1,0:T(8,128)(2,1)}, u32[]{:S(2)}, u32[]{:S(2)}) collective-permute-start(bf16[2,8,192,256]{3,2,1,0:T(8,128)(2,1)} %get-tuple-element.96), channel_id=1, source_target_pairs={{0,8},{8,16},{16,24},{24,0},{1,9},{9,17},{17,25},{25,1},{2,10},{10... | collective-permute-start | bytes 4718600 | tf_op jit(solution)/shard_map/ppermute | solution.py:488
  323.7 13.3 %exchange.12 = (bf16[2,8,192,256]{3,2,1,0:T(8,128)(2,1)S(1)}, bf16[2,8,192,256]{3,2,1,0:T(8,128)(2,1)}, bf16[2,8,192,256]{3,2,1,0:T(8,128)(2,1)}, bf16[2,8,192,256]{3,2,1,0:T(8,128)(2,1)}, f32[8,128]{1,0:T(8,128)S(1)}) custom-call(s32[1]{0:T(128)} %bitcast.me_ref, f32[8,128]{1,0:T(8,128)S(1)} %get-tuple-element.88.refs_0_, bf16[48,768,256]{2,1,0:T(8,128)(2,1)} %bitcast.31, ...), custom_call_target="tpu_custom_call" | custom-call | flops 49999998976 | bytes 1000 | tf_op jit(solution)/shard_map/exchange/pallas_call | solution.py:228
  338.1 33.6 %collective-permute-start.12 = (bf16[2,8,192,256]{3,2,1,0:T(8,128)(2,1)}, bf16[2,8,192,256]{3,2,1,0:T(8,128)(2,1)}, u32[]{:S(2)}, u32[]{:S(2)}) collective-permute-start(bf16[2,8,192,256]{3,2,1,0:T(8,128)(2,1)} %get-tuple-element.102), channel_id=1, source_target_pairs={{0,8},{8,16},{16,24},{24,0},{1,9},{9,17},{17,25},{25,1},{2,10},{10... | collective-permute-start | bytes 4718600 | tf_op jit(solution)/shard_map/ppermute | solution.py:488
  371.7 3.3 collective-permute-start.13
  375.0 1.4 copy-done.14
  376.4 17.9 %backward.6 = (bf16[8,48,8,512]{3,2,1,0:T(8,128)(2,1)}, f32[8,128]{1,0:T(8,128)S(1)}) custom-call(s32[1]{0:T(128)} %bitcast.me_ref, bf16[48,768,256]{2,1,0:T(8,128)(2,1)} %bitcast.32, bf16[256,512]{1,0:T(8,128)(2,1)S(1)} %copy-done.8, bf16[256,512]{1,0:T(8,128)(2,1)S(1)} %bitcast.8, bf16[512,256]{1,0:T(8,128)(2,1)S(1)} %bitcast.14, ...), custom_call_target="tpu_custom_call" | custom-call | flops 49999998976 | bytes 1000 | tf_op jit(solution)/shard_map/backward/pallas_call | solution.py:286
  394.3 4.5 all-to-all-start
  398.8 58.0 %collective-permute-done.10.refs_9_.refs_2_.refs_6_ = bf16[2,8,192,256]{3,2,1,0:T(8,128)(2,1)} collective-permute-done((bf16[2,8,192,256]{3,2,1,0:T(8,128)(2,1)}, bf16[2,8,192,256]{3,2,1,0:T(8,128)(2,1)}, u32[]{:S(2)}, u32[]{:S(2)}) %collective-permute-start.10) | collective-permute-done | bytes 1572896 | tf_op jit(solution)/shard_map/ppermute | solution.py:488
  458.0 13.3 %exchange.13 = (bf16[2,8,192,256]{3,2,1,0:T(8,128)(2,1)S(1)}, bf16[2,8,192,256]{3,2,1,0:T(8,128)(2,1)}, bf16[2,8,192,256]{3,2,1,0:T(8,128)(2,1)}, bf16[2,8,192,256]{3,2,1,0:T(8,128)(2,1)}, f32[8,128]{1,0:T(8,128)S(1)}) custom-call(s32[1]{0:T(128)} %bitcast.me_ref, f32[8,128]{1,0:T(8,128)S(1)} %get-tuple-element.94.refs_0_, bf16[48,768,256]{2,1,0:T(8,128)(2,1)} %bitcast.33, ...), custom_call_target="tpu_custom_call" | custom-call | flops 49999998976 | bytes 1000 | tf_op jit(solution)/shard_map/exchange/pallas_call | solution.py:228
  472.4 34.2 %collective-permute-start.15 = (bf16[2,8,192,256]{3,2,1,0:T(8,128)(2,1)}, bf16[2,8,192,256]{3,2,1,0:T(8,128)(2,1)}, u32[]{:S(2)}, u32[]{:S(2)}) collective-permute-start(bf16[2,8,192,256]{3,2,1,0:T(8,128)(2,1)} %get-tuple-element.109), channel_id=1, source_target_pairs={{0,8},{8,16},{16,24},{24,0},{1,9},{9,17},{17,25},{25,1},{2,10},{10... | collective-permute-start | bytes 4718600 | tf_op jit(solution)/shard_map/ppermute | solution.py:488
  506.6 1.4 copy-done.17
  508.0 18.1 %backward.7 = (bf16[8,48,8,512]{3,2,1,0:T(8,128)(2,1)}, f32[8,128]{1,0:T(8,128)S(1)}) custom-call(s32[1]{0:T(128)} %bitcast.me_ref, bf16[48,768,256]{2,1,0:T(8,128)(2,1)} %bitcast.34, bf16[256,512]{1,0:T(8,128)(2,1)S(1)} %copy-done.8, bf16[256,512]{1,0:T(8,128)(2,1)S(1)} %bitcast.9, bf16[512,256]{1,0:T(8,128)(2,1)S(1)} %bitcast.15, ...), custom_call_target="tpu_custom_call" | custom-call | flops 49999998976 | bytes 1000 | tf_op jit(solution)/shard_map/backward/pallas_call | solution.py:286
  526.1 2.4 collective-permute-start.17
  528.5 63.2 %collective-permute-done.13.refs_5_.refs_2_ = bf16[2,8,192,256]{3,2,1,0:T(8,128)(2,1)} collective-permute-done((bf16[2,8,192,256]{3,2,1,0:T(8,128)(2,1)}, bf16[2,8,192,256]{3,2,1,0:T(8,128)(2,1)}, u32[]{:S(2)}, u32[]{:S(2)}) %collective-permute-start.13) | collective-permute-done | bytes 1572896 | tf_op jit(solution)/shard_map/ppermute | solution.py:488
  592.9 9.0 exchange.14
  602.7 36.4 %collective-permute-start.18 = (bf16[1,8,192,256]{3,2,1,0:T(8,128)(2,1)}, bf16[1,8,192,256]{3,2,1,0:T(8,128)(2,1)}, u32[]{:S(2)}, u32[]{:S(2)}) collective-permute-start(bf16[1,8,192,256]{3,2,1,0:T(8,128)(2,1)} %get-tuple-element.118), channel_id=1, source_target_pairs={{0,24},{8,0},{16,8},{24,16},{1,25},{9,1},{17,9},{25,17},{2,26},{10... | collective-permute-start | bytes 2359304 | tf_op jit(solution)/shard_map/ppermute | solution.py:488
  639.2 4.6 all-to-all-start.1
  645.0 1.4 copy-done.42
  646.5 18.1 %backward.8 = (bf16[8,48,8,512]{3,2,1,0:T(8,128)(2,1)}, f32[8,128]{1,0:T(8,128)S(1)}) custom-call(s32[1]{0:T(128)} %bitcast.me_ref, bf16[48,768,256]{2,1,0:T(8,128)(2,1)} %bitcast.35, bf16[256,512]{1,0:T(8,128)(2,1)S(1)} %copy-done.8, bf16[256,512]{1,0:T(8,128)(2,1)S(1)} %bitcast.10, bf16[512,256]{1,0:T(8,128)(2,1)S(1)} %bitcast.16, ...), custom_call_target="tpu_custom_call" | custom-call | flops 49999998976 | bytes 1000 | tf_op jit(solution)/shard_map/backward/pallas_call | solution.py:286
  664.5 28.4 %collective-permute-start.20 = (bf16[1,8,192,256]{3,2,1,0:T(8,128)(2,1)}, bf16[1,8,192,256]{3,2,1,0:T(8,128)(2,1)S(1)}, u32[]{:S(2)}, u32[]{:S(2)}) collective-permute-start(bf16[1,8,192,256]{3,2,1,0:T(8,128)(2,1)} %get-tuple-element.120), channel_id=1, source_target_pairs={{0,8},{8,16},{16,24},{24,0},{1,9},{9,17},{17,25},{25,1},{2,10},{10... | collective-permute-start | bytes 2359304 | tf_op jit(solution)/shard_map/ppermute | solution.py:488
  692.9 8.2 exchange.15
  704.7 4.6 all-to-all-start.2
  709.3 1.4 copy-done.46
  710.7 18.0 %backward.9 = (bf16[8,48,8,512]{3,2,1,0:T(8,128)(2,1)}, f32[8,128]{1,0:T(8,128)S(1)}) custom-call(s32[1]{0:T(128)} %bitcast.me_ref, bf16[48,768,256]{2,1,0:T(8,128)(2,1)} %bitcast.36, bf16[256,512]{1,0:T(8,128)(2,1)S(1)} %copy-done.8, bf16[256,512]{1,0:T(8,128)(2,1)S(1)} %bitcast.11, bf16[512,256]{1,0:T(8,128)(2,1)S(1)} %bitcast.17, ...), custom_call_target="tpu_custom_call" | custom-call | flops 49999998976 | bytes 1000 | tf_op jit(solution)/shard_map/backward/pallas_call | solution.py:286
  728.7 31.4 %collective-permute-done.19.__5_.refs_2_ = bf16[1,8,192,256]{3,2,1,0:T(8,128)(2,1)} collective-permute-done((bf16[1,8,192,256]{3,2,1,0:T(8,128)(2,1)}, bf16[1,8,192,256]{3,2,1,0:T(8,128)(2,1)}, u32[]{:S(2)}, u32[]{:S(2)}) %collective-permute-start.19) | collective-permute-done | bytes 786464 | tf_op jit(solution)/shard_map/ppermute | solution.py:488
  761.1 5.0 collective-permute-start.21
  766.7 4.6 all-to-all-start.3
  773.7 17.9 %backward.10 = (bf16[8,48,8,512]{3,2,1,0:T(8,128)(2,1)}, f32[8,128]{1,0:T(8,128)S(1)}) custom-call(s32[1]{0:T(128)} %bitcast.me_ref, bf16[48,768,256]{2,1,0:T(8,128)(2,1)} %bitcast.37, bf16[256,512]{1,0:T(8,128)(2,1)S(1)} %copy-done.8, bf16[256,512]{1,0:T(8,128)(2,1)S(1)} %bitcast.12, bf16[512,256]{1,0:T(8,128)(2,1)S(1)} %bitcast.18, ...), custom_call_target="tpu_custom_call" | custom-call | flops 49999998976 | bytes 1000 | tf_op jit(solution)/shard_map/backward/pallas_call | solution.py:286
  791.6 17.5 %all-to-all-done.3.__.refs_3_ = bf16[8,48,8,512]{3,2,1,0:T(8,128)(2,1)} async-done(((bf16[8,48,8,512]{3,2,1,0:T(8,128)(2,1)}), bf16[8,48,8,512]{3,2,1,0:T(8,128)(2,1)}, u32[]{:S(2)}, u32[]{:S(2)}) %all-to-all-start.3) | async-done | bytes 3145760 | tf_op jit(solution)/shard_map/all_to_all | solution.py:598
  809.2 4.5 all-to-all-start.4
  813.7 20.3 %collective-permute-done.22.refs_2_.refs_6_ = bf16[1,8,192,256]{3,2,1,0:T(8,128)(2,1)S(1)} collective-permute-done((bf16[1,8,192,256]{3,2,1,0:T(8,128)(2,1)}, bf16[1,8,192,256]{3,2,1,0:T(8,128)(2,1)S(1)}, u32[]{:S(2)}, u32[]{:S(2)}) %collective-permute-start.22) | collective-permute-done | bytes 786464 | tf_op jit(solution)/shard_map/ppermute | solution.py:488
  833.9 1.6 copy-done.34
  836.6 17.9 %backward.11 = (bf16[8,48,8,512]{3,2,1,0:T(8,128)(2,1)}, f32[8,128]{1,0:T(8,128)S(1)}) custom-call(s32[1]{0:T(128)} %bitcast.me_ref, bf16[48,768,256]{2,1,0:T(8,128)(2,1)} %bitcast.38, bf16[256,512]{1,0:T(8,128)(2,1)S(1)} %copy-done.8, bf16[256,512]{1,0:T(8,128)(2,1)S(1)} %bitcast.13, bf16[512,256]{1,0:T(8,128)(2,1)S(1)} %bitcast.19, ...), custom_call_target="tpu_custom_call" | custom-call | flops 49999998976 | bytes 1000 | tf_op jit(solution)/shard_map/backward/pallas_call | solution.py:286
  854.5 4.6 all-to-all-start.5
  859.5 37.4 %all-to-all-done.5.refs_5_ = bf16[8,48,8,512]{3,2,1,0:T(8,128)(2,1)} async-done(((bf16[8,48,8,512]{3,2,1,0:T(8,128)(2,1)}), bf16[8,48,8,512]{3,2,1,0:T(8,128)(2,1)}, u32[]{:S(2)}, u32[]{:S(2)}) %all-to-all-start.5) | async-done | bytes 3145760 | tf_op jit(solution)/shard_map/all_to_all | solution.py:598
  897.0 25.8 %spectral.1 = (bf16[48,384,512]{2,1,0:T(8,128)(2,1)}, bf16[8,48,16,512]{3,2,1,0:T(8,128)(2,1)}, f32[8,128]{1,0:T(8,128)S(1)}) custom-call(bf16[48,384,384]{2,1,0:T(8,128)(2,1)} %get-tuple-element.77.table_ref, f32[384,1]{1,0:T(8,128)S(1)} %broadcast_in_dim.70.gain_ref, bf16[256,256]{1,0:T(8,128)(2,1)S(1)} %bitcast.20, f32[128,1]{1,0:T(8,128)S(1)} %slice.28.quad_ref, ...), custom_call_target="tpu_custom_call" | custom-call | flops 49999998976 | bytes 1000 | tf_op jit(solution)/shard_map/spectral/pallas_call | solution.py:354
  922.8 4.8 all-to-all-start.6
  927.7 15.6 %latitude.2 = (bf16[8,48,16,512]{3,2,1,0:T(8,128)(2,1)}, f32[8,128]{1,0:T(8,128)S(1)}) custom-call(bf16[48,384,384]{2,1,0:T(8,128)(2,1)} %get-tuple-element.77.table_ref, f32[128,1]{1,0:T(8,128)S(1)} %slice.29.quad_ref, bf16[48,384,512]{2,1,0:T(8,128)(2,1)} %get-tuple-element.133.coeff_ref, f32[8,128]{1,0:T(8,128)S(1)} %get-tuple-element.135._), custom_call_target="tpu_custom_call" | custom-call | flops 49999998976 | bytes 1000 | tf_op jit(solution)/shard_map/latitude/pallas_call | solution.py:392
  943.3 55.8 %all-to-all-done.6.wave_ref = bf16[8,48,16,512]{3,2,1,0:T(8,128)(2,1)} async-done(((bf16[8,48,16,512]{3,2,1,0:T(8,128)(2,1)}), bf16[8,48,16,512]{3,2,1,0:T(8,128)(2,1)}, u32[]{:S(2)}, u32[]{:S(2)}) %all-to-all-start.6) | async-done | bytes 6291488 | tf_op jit(solution)/shard_map/all_to_all | solution.py:609
  999.2 5.2 all-to-all-start.8
  1004.4 1.4 copy-done.15
  1007.0 1.4 copy-done.37
  1008.4 21.3 %output.3 = (bf16[1,48,768,256]{3,2,1,0:T(8,128)(2,1)}, f32[8,128]{1,0:T(8,128)S(1)}) custom-call(s32[1]{0:T(128)} %bitcast.me_ref, bf16[8,48,16,512]{3,2,1,0:T(8,128)(2,1)} %all-to-all-done.6.wave_ref, bf16[768,768]{1,0:T(8,128)(2,1)S(1)} %copy-done.27, f32[8,128]{1,0:T(8,128)S(1)} %get-tuple-element.136._, bf16[2,8,192,256]{3,2,1,0:T(8,128)(2,1)S(1)} %copy-done.37, ...), custom_call_target="tpu_custom_call" | custom-call | flops 49999998976 | bytes 1000 | tf_op jit(solution)/shard_map/output/pallas_call | solution.py:463
  1029.7 15.6 %latitude.3 = (bf16[8,48,16,512]{3,2,1,0:T(8,128)(2,1)}, f32[8,128]{1,0:T(8,128)S(1)}) custom-call(bf16[48,384,384]{2,1,0:T(8,128)(2,1)} %get-tuple-element.77.table_ref, f32[128,1]{1,0:T(8,128)S(1)} %slice.27.quad_ref, bf16[48,384,512]{2,1,0:T(8,128)(2,1)} %get-tuple-element.133.coeff_ref, f32[8,128]{1,0:T(8,128)S(1)} %get-tuple-element.137._), custom_call_target="tpu_custom_call" | custom-call | flops 49999998976 | bytes 1000 | tf_op jit(solution)/shard_map/latitude/pallas_call | solution.py:392
  1045.3 30.7 %all-to-all-done.8.wave_ref = bf16[8,48,16,512]{3,2,1,0:T(8,128)(2,1)} async-done(((bf16[8,48,16,512]{3,2,1,0:T(8,128)(2,1)}), bf16[8,48,16,512]{3,2,1,0:T(8,128)(2,1)}, u32[]{:S(2)}, u32[]{:S(2)}) %all-to-all-start.8) | async-done | bytes 6291488 | tf_op jit(solution)/shard_map/all_to_all | solution.py:613
  1076.0 4.9 all-to-all-start.7
  1082.1 1.4 copy-done.43
  1083.6 21.6 %output.4 = (bf16[1,48,768,256]{3,2,1,0:T(8,128)(2,1)}, f32[8,128]{1,0:T(8,128)S(1)}) custom-call(s32[1]{0:T(128)} %bitcast.me_ref, bf16[8,48,16,512]{3,2,1,0:T(8,128)(2,1)} %all-to-all-done.8.wave_ref, bf16[768,768]{1,0:T(8,128)(2,1)S(1)} %copy-done.28, f32[8,128]{1,0:T(8,128)S(1)} %get-tuple-element.140._, ...), custom_call_target="tpu_custom_call", output_to_operand_aliasing={{0}: (12, {})} | custom-call | flops 49999998976 | bytes 1000 | tf_op jit(solution)/shard_map/output/pallas_call | solution.py:463
  1105.1 47.3 %all-to-all-done.7.wave_ref = bf16[8,48,16,512]{3,2,1,0:T(8,128)(2,1)} async-done(((bf16[8,48,16,512]{3,2,1,0:T(8,128)(2,1)}), bf16[8,48,16,512]{3,2,1,0:T(8,128)(2,1)}, u32[]{:S(2)}, u32[]{:S(2)}) %all-to-all-start.7) | async-done | bytes 6291488 | tf_op jit(solution)/shard_map/all_to_all | solution.py:613
  1155.9 21.1 %output.5 = (bf16[1,48,768,256]{3,2,1,0:T(8,128)(2,1)}, f32[8,128]{1,0:T(8,128)}) custom-call(s32[1]{0:T(128)} %bitcast.me_ref, bf16[8,48,16,512]{3,2,1,0:T(8,128)(2,1)} %all-to-all-done.7.wave_ref, bf16[768,768]{1,0:T(8,128)(2,1)} %get-tuple-element.148.analysis_ref, f32[8,128]{1,0:T(8,128)S(1)} %get-tuple-element.142._, ...), custom_call_target="tpu_custom_call", output_to_operand_aliasing={{0}: (12, {})} | custom-call | flops 49999998976 | bytes 1000 | tf_op jit(solution)/shard_map/output/pallas_call | solution.py:463
  (175 shorter events, 35.8 us)
Async XLA Ops:
  1.9 17.5 %copy-start.6 = (bf16[512,256]{1,0:T(8,128)(2,1)S(1)}, bf16[512,256]{1,0:T(8,128)(2,1)}, u32[]{:S(2)}) copy-start(bf16[512,256]{1,0:T(8,128)(2,1)} %refs_4_.11) | copy-start | bytes 786436
  12.4 78.4 %collective-permute-start = (bf16[1,8,192,256]{3,2,1,0:T(8,128)(2,1)}, bf16[1,8,192,256]{3,2,1,0:T(8,128)(2,1)}, u32[]{:S(2)}, u32[]{:S(2)}) collective-permute-start(bf16[1,8,192,256]{3,2,1,0:T(8,128)(2,1)} %get-tuple-element.80), channel_id=1, source_target_pairs={{0,8},{8,16},{16,24},{24,0},{1,9},{9,17},{17,25},{25,1},{2,10},{10... | collective-permute-start | bytes 2359304 | tf_op jit(solution)/shard_map/ppermute | solution.py:488
  15.4 78.3 %collective-permute-start.1 = (bf16[1,8,192,256]{3,2,1,0:T(8,128)(2,1)}, bf16[1,8,192,256]{3,2,1,0:T(8,128)(2,1)}, u32[]{:S(2)}, u32[]{:S(2)}) collective-permute-start(bf16[1,8,192,256]{3,2,1,0:T(8,128)(2,1)} %get-tuple-element.81), channel_id=1, source_target_pairs={{0,16},{8,24},{16,0},{24,8},{1,17},{9,25},{17,1},{25,9},{2,18},{10... | collective-permute-start | bytes 2359304 | tf_op jit(solution)/shard_map/ppermute | solution.py:488
  18.0 75.7 %collective-permute-start.2 = (bf16[1,8,192,256]{3,2,1,0:T(8,128)(2,1)}, bf16[1,8,192,256]{3,2,1,0:T(8,128)(2,1)}, u32[]{:S(2)}, u32[]{:S(2)}) collective-permute-start(bf16[1,8,192,256]{3,2,1,0:T(8,128)(2,1)} %get-tuple-element.82), channel_id=1, source_target_pairs={{0,24},{8,0},{16,8},{24,16},{1,25},{9,1},{17,9},{25,17},{2,26},{10... | collective-permute-start | bytes 2359304 | tf_op jit(solution)/shard_map/ppermute | solution.py:488
  30.5 106.6 %collective-permute-start.3 = (bf16[1,8,192,256]{3,2,1,0:T(8,128)(2,1)}, bf16[1,8,192,256]{3,2,1,0:T(8,128)(2,1)S(1)}, u32[]{:S(2)}, u32[]{:S(2)}) collective-permute-start(bf16[1,8,192,256]{3,2,1,0:T(8,128)(2,1)} %get-tuple-element.85), channel_id=1, source_target_pairs={{0,8},{8,16},{16,24},{24,0},{1,9},{9,17},{17,25},{25,1},{2,10},{10... | collective-permute-start | bytes 2359304 | tf_op jit(solution)/shard_map/ppermute | solution.py:488
  31.2 170.8 %collective-permute-start.4 = (bf16[1,8,192,256]{3,2,1,0:T(8,128)(2,1)}, bf16[1,8,192,256]{3,2,1,0:T(8,128)(2,1)S(1)}, u32[]{:S(2)}, u32[]{:S(2)}) collective-permute-start(bf16[1,8,192,256]{3,2,1,0:T(8,128)(2,1)} %get-tuple-element.86), channel_id=1, source_target_pairs={{0,16},{8,24},{16,0},{24,8},{1,17},{9,25},{17,1},{25,9},{2,18},{10... | collective-permute-start | bytes 2359304 | tf_op jit(solution)/shard_map/ppermute | solution.py:488
  32.3 36.8 %copy-start.8 = (bf16[256,512]{1,0:T(8,128)(2,1)S(1)}, bf16[256,512]{1,0:T(8,128)(2,1)}, u32[]{:S(2)}) copy-start(bf16[256,512]{1,0:T(8,128)(2,1)} %up_ref.11) | copy-start | bytes 786436
  32.3 36.9 %copy-start.57 = (s32[48,768]{1,0:T(8,128)S(1)}, s32[48,768]{1,0:T(8,128)}, u32[]{:S(2)}) copy-start(s32[48,768]{1,0:T(8,128)} %param.11) | copy-start | bytes 442372
  69.4 21.4 %copy-start.26 = (bf16[1,8,192,256]{3,2,1,0:T(8,128)(2,1)S(1)}, bf16[1,8,192,256]{3,2,1,0:T(8,128)(2,1)}, u32[]{:S(2)}) copy-start(bf16[1,8,192,256]{3,2,1,0:T(8,128)(2,1)} %copy-done.25) | copy-start | bytes 2359300
  69.4 24.3 %copy-start.50 = (bf16[1,8,192,256]{3,2,1,0:T(8,128)(2,1)S(1)}, bf16[1,8,192,256]{3,2,1,0:T(8,128)(2,1)}, u32[]{:S(2)}) copy-start(bf16[1,8,192,256]{3,2,1,0:T(8,128)(2,1)} %copy-done.49) | copy-start | bytes 2359300
  90.8 284.2 %copy-start.29 = (bf16[768,768]{1,0:T(8,128)(2,1)}, bf16[768,768]{1,0:T(8,128)(2,1)S(1)}, u32[]{:S(2)}) copy-start(bf16[768,768]{1,0:T(8,128)(2,1)S(1)} %get-tuple-element.149.synth_ref) | copy-start | bytes 3538948
  90.8 111.1 %collective-permute-start.5 = (bf16[1,8,192,256]{3,2,1,0:T(8,128)(2,1)S(1)}, bf16[1,8,192,256]{3,2,1,0:T(8,128)(2,1)S(1)}, u32[]{:S(2)}, u32[]{:S(2)}) collective-permute-start(bf16[1,8,192,256]{3,2,1,0:T(8,128)(2,1)S(1)} %copy-done.26), channel_id=1, source_target_pairs={{0,24},{8,0},{16,8},{24,16},{1,25},{9,1},{17,9},{25,17},{2,26},{10... | collective-permute-start | bytes 2359304 | tf_op jit(solution)/shard_map/ppermute | solution.py:488
  107.9 130.7 %collective-permute-start.6 = (bf16[2,8,192,256]{3,2,1,0:T(8,128)(2,1)}, bf16[2,8,192,256]{3,2,1,0:T(8,128)(2,1)S(1)}, u32[]{:S(2)}, u32[]{:S(2)}) collective-permute-start(bf16[2,8,192,256]{3,2,1,0:T(8,128)(2,1)} %get-tuple-element.90), channel_id=1, source_target_pairs={{0,8},{8,16},{16,24},{24,0},{1,9},{9,17},{17,25},{25,1},{2,10},{10... | collective-permute-start | bytes 4718600 | tf_op jit(solution)/shard_map/ppermute | solution.py:488
  135.2 186.8 %collective-permute-start.7 = (bf16[2,8,192,256]{3,2,1,0:T(8,128)(2,1)}, bf16[2,8,192,256]{3,2,1,0:T(8,128)(2,1)S(1)}, u32[]{:S(2)}, u32[]{:S(2)}) collective-permute-start(bf16[2,8,192,256]{3,2,1,0:T(8,128)(2,1)} %get-tuple-element.91), channel_id=1, source_target_pairs={{0,16},{8,24},{16,0},{24,8},{1,17},{9,25},{17,1},{25,9},{2,18},{10... | collective-permute-start | bytes 4718600 | tf_op jit(solution)/shard_map/ppermute | solution.py:488
  137.1 184.9 %collective-permute-start.8 = (bf16[2,8,192,256]{3,2,1,0:T(8,128)(2,1)}, bf16[2,8,192,256]{3,2,1,0:T(8,128)(2,1)S(1)}, u32[]{:S(2)}, u32[]{:S(2)}) collective-permute-start(bf16[2,8,192,256]{3,2,1,0:T(8,128)(2,1)} %get-tuple-element.92), channel_id=1, source_target_pairs={{0,24},{8,0},{16,8},{24,16},{1,25},{9,1},{17,9},{25,17},{2,26},{10... | collective-permute-start | bytes 4718600 | tf_op jit(solution)/shard_map/ppermute | solution.py:488
  216.9 239.9 %collective-permute-start.10 = (bf16[2,8,192,256]{3,2,1,0:T(8,128)(2,1)}, bf16[2,8,192,256]{3,2,1,0:T(8,128)(2,1)}, u32[]{:S(2)}, u32[]{:S(2)}) collective-permute-start(bf16[2,8,192,256]{3,2,1,0:T(8,128)(2,1)} %get-tuple-element.97), channel_id=1, source_target_pairs={{0,16},{8,24},{16,0},{24,8},{1,17},{9,25},{17,1},{25,9},{2,18},{10... | collective-permute-start | bytes 4718600 | tf_op jit(solution)/shard_map/ppermute | solution.py:488
  235.2 221.6 %collective-permute-start.11 = (bf16[2,8,192,256]{3,2,1,0:T(8,128)(2,1)}, bf16[2,8,192,256]{3,2,1,0:T(8,128)(2,1)S(1)}, u32[]{:S(2)}, u32[]{:S(2)}) collective-permute-start(bf16[2,8,192,256]{3,2,1,0:T(8,128)(2,1)} %get-tuple-element.98), channel_id=1, source_target_pairs={{0,24},{8,0},{16,8},{24,16},{1,25},{9,1},{17,9},{25,17},{2,26},{10... | collective-permute-start | bytes 4718600 | tf_op jit(solution)/shard_map/ppermute | solution.py:488
  238.6 83.4 %copy-start.60 = (bf16[2,8,192,256]{3,2,1,0:T(8,128)(2,1)}, bf16[2,8,192,256]{3,2,1,0:T(8,128)(2,1)S(1)}, u32[]{:S(2)}) copy-start(bf16[2,8,192,256]{3,2,1,0:T(8,128)(2,1)S(1)} %collective-permute-done.6.refs_8_.refs_3_) | copy-start | bytes 4718596
  238.6 218.2 %collective-permute-start.9 = (bf16[2,8,192,256]{3,2,1,0:T(8,128)(2,1)}, bf16[2,8,192,256]{3,2,1,0:T(8,128)(2,1)}, u32[]{:S(2)}, u32[]{:S(2)}) collective-permute-start(bf16[2,8,192,256]{3,2,1,0:T(8,128)(2,1)} %get-tuple-element.96), channel_id=1, source_target_pairs={{0,8},{8,16},{16,24},{24,0},{1,9},{9,17},{17,25},{25,1},{2,10},{10... | collective-permute-start | bytes 4718600 | tf_op jit(solution)/shard_map/ppermute | solution.py:488
  322.0 1.7 copy-start.13
  323.7 51.3 %copy-start.36 = (bf16[2,8,192,256]{3,2,1,0:T(8,128)(2,1)S(1)}, bf16[2,8,192,256]{3,2,1,0:T(8,128)(2,1)}, u32[]{:S(2)}) copy-start(bf16[2,8,192,256]{3,2,1,0:T(8,128)(2,1)} %copy-done.35) | copy-start | bytes 4718596
  338.1 188.1 %collective-permute-start.12 = (bf16[2,8,192,256]{3,2,1,0:T(8,128)(2,1)}, bf16[2,8,192,256]{3,2,1,0:T(8,128)(2,1)}, u32[]{:S(2)}, u32[]{:S(2)}) collective-permute-start(bf16[2,8,192,256]{3,2,1,0:T(8,128)(2,1)} %get-tuple-element.102), channel_id=1, source_target_pairs={{0,8},{8,16},{16,24},{24,0},{1,9},{9,17},{17,25},{25,1},{2,10},{10... | collective-permute-start | bytes 4718600 | tf_op jit(solution)/shard_map/ppermute | solution.py:488
  371.7 220.0 %collective-permute-start.13 = (bf16[2,8,192,256]{3,2,1,0:T(8,128)(2,1)}, bf16[2,8,192,256]{3,2,1,0:T(8,128)(2,1)}, u32[]{:S(2)}, u32[]{:S(2)}) collective-permute-start(bf16[2,8,192,256]{3,2,1,0:T(8,128)(2,1)} %get-tuple-element.103), channel_id=1, source_target_pairs={{0,16},{8,24},{16,0},{24,8},{1,17},{9,25},{17,1},{25,9},{2,18},{10... | collective-permute-start | bytes 4718600 | tf_op jit(solution)/shard_map/ppermute | solution.py:488
  375.0 1.4 copy-start.14
  394.3 244.8 %all-to-all-start = ((bf16[8,48,8,512]{3,2,1,0:T(8,128)(2,1)}), bf16[8,48,8,512]{3,2,1,0:T(8,128)(2,1)}, u32[]{:S(2)}, u32[]{:S(2)}) async-start(bf16[8,48,8,512]{3,2,1,0:T(8,128)(2,1)} %get-tuple-element.106), calls=%async_computation | async-start | bytes 6291456 | tf_op jit(solution)/shard_map/all_to_all | solution.py:598
  456.8 134.9 %collective-permute-start.14 = (bf16[2,8,192,256]{3,2,1,0:T(8,128)(2,1)}, bf16[2,8,192,256]{3,2,1,0:T(8,128)(2,1)S(1)}, u32[]{:S(2)}, u32[]{:S(2)}) collective-permute-start(bf16[2,8,192,256]{3,2,1,0:T(8,128)(2,1)} %get-tuple-element.104), channel_id=1, source_target_pairs={{0,24},{8,0},{16,8},{24,16},{1,25},{9,1},{17,9},{25,17},{2,26},{10... | collective-permute-start | bytes 4718600 | tf_op jit(solution)/shard_map/ppermute | solution.py:488
  458.0 48.6 %copy-start.30 = (bf16[768,768]{1,0:T(8,128)(2,1)S(1)}, bf16[768,768]{1,0:T(8,128)(2,1)}, u32[]{:S(2)}) copy-start(bf16[768,768]{1,0:T(8,128)(2,1)} %copy-done.29) | copy-start | bytes 3538948
  458.0 48.6 %copy-start.39 = (bf16[2,8,192,256]{3,2,1,0:T(8,128)(2,1)S(1)}, bf16[2,8,192,256]{3,2,1,0:T(8,128)(2,1)}, u32[]{:S(2)}) copy-start(bf16[2,8,192,256]{3,2,1,0:T(8,128)(2,1)} %copy-done.38) | copy-start | bytes 4718596
  472.4 192.1 %collective-permute-start.15 = (bf16[2,8,192,256]{3,2,1,0:T(8,128)(2,1)}, bf16[2,8,192,256]{3,2,1,0:T(8,128)(2,1)}, u32[]{:S(2)}, u32[]{:S(2)}) collective-permute-start(bf16[2,8,192,256]{3,2,1,0:T(8,128)(2,1)} %get-tuple-element.109), channel_id=1, source_target_pairs={{0,8},{8,16},{16,24},{24,0},{1,9},{9,17},{17,25},{25,1},{2,10},{10... | collective-permute-start | bytes 4718600 | tf_op jit(solution)/shard_map/ppermute | solution.py:488
  506.6 186.3 %collective-permute-start.16 = (bf16[2,8,192,256]{3,2,1,0:T(8,128)(2,1)}, bf16[2,8,192,256]{3,2,1,0:T(8,128)(2,1)}, u32[]{:S(2)}, u32[]{:S(2)}) collective-permute-start(bf16[2,8,192,256]{3,2,1,0:T(8,128)(2,1)} %get-tuple-element.110), channel_id=1, source_target_pairs={{0,16},{8,24},{16,0},{24,8},{1,17},{9,25},{17,1},{25,9},{2,18},{10... | collective-permute-start | bytes 4718600 | tf_op jit(solution)/shard_map/ppermute | solution.py:488
  506.6 1.4 copy-start.17
  508.0 84.9 %copy-start.41 = (bf16[2,8,192,256]{3,2,1,0:T(8,128)(2,1)S(1)}, bf16[2,8,192,256]{3,2,1,0:T(8,128)(2,1)}, u32[]{:S(2)}) copy-start(bf16[2,8,192,256]{3,2,1,0:T(8,128)(2,1)} %copy-done.40) | copy-start | bytes 4718596
  526.1 166.8 %collective-permute-start.17 = (bf16[2,8,192,256]{3,2,1,0:T(8,128)(2,1)}, bf16[2,8,192,256]{3,2,1,0:T(8,128)(2,1)}, u32[]{:S(2)}, u32[]{:S(2)}) collective-permute-start(bf16[2,8,192,256]{3,2,1,0:T(8,128)(2,1)} %get-tuple-element.111), channel_id=1, source_target_pairs={{0,24},{8,0},{16,8},{24,16},{1,25},{9,1},{17,9},{25,17},{2,26},{10... | collective-permute-start | bytes 4718600 | tf_op jit(solution)/shard_map/ppermute | solution.py:488
  602.7 126.0 %collective-permute-start.18 = (bf16[1,8,192,256]{3,2,1,0:T(8,128)(2,1)}, bf16[1,8,192,256]{3,2,1,0:T(8,128)(2,1)}, u32[]{:S(2)}, u32[]{:S(2)}) collective-permute-start(bf16[1,8,192,256]{3,2,1,0:T(8,128)(2,1)} %get-tuple-element.118), channel_id=1, source_target_pairs={{0,24},{8,0},{16,8},{24,16},{1,25},{9,1},{17,9},{25,17},{2,26},{10... | collective-permute-start | bytes 2359304 | tf_op jit(solution)/shard_map/ppermute | solution.py:488
  639.2 121.0 %collective-permute-start.19 = (bf16[1,8,192,256]{3,2,1,0:T(8,128)(2,1)}, bf16[1,8,192,256]{3,2,1,0:T(8,128)(2,1)}, u32[]{:S(2)}, u32[]{:S(2)}) collective-permute-start(bf16[1,8,192,256]{3,2,1,0:T(8,128)(2,1)} %get-tuple-element.119), channel_id=1, source_target_pairs={{0,16},{8,24},{16,0},{24,8},{1,17},{9,25},{17,1},{25,9},{2,18},{10... | collective-permute-start | bytes 2359304 | tf_op jit(solution)/shard_map/ppermute | solution.py:488
  639.2 4.6 copy-start.19
  639.2 65.5 %all-to-all-start.1 = ((bf16[8,48,8,512]{3,2,1,0:T(8,128)(2,1)}), bf16[8,48,8,512]{3,2,1,0:T(8,128)(2,1)}, u32[]{:S(2)}, u32[]{:S(2)}) async-start(bf16[8,48,8,512]{3,2,1,0:T(8,128)(2,1)} %get-tuple-element.116), calls=%async_computation.1 | async-start | bytes 6291456 | tf_op jit(solution)/shard_map/all_to_all | solution.py:598
  645.0 1.4 copy-start.42
  646.5 46.4 %copy-start.45 = (bf16[2,8,192,256]{3,2,1,0:T(8,128)(2,1)S(1)}, bf16[2,8,192,256]{3,2,1,0:T(8,128)(2,1)}, u32[]{:S(2)}) copy-start(bf16[2,8,192,256]{3,2,1,0:T(8,128)(2,1)} %copy-done.44) | copy-start | bytes 4718596
  664.5 95.7 %collective-permute-start.20 = (bf16[1,8,192,256]{3,2,1,0:T(8,128)(2,1)}, bf16[1,8,192,256]{3,2,1,0:T(8,128)(2,1)S(1)}, u32[]{:S(2)}, u32[]{:S(2)}) collective-permute-start(bf16[1,8,192,256]{3,2,1,0:T(8,128)(2,1)} %get-tuple-element.120), channel_id=1, source_target_pairs={{0,8},{8,16},{16,24},{24,0},{1,9},{9,17},{17,25},{25,1},{2,10},{10... | collective-permute-start | bytes 2359304 | tf_op jit(solution)/shard_map/ppermute | solution.py:488
  704.7 4.6 copy-start.32
  704.7 62.0 %all-to-all-start.2 = ((bf16[8,48,8,512]{3,2,1,0:T(8,128)(2,1)}), bf16[8,48,8,512]{3,2,1,0:T(8,128)(2,1)}, u32[]{:S(2)}, u32[]{:S(2)}) async-start(bf16[8,48,8,512]{3,2,1,0:T(8,128)(2,1)} %get-tuple-element.122), calls=%async_computation.2 | async-start | bytes 6291456 | tf_op jit(solution)/shard_map/all_to_all | solution.py:598
  709.3 1.4 copy-start.46
  728.7 31.4 %copy-start.9 = (f32[8,128]{1,0:T(8,128)}, f32[8,128]{1,0:T(8,128)S(1)}, u32[]{:S(2)}) copy-start(f32[8,128]{1,0:T(8,128)S(1)} %get-tuple-element.117.__3_) | copy-start | bytes 12292
  761.1 52.5 %collective-permute-start.21 = (bf16[1,8,192,256]{3,2,1,0:T(8,128)(2,1)}, bf16[1,8,192,256]{3,2,1,0:T(8,128)(2,1)S(1)}, u32[]{:S(2)}, u32[]{:S(2)}) collective-permute-start(bf16[1,8,192,256]{3,2,1,0:T(8,128)(2,1)} %get-tuple-element.127), channel_id=1, source_target_pairs={{0,24},{8,0},{16,8},{24,16},{1,25},{9,1},{17,9},{25,17},{2,26},{10... | collective-permute-start | bytes 2359304 | tf_op jit(solution)/shard_map/ppermute | solution.py:488
  766.1 67.8 %collective-permute-start.22 = (bf16[1,8,192,256]{3,2,1,0:T(8,128)(2,1)}, bf16[1,8,192,256]{3,2,1,0:T(8,128)(2,1)S(1)}, u32[]{:S(2)}, u32[]{:S(2)}) collective-permute-start(bf16[1,8,192,256]{3,2,1,0:T(8,128)(2,1)} %get-tuple-element.128), channel_id=1, source_target_pairs={{0,16},{8,24},{16,0},{24,8},{1,17},{9,25},{17,1},{25,9},{2,18},{10... | collective-permute-start | bytes 2359304 | tf_op jit(solution)/shard_map/ppermute | solution.py:488
  766.1 67.8 %collective-permute-start.23 = (bf16[1,8,192,256]{3,2,1,0:T(8,128)(2,1)}, bf16[1,8,192,256]{3,2,1,0:T(8,128)(2,1)}, u32[]{:S(2)}, u32[]{:S(2)}) collective-permute-start(bf16[1,8,192,256]{3,2,1,0:T(8,128)(2,1)} %get-tuple-element.129), channel_id=1, source_target_pairs={{0,8},{8,16},{16,24},{24,0},{1,9},{9,17},{17,25},{25,1},{2,10},{10... | collective-permute-start | bytes 2359304 | tf_op jit(solution)/shard_map/ppermute | solution.py:488
  766.7 4.6 copy-start.1
  766.7 4.6 copy-start.10
  766.7 42.5 %all-to-all-start.3 = ((bf16[8,48,8,512]{3,2,1,0:T(8,128)(2,1)}), bf16[8,48,8,512]{3,2,1,0:T(8,128)(2,1)}, u32[]{:S(2)}, u32[]{:S(2)}) async-start(bf16[8,48,8,512]{3,2,1,0:T(8,128)(2,1)} %get-tuple-element.125), calls=%async_computation.3 | async-start | bytes 6291456 | tf_op jit(solution)/shard_map/all_to_all | solution.py:598
  809.2 45.3 %all-to-all-start.4 = ((bf16[8,48,8,512]{3,2,1,0:T(8,128)(2,1)}), bf16[8,48,8,512]{3,2,1,0:T(8,128)(2,1)}, u32[]{:S(2)}, u32[]{:S(2)}) async-start(bf16[8,48,8,512]{3,2,1,0:T(8,128)(2,1)} %get-tuple-element.131), calls=%async_computation.4 | async-start | bytes 6291456 | tf_op jit(solution)/shard_map/all_to_all | solution.py:598
  813.7 40.8 %copy-start.21 = (bf16[1,8,192,256]{3,2,1,0:T(8,128)(2,1)}, bf16[1,8,192,256]{3,2,1,0:T(8,128)(2,1)S(1)}, u32[]{:S(2)}) copy-start(bf16[1,8,192,256]{3,2,1,0:T(8,128)(2,1)S(1)} %collective-permute-done.21.refs_1_.refs_5_) | copy-start | bytes 2359300
  833.9 20.6 %copy-start.23 = (bf16[1,8,192,256]{3,2,1,0:T(8,128)(2,1)}, bf16[1,8,192,256]{3,2,1,0:T(8,128)(2,1)S(1)}, u32[]{:S(2)}) copy-start(bf16[1,8,192,256]{3,2,1,0:T(8,128)(2,1)S(1)} %collective-permute-done.22.refs_2_.refs_6_) | copy-start | bytes 2359300
  833.9 1.6 copy-start.34
  854.5 4.8 copy-start.59
  854.5 4.9 copy-start.58
  854.5 42.5 %all-to-all-start.5 = ((bf16[8,48,8,512]{3,2,1,0:T(8,128)(2,1)}), bf16[8,48,8,512]{3,2,1,0:T(8,128)(2,1)}, u32[]{:S(2)}, u32[]{:S(2)}) async-start(bf16[8,48,8,512]{3,2,1,0:T(8,128)(2,1)} %after.3), calls=%async_computation.5 | async-start | bytes 6291456 | tf_op jit(solution)/shard_map/all_to_all | solution.py:598
  922.8 76.4 %all-to-all-start.6 = ((bf16[8,48,16,512]{3,2,1,0:T(8,128)(2,1)}), bf16[8,48,16,512]{3,2,1,0:T(8,128)(2,1)}, u32[]{:S(2)}, u32[]{:S(2)}) async-start(bf16[8,48,16,512]{3,2,1,0:T(8,128)(2,1)} %get-tuple-element.134), calls=%async_computation.6 | async-start | bytes 12582912 | tf_op jit(solution)/shard_map/all_to_all | solution.py:609
  999.2 5.2 copy-start.12
  999.2 76.8 %all-to-all-start.8 = ((bf16[8,48,16,512]{3,2,1,0:T(8,128)(2,1)}), bf16[8,48,16,512]{3,2,1,0:T(8,128)(2,1)}, u32[]{:S(2)}, u32[]{:S(2)}) async-start(bf16[8,48,16,512]{3,2,1,0:T(8,128)(2,1)} %get-tuple-element.139), calls=%async_computation.8 | async-start | bytes 12582912 | tf_op jit(solution)/shard_map/all_to_all | solution.py:613
  1004.4 1.4 copy-start.15
  1076.0 4.9 copy-start.20
  1076.0 76.5 %all-to-all-start.7 = ((bf16[8,48,16,512]{3,2,1,0:T(8,128)(2,1)}), bf16[8,48,16,512]{3,2,1,0:T(8,128)(2,1)}, u32[]{:S(2)}, u32[]{:S(2)}) async-start(bf16[8,48,16,512]{3,2,1,0:T(8,128)(2,1)} %get-tuple-element.138), calls=%async_computation.7 | async-start | bytes 12582912 | tf_op jit(solution)/shard_map/all_to_all | solution.py:613
  1083.6 68.9 %copy-start.22 = (bf16[1,8,192,256]{3,2,1,0:T(8,128)(2,1)S(1)}, bf16[1,8,192,256]{3,2,1,0:T(8,128)(2,1)}, u32[]{:S(2)}) copy-start(bf16[1,8,192,256]{3,2,1,0:T(8,128)(2,1)} %copy-done.21) | copy-start | bytes 2359300
  (30 other events, 32.8 us)

commit v4 on v3

--- a/solution.py
+++ b/solution.py
@@ -196,8 +196,8 @@
         cotangent_row(row, member_refs, target_ref, weight_ref, put)
 
 
-def pick(slot, share, channels):
-    return pl.BlockSpec((1, 1, share, channels), lambda i, q: (slot, i, 0, 0))
+def pick(slot, share, channels, batch=1):
+    return pl.BlockSpec((1, batch, share, channels), lambda i, q: (slot, i, 0, 0))
 
 
 def exchange_rows(
@@ -242,36 +242,43 @@
 
 
 def backward_kernel(me_ref, saved_ref, up_ref, down_t_ref, up_t_ref, synth_ref, _, __, *refs):
-    members = len(refs) - 5
-    out_ref, token_ref, cot_ref, mixed_ref, waves_ref = refs[members:]
+    members = len(refs) - 4
+    out_ref, token_ref, cot_ref, waves_ref = refs[members:]
     put_token(token_ref)
-    lon, channels = mixed_ref.shape
+    batch, lon, channels = saved_ref.shape
     share = lon // members
-    for piece in range(members):
-        cot_ref[share_of(me_ref, piece, members, share), :] = refs[piece][0, 0]
-    for start in range(0, lon, lon // 2):
-        place = pl.ds(start, lon // 2)
-        v = dot(saved_ref[0, place, :], up_ref[...])
-        square = v * v
-        half = 0.5 + 0.5 * jnp.tanh(v * (kappa_gelu + (kappa_gelu * cubic_gelu) * square))
-        inner = v * (2.0 * kappa_gelu + (6.0 * kappa_gelu * cubic_gelu) * square)
-        slopes = half * (1.0 + (1.0 - half) * inner)
-        act_grad = dot(cot_ref[place, :], down_t_ref[...])
-        pre_grad = (act_grad * slopes).astype(BF16)
-        mixed_ref[place, :] = dot(pre_grad, up_t_ref[...]).astype(BF16)
-    wave = dot(synth_ref[...], mixed_ref[...])
+    for b in range(batch):
+        for piece in range(members):
+            cot_ref[b, share_of(me_ref, piece, members, share), :] = refs[piece][0, b]
+    mixed = []
+    for b in range(batch):
+        halves = []
+        for start in range(0, lon, lon // 2):
+            place = pl.ds(start, lon // 2)
+            v = dot(saved_ref[b, place, :], up_ref[...])
+            square = v * v
+            half = 0.5 + 0.5 * jnp.tanh(v * (kappa_gelu + (kappa_gelu * cubic_gelu) * square))
+            inner = v * (2.0 * kappa_gelu + (6.0 * kappa_gelu * cubic_gelu) * square)
+            slopes = half * (1.0 + (1.0 - half) * inner)
+            act_grad = dot(cot_ref[b, place, :], down_t_ref[...])
+            pre_grad = (act_grad * slopes).astype(BF16)
+            halves.append(dot(pre_grad, up_t_ref[...]).astype(BF16))
+        mixed.append(jnp.concatenate(halves, axis=0))
+    wave = dot(synth_ref[...], jnp.concatenate(mixed, axis=1))
     modes = wave.shape[0] // 2
-    row = pl.program_id(0)
+    step = pl.program_id(0)
     rows = out_ref.shape[2]
-    place = pl.ds(row, modes, stride=rows)
-    lanes = waves_ref.shape[2]
-    for index in range(waves_ref.shape[0]):
-        part, lane = divmod(index * lanes, channels)
-        waves_ref[index, place, :] = wave[part * modes : (part + 1) * modes, lane : lane + lanes]
-
-    @pl.when(row == rows - 1)
+    count, _, lanes = waves_ref.shape
+    for b in range(batch):
+        place = pl.ds(step * batch + b, modes, stride=rows)
+        for index in range(count):
+            part, lane = divmod(index * lanes, channels)
+            lane += b * channels
+            waves_ref[index, place, :] = wave[part * modes : (part + 1) * modes, lane : lane + lanes]
+
+    @pl.when(step == pl.num_programs(0) - 1)
     def _():
-        for index in range(waves_ref.shape[0]):
+        for index in range(count):
             block = waves_ref[index].reshape(out_ref.shape[:3] + (lanes,))
             out_ref[..., index * lanes : (index + 1) * lanes] = block.astype(BF16)
 
@@ -281,15 +288,16 @@
     _, rows, share, channels = cot[0][0].shape
     lon = saved.shape[1]
     modes = synth.shape[0] // 2
+    batch = math.gcd(rows, 2)
     whole = lambda a: pl.BlockSpec(a.shape, lambda i, q: (0, 0))
     out_shape = (groups, modes // groups, rows, 2 * channels)
     return pl.pallas_call(
         backward_kernel,
         grid_spec=pltpu.PrefetchScalarGridSpec(
             num_scalar_prefetch=1,
-            grid=(rows,),
+            grid=(rows // batch,),
             in_specs=[
-                pl.BlockSpec((1, lon, channels), lambda i, q: (first + i, 0, 0)),
+                pl.BlockSpec((batch, lon, channels), lambda i, q: (first // batch + i, 0, 0)),
                 whole(up_weight),
                 whole(down_t),
                 whole(up_t),
@@ -297,11 +305,10 @@
                 TOKEN_IN,
                 TOKEN_IN,
             ]
-            + [pick(slot, share, channels) for _, slot in cot],
+            + [pick(slot, share, channels, batch) for _, slot in cot],
             out_specs=[pl.BlockSpec(out_shape, lambda i, q: (0, 0, 0, 0)), TOKEN_OUT],
             scratch_shapes=[
-                pltpu.VMEM((lon, channels), BF16),
-                pltpu.VMEM((lon, channels), BF16),
+                pltpu.VMEM((batch, lon, channels), BF16),
                 strips(modes * rows, 2 * channels),
             ],
         ),
@@ -416,27 +423,31 @@
     rows = every // joined
     count, _, lanes = waves_ref.shape
     channels = out_ref.shape[-1]
-    row = pl.program_id(0)
-
-    @pl.when(row == 0)
+    batch = out_ref.shape[1]
+    step = pl.program_id(0)
+
+    @pl.when(step == 0)
     def _():
         for index in range(count):
             block = wave_ref[..., index * lanes : (index + 1) * lanes].astype(F32)
             waves_ref[index] = block.reshape(waves_ref.shape[1:])
 
-    at = pl.ds(row, waves_ref.shape[1] // every, stride=every)
-    strip = [waves_ref[index, at, :].astype(BF16) for index in range(count)]
     half = count // 2
-    wave = jnp.concatenate(
-        [jnp.concatenate(strip[:half], axis=1), jnp.concatenate(strip[half:], axis=1)], axis=0
-    )
+    columns = [[], []]
+    for b in range(batch):
+        at = pl.ds(step * batch + b, waves_ref.shape[1] // every, stride=every)
+        for index in range(count):
+            columns[index // half].append(waves_ref[index, at, :].astype(BF16))
+    wave = jnp.concatenate([jnp.concatenate(column, axis=1) for column in columns], axis=0)
     spatial_ref[...] = dot(analysis_ref[...], wave)
-    for piece in range(members):
-        place = share_of(me_ref, piece, members, share)
-        cot = refs[piece][0, 0]
-        for part in range(1, joined):
-            cot = jnp.where(row >= part * rows, refs[part * members + piece][0, 0], cot)
-        out_ref[0, 0, place, :] = (cot.astype(F32) + spatial_ref[place, :] * scale).astype(BF16)
+    for b in range(batch):
+        for piece in range(members):
+            place = share_of(me_ref, piece, members, share)
+            cot = refs[piece][0, b]
+            for part in range(1, joined):
+                cot = jnp.where(step * batch >= part * rows, refs[part * members + piece][0, b], cot)
+            spatial = spatial_ref[place, b * channels : (b + 1) * channels]
+            out_ref[0, b, place, :] = (cot.astype(F32) + spatial * scale).astype(BF16)
 
 
 def output_rows(token, index, shape, me, wave, cots, analysis, held):
@@ -444,6 +455,7 @@
     joined, members = len(cots), len(cots[0])
     _, each, share, channels = cots[0][0][0].shape
     lon = shape[2]
+    batch = math.gcd(each, 4)
     in_specs = [
         pl.BlockSpec(wave.shape, lambda i, q: (0, 0, 0, 0)),
         pl.BlockSpec(analysis.shape, lambda i, q: (0, 0)),
@@ -452,8 +464,13 @@
     operands = [me, wave, analysis, token]
     for part, cot in enumerate(cots):
         for array, slot in cot:
-            place = lambda i, q, at=part * each, slot=slot: (slot, jnp.clip(i - at, 0, each - 1), 0, 0)
-            in_specs.append(pl.BlockSpec((1, 1, share, channels), place))
+            place = lambda i, q, at=part * each // batch, slot=slot: (
+                slot,
+                jnp.clip(i - at, 0, each // batch - 1),
+                0,
+                0,
+            )
+            in_specs.append(pl.BlockSpec((1, batch, share, channels), place))
             operands.append(array)
     aliases = {}
     if held is not None:
@@ -464,13 +481,15 @@
         functools.partial(output_kernel, joined, members, 1.0 / lon),
         grid_spec=pltpu.PrefetchScalarGridSpec(
             num_scalar_prefetch=1,
-            grid=(rows,),
+            grid=(rows // batch,),
             in_specs=in_specs,
             out_specs=[
-                pl.BlockSpec((1, 1, lon, channels), lambda i, q: (0, index * rows + i, 0, 0)),
+                pl.BlockSpec(
+                    (1, batch, lon, channels), lambda i, q: (0, index * (rows // batch) + i, 0, 0)
+                ),
                 TOKEN_OUT,
             ],
-            scratch_shapes=[strips(groups * modes * rows, columns), pltpu.VMEM((lon, channels), F32)],
+            scratch_shapes=[strips(groups * modes * rows, columns), pltpu.VMEM((lon, batch * channels), F32)],
         ),
         out_shape=[jax.ShapeDtypeStruct(shape, BF16), TOKEN],
         input_output_aliases=aliases,
@@ -505,12 +524,12 @@
 
 
 def kernel_order(parts, ahead):
-    order = [("exchange", -ahead), ("exchange", 1 - ahead), ("table", 0)]
-    for step in range(2 - ahead, parts + 2):
-        order.append(("exchange", step) if step < parts else None)
-        order.append(("backward", step - 2) if step >= 2 else None)
-        order.append(("gate", 0) if step == parts - 1 else None)
-    return [entry for entry in order if entry is not None]
+    order = [("exchange", step) for step in range(-ahead, parts)]
+    order.insert(2, ("table", 0))
+    for part in range(parts):
+        place = order.index(("exchange", min(part + 2, parts - 1))) + 1
+        order.insert(place if part + 2 < parts else len(order), ("backward", part))
+    return order
 
 
 def shards(
@@ -545,7 +564,7 @@
     token = jnp.zeros(TOKEN.shape, F32)
     values, cots, waves = {}, {}, {}
     table = None
-    ahead = 2
+    ahead = min(3, parts)
     for kind, part in kernel_order(parts, ahead):
         if kind == "table":
             table, token = legendre_table(token, local_orders, angles, total_lat)
@@ -567,19 +586,11 @@
                 weights,
                 values.get(cotangent),
             )
-            held = pieces
-            if part == parts - 1:
-                continue
-        if kind == "gate":
-            earlier = [array for array, _ in cots[parts - 2][1:]]
-            *moved, token = after(held[1:] + [token], *earlier)
-            held = held[:1] + moved
-        if kind in ("exchange", "gate"):
-            moved = shift(held)
+            moved = shift(pieces)
             values[forward] = [(array, 0) for array in moved]
             slot = 0 if forward is None else 1
             cots[cotangent] = [(moved[-piece % members], slot) for piece in range(members)]
-        if kind == "backward":
+        else:
             wave, token = backward_rows(
                 token,
                 waves.get(part - 2, token),

time: 1200 us -> 1180 us (0.983); the launches traced: 1180 us -> 1170 us
  Pallas kernels: 354 us -> 320 us
  waiting for transfers between devices: 426 us -> 449 us
  starting transfers between devices: 332 us -> 346 us
    pallas_call x6, Pallas kernels: 108 us -> 87.5 us  [backward_rows(): pl.pallas_call(backward_kernel, grid_spec=pltpu.PrefetchScalarGridSpec(nu...]
    pallas_call x3, Pallas kernels: 64 us -> 45.3 us  [output_rows(): pl.pallas_call(functools.partial(output_kernel, joined, members, 1.0 / lo...]
    ppermute x24 -> x27, waiting for transfers between devices: 237 us -> 253 us  [shift(): moved.append(lax.ppermute(pieces[piece], 'member', pairs))]
    all_to_all x2, waiting for transfers between devices: 78 us -> 93.5 us  [shards(): lat_waves[step] = lax.all_to_all(wave, 'lat', 0, 0, tiled=True)]
    ppermute x24 -> x27, starting transfers between devices: 289 us -> 305 us  [shift(): moved.append(lax.ppermute(pieces[piece], 'member', pairs))]
    unnamed x126 -> x102, local copies, waits for them, and re-layouts: 42.4 us -> 31.6 us
    pallas_call x8 -> x9, Pallas kernels: 88.3 us -> 93.6 us  [exchange_rows(): pl.pallas_call(functools.partial(exchange_kernel, members, forward, cotan...]
  transfers between devices with their start and end apart: 33 -> 36, of which waited for: 10 -> 12; matrix products, arithmetic and copies ran while one was open for 2% -> 2% of each run, Pallas kernels for 25% -> 23%
where the time goes in v4:
time: 1180 us; the launch traced here: 1170 us
  waiting for transfers between devices  449 us (38%)
  starting transfers between devices  346 us (29%)
  Pallas kernels  320 us (27%)
  local copies, waits for them, and re-layouts  32.7 us (3%)
  other arithmetic  22.1 us (2%)
    ppermute x27, starting transfers between devices, shift(): moved.append(lax.ppermute(pieces[piece], 'member', pairs))  305 us
    ppermute x27, waiting for transfers between devices, shift(): moved.append(lax.ppermute(pieces[piece], 'member', pairs))  253 us
    pallas_call x9, Pallas kernels, exchange_rows(): pl.pallas_call(functools.partial(exchange_kernel, members, forward, cotan...  93.6 us
    all_to_all x2, waiting for transfers between devices, shards(): lat_waves[step] = lax.all_to_all(wave, 'lat', 0, 0, tiled=True)  93.5 us
    pallas_call x6, Pallas kernels, backward_rows(): pl.pallas_call(backward_kernel, grid_spec=pltpu.PrefetchScalarGridSpec(nu...  87.5 us
    all_to_all x1, waiting for transfers between devices, shards(): lat_waves = {0: lax.all_to_all(wave, 'lat', 0, 0, tiled=True)}  55.9 us
    all_to_all x6, waiting for transfers between devices, shards(): waves[part] = lax.all_to_all(wave, 'lat', 0, 0, tiled=True)  46.2 us
    pallas_call x3, Pallas kernels, output_rows(): pl.pallas_call(functools.partial(output_kernel, joined, members, 1.0 / lo...  45.3 us
  transfers between devices with their start and end apart: 36, of which 12 were waited for; matrix products, arithmetic and copies ran while one was open for 2% of the time, Pallas kernels for 23%

profile of v4, /device:TPU:0, one launch (start us, length us, event | category | flops | bytes accessed | tf_op | source)
XLA Modules:
  0.0 1171.0 jit_solution(15205387662645099173)
XLA Ops:
  1.9 9.6 exchange.9
  12.4 3.0 collective-permute-start
  15.4 2.6 collective-permute-start.1
  19.3 9.5 exchange.10
  31.6 36.6 %legendre.1 = (bf16[48,384,384]{2,1,0:T(8,128)(2,1)}, f32[8,128]{1,0:T(8,128)S(1)}) custom-call(f32[48,384]{1,0:T(8,128)S(1)} %multiply_add_fusion.start_ref, f32[1,384]{1,0:T(1,128)S(1)} %reshape.204.cosine_ref, f32[48,1]{1,0:T(8,128)S(1)} %add_convert_fusion.order_ref, f32[8,128]{1,0:T(8,128)S(1)} %get-tuple-element.77._), custom_call_target="tpu_custom_call" | custom-call | flops 49999998976 | bytes 1000 | tf_op jit(solution)/shard_map/legendre/pallas_call | solution.py:108
  68.1 9.6 exchange.11
  79.1 21.4 %select_convert_fusion = (bf16[768,768]{1,0:T(8,128)(2,1)}, bf16[768,768]{1,0:T(8,128)(2,1)S(1)}) fusion(s32[768]{0:T(1024)S(1)} %fusion.14, pred[768]{0:T(1024)(128)(4,1)S(1)} %fusion.20, f32[768]{0:T(1024)S(1)} %compare_select_fusion), kind=kLoop, calls=%fused_computation.6 | loop fusion | flops 14745600 | bytes 2366208 | tf_op jit(solution)/shard_map/convert_element_type | solution.py:54
  100.5 2.8 collective-permute-start.5
  103.9 16.5 %collective-permute-start.7 = (bf16[1,8,192,256]{3,2,1,0:T(8,128)(2,1)}, bf16[1,8,192,256]{3,2,1,0:T(8,128)(2,1)S(1)}, u32[]{:S(2)}, u32[]{:S(2)}) collective-permute-start(bf16[1,8,192,256]{3,2,1,0:T(8,128)(2,1)} %get-tuple-element.93), channel_id=1, source_target_pairs={{0,16},{8,24},{16,0},{24,8},{1,17},{9,25},{17,1},{25,9},{2,18},{10... | collective-permute-start | bytes 2359304 | tf_op jit(solution)/shard_map/ppermute | solution.py:507
  120.4 13.0 %exchange.12 = (bf16[2,8,192,256]{3,2,1,0:T(8,128)(2,1)S(1)}, bf16[2,8,192,256]{3,2,1,0:T(8,128)(2,1)}, bf16[2,8,192,256]{3,2,1,0:T(8,128)(2,1)}, bf16[2,8,192,256]{3,2,1,0:T(8,128)(2,1)}, f32[8,128]{1,0:T(8,128)S(1)}) custom-call(s32[1]{0:T(128)} %bitcast.me_ref, f32[8,128]{1,0:T(8,128)S(1)} %get-tuple-element.80.refs_0_, bf16[48,768,256]{2,1,0:T(8,128)(2,1)} %bitcast.30, ...), custom_call_target="tpu_custom_call" | custom-call | flops 49999998976 | bytes 1000 | tf_op jit(solution)/shard_map/exchange/pallas_call | solution.py:228
  133.5 3.8 collective-permute-start.8
  137.3 33.0 %collective-permute-done.4.refs_9_ = bf16[1,8,192,256]{3,2,1,0:T(8,128)(2,1)} collective-permute-done((bf16[1,8,192,256]{3,2,1,0:T(8,128)(2,1)}, bf16[1,8,192,256]{3,2,1,0:T(8,128)(2,1)}, u32[]{:S(2)}, u32[]{:S(2)}) %collective-permute-start.4) | collective-permute-done | bytes 786464 | tf_op jit(solution)/shard_map/ppermute | solution.py:507
  170.3 53.8 %collective-permute-start.11 = (bf16[2,8,192,256]{3,2,1,0:T(8,128)(2,1)}, bf16[2,8,192,256]{3,2,1,0:T(8,128)(2,1)}, u32[]{:S(2)}, u32[]{:S(2)}) collective-permute-start(bf16[2,8,192,256]{3,2,1,0:T(8,128)(2,1)} %get-tuple-element.99), channel_id=1, source_target_pairs={{0,8},{8,16},{16,24},{24,0},{1,9},{9,17},{17,25},{25,1},{2,10},{10... | collective-permute-start | bytes 4718600 | tf_op jit(solution)/shard_map/ppermute | solution.py:507
  224.1 12.9 %exchange.13 = (bf16[2,8,192,256]{3,2,1,0:T(8,128)(2,1)S(1)}, bf16[2,8,192,256]{3,2,1,0:T(8,128)(2,1)}, bf16[2,8,192,256]{3,2,1,0:T(8,128)(2,1)}, bf16[2,8,192,256]{3,2,1,0:T(8,128)(2,1)}, f32[8,128]{1,0:T(8,128)S(1)}) custom-call(s32[1]{0:T(128)} %bitcast.me_ref, f32[8,128]{1,0:T(8,128)S(1)} %get-tuple-element.85.refs_0_, bf16[48,768,256]{2,1,0:T(8,128)(2,1)} %bitcast.31, ...), custom_call_target="tpu_custom_call" | custom-call | flops 49999998976 | bytes 1000 | tf_op jit(solution)/shard_map/exchange/pallas_call | solution.py:228
  238.2 20.2 %collective-permute-start.12 = (bf16[2,8,192,256]{3,2,1,0:T(8,128)(2,1)}, bf16[2,8,192,256]{3,2,1,0:T(8,128)(2,1)}, u32[]{:S(2)}, u32[]{:S(2)}) collective-permute-start(bf16[2,8,192,256]{3,2,1,0:T(8,128)(2,1)} %get-tuple-element.103), channel_id=1, source_target_pairs={{0,24},{8,0},{16,8},{24,16},{1,25},{9,1},{17,9},{25,17},{2,26},{10... | collective-permute-start | bytes 4718600 | tf_op jit(solution)/shard_map/ppermute | solution.py:507
  258.4 12.7 %exchange.14 = (bf16[2,8,192,256]{3,2,1,0:T(8,128)(2,1)S(1)}, bf16[2,8,192,256]{3,2,1,0:T(8,128)(2,1)}, bf16[2,8,192,256]{3,2,1,0:T(8,128)(2,1)}, bf16[2,8,192,256]{3,2,1,0:T(8,128)(2,1)}, f32[8,128]{1,0:T(8,128)S(1)}) custom-call(s32[1]{0:T(128)} %bitcast.me_ref, f32[8,128]{1,0:T(8,128)S(1)} %get-tuple-element.90.refs_0_, bf16[48,768,256]{2,1,0:T(8,128)(2,1)} %bitcast.32, ...), custom_call_target="tpu_custom_call" | custom-call | flops 49999998976 | bytes 1000 | tf_op jit(solution)/shard_map/exchange/pallas_call | solution.py:228
  272.2 49.7 %collective-permute-done.10.refs_2_.refs_5_ = bf16[2,8,192,256]{3,2,1,0:T(8,128)(2,1)S(1)} collective-permute-done((bf16[2,8,192,256]{3,2,1,0:T(8,128)(2,1)}, bf16[2,8,192,256]{3,2,1,0:T(8,128)(2,1)S(1)}, u32[]{:S(2)}, u32[]{:S(2)}) %collective-permute-start.10) | collective-permute-done | bytes 1572896 | tf_op jit(solution)/shard_map/ppermute | solution.py:507
  321.9 67.3 %collective-permute-start.14 = (bf16[2,8,192,256]{3,2,1,0:T(8,128)(2,1)}, bf16[2,8,192,256]{3,2,1,0:T(8,128)(2,1)}, u32[]{:S(2)}, u32[]{:S(2)}) collective-permute-start(bf16[2,8,192,256]{3,2,1,0:T(8,128)(2,1)} %get-tuple-element.105), channel_id=1, source_target_pairs={{0,8},{8,16},{16,24},{24,0},{1,9},{9,17},{17,25},{25,1},{2,10},{10... | collective-permute-start | bytes 4718600 | tf_op jit(solution)/shard_map/ppermute | solution.py:507
  389.3 2.8 collective-permute-start.15
  392.0 83.5 %collective-permute-start.16 = (bf16[2,8,192,256]{3,2,1,0:T(8,128)(2,1)}, bf16[2,8,192,256]{3,2,1,0:T(8,128)(2,1)}, u32[]{:S(2)}, u32[]{:S(2)}) collective-permute-start(bf16[2,8,192,256]{3,2,1,0:T(8,128)(2,1)} %get-tuple-element.111), channel_id=1, source_target_pairs={{0,16},{8,24},{16,0},{24,8},{1,17},{9,25},{17,1},{25,9},{2,18},{10... | collective-permute-start | bytes 4718600 | tf_op jit(solution)/shard_map/ppermute | solution.py:507
  475.5 14.6 %backward.6 = (bf16[8,48,8,512]{3,2,1,0:T(8,128)(2,1)}, f32[8,128]{1,0:T(8,128)S(1)}) custom-call(s32[1]{0:T(128)} %bitcast.me_ref, bf16[48,768,256]{2,1,0:T(8,128)(2,1)} %bitcast.33, bf16[256,512]{1,0:T(8,128)(2,1)S(1)} %copy-done.3, bf16[256,512]{1,0:T(8,128)(2,1)S(1)} %bitcast.8, bf16[512,256]{1,0:T(8,128)(2,1)S(1)} %bitcast.14, ...), custom_call_target="tpu_custom_call" | custom-call | flops 49999998976 | bytes 1000 | tf_op jit(solution)/shard_map/backward/pallas_call | solution.py:294
  490.1 4.5 all-to-all-start
  496.0 9.1 exchange.15
  505.9 2.0 collective-permute-start.17
  507.9 50.0 %collective-permute-done.13.refs_2_.refs_5_.refs_6_ = bf16[2,8,192,256]{3,2,1,0:T(8,128)(2,1)} collective-permute-done((bf16[2,8,192,256]{3,2,1,0:T(8,128)(2,1)}, bf16[2,8,192,256]{3,2,1,0:T(8,128)(2,1)}, u32[]{:S(2)}, u32[]{:S(2)}) %collective-permute-start.13) | collective-permute-done | bytes 1572896 | tf_op jit(solution)/shard_map/ppermute | solution.py:507
  558.0 1.8 collective-permute-start.19
  559.7 14.7 %backward.7 = (bf16[8,48,8,512]{3,2,1,0:T(8,128)(2,1)}, f32[8,128]{1,0:T(8,128)S(1)}) custom-call(s32[1]{0:T(128)} %bitcast.me_ref, bf16[48,768,256]{2,1,0:T(8,128)(2,1)} %bitcast.34, bf16[256,512]{1,0:T(8,128)(2,1)S(1)} %copy-done.3, bf16[256,512]{1,0:T(8,128)(2,1)S(1)} %bitcast.9, bf16[512,256]{1,0:T(8,128)(2,1)S(1)} %bitcast.15, ...), custom_call_target="tpu_custom_call" | custom-call | flops 49999998976 | bytes 1000 | tf_op jit(solution)/shard_map/backward/pallas_call | solution.py:294
  574.4 9.0 exchange.16
  584.3 4.4 all-to-all-start.1
  588.7 37.2 %collective-permute-start.20 = (bf16[1,8,192,256]{3,2,1,0:T(8,128)(2,1)}, bf16[1,8,192,256]{3,2,1,0:T(8,128)(2,1)S(1)}, u32[]{:S(2)}, u32[]{:S(2)}) collective-permute-start(bf16[1,8,192,256]{3,2,1,0:T(8,128)(2,1)} %get-tuple-element.119), channel_id=1, source_target_pairs={{0,8},{8,16},{16,24},{24,0},{1,9},{9,17},{17,25},{25,1},{2,10},{10... | collective-permute-start | bytes 2359304 | tf_op jit(solution)/shard_map/ppermute | solution.py:507
  625.9 33.1 %collective-permute-done.16.refs_2_.refs_5_ = bf16[2,8,192,256]{3,2,1,0:T(8,128)(2,1)} collective-permute-done((bf16[2,8,192,256]{3,2,1,0:T(8,128)(2,1)}, bf16[2,8,192,256]{3,2,1,0:T(8,128)(2,1)}, u32[]{:S(2)}, u32[]{:S(2)}) %collective-permute-start.16) | collective-permute-done | bytes 1572896 | tf_op jit(solution)/shard_map/ppermute | solution.py:507
  659.2 1.6 collective-permute-start.22
  662.1 1.4 copy-done.28
  663.5 14.6 %backward.8 = (bf16[8,48,8,512]{3,2,1,0:T(8,128)(2,1)}, f32[8,128]{1,0:T(8,128)S(1)}) custom-call(s32[1]{0:T(128)} %bitcast.me_ref, bf16[48,768,256]{2,1,0:T(8,128)(2,1)} %bitcast.35, bf16[256,512]{1,0:T(8,128)(2,1)S(1)} %copy-done.3, bf16[256,512]{1,0:T(8,128)(2,1)S(1)} %bitcast.10, bf16[512,256]{1,0:T(8,128)(2,1)S(1)} %bitcast.16, ...), custom_call_target="tpu_custom_call" | custom-call | flops 49999998976 | bytes 1000 | tf_op jit(solution)/shard_map/backward/pallas_call | solution.py:294
  678.2 8.2 exchange.17
  689.5 4.5 all-to-all-start.2
  694.0 32.5 %collective-permute-done.19.refs_2_.refs_6_ = bf16[1,8,192,256]{3,2,1,0:T(8,128)(2,1)} collective-permute-done((bf16[1,8,192,256]{3,2,1,0:T(8,128)(2,1)}, bf16[1,8,192,256]{3,2,1,0:T(8,128)(2,1)}, u32[]{:S(2)}, u32[]{:S(2)}) %collective-permute-start.19) | collective-permute-done | bytes 786464 | tf_op jit(solution)/shard_map/ppermute | solution.py:507
  726.5 1.7 collective-permute-start.25
  730.6 14.6 %backward.9 = (bf16[8,48,8,512]{3,2,1,0:T(8,128)(2,1)}, f32[8,128]{1,0:T(8,128)S(1)}) custom-call(s32[1]{0:T(128)} %bitcast.me_ref, bf16[48,768,256]{2,1,0:T(8,128)(2,1)} %bitcast.36, bf16[256,512]{1,0:T(8,128)(2,1)S(1)} %copy-done.3, bf16[256,512]{1,0:T(8,128)(2,1)S(1)} %bitcast.11, bf16[512,256]{1,0:T(8,128)(2,1)S(1)} %bitcast.17, ...), custom_call_target="tpu_custom_call" | custom-call | flops 49999998976 | bytes 1000 | tf_op jit(solution)/shard_map/backward/pallas_call | solution.py:294
  745.2 4.4 all-to-all-start.3
  750.3 43.6 %collective-permute-done.22.refs_2_ = bf16[1,8,192,256]{3,2,1,0:T(8,128)(2,1)} collective-permute-done((bf16[1,8,192,256]{3,2,1,0:T(8,128)(2,1)}, bf16[1,8,192,256]{3,2,1,0:T(8,128)(2,1)}, u32[]{:S(2)}, u32[]{:S(2)}) %collective-permute-start.22) | collective-permute-done | bytes 786464 | tf_op jit(solution)/shard_map/ppermute | solution.py:507
  793.9 1.6 copy-done.20
  796.6 14.6 %backward.10 = (bf16[8,48,8,512]{3,2,1,0:T(8,128)(2,1)}, f32[8,128]{1,0:T(8,128)S(1)}) custom-call(s32[1]{0:T(128)} %bitcast.me_ref, bf16[48,768,256]{2,1,0:T(8,128)(2,1)} %bitcast.37, bf16[256,512]{1,0:T(8,128)(2,1)S(1)} %copy-done.3, bf16[256,512]{1,0:T(8,128)(2,1)S(1)} %bitcast.12, bf16[512,256]{1,0:T(8,128)(2,1)S(1)} %bitcast.18, ...), custom_call_target="tpu_custom_call" | custom-call | flops 49999998976 | bytes 1000 | tf_op jit(solution)/shard_map/backward/pallas_call | solution.py:294
  811.2 4.8 all-to-all-start.4
  816.0 11.5 collective-permute-done.25.refs_2_.refs_6_
  827.5 1.5 copy-done.21
  829.1 14.6 %backward.11 = (bf16[8,48,8,512]{3,2,1,0:T(8,128)(2,1)}, f32[8,128]{1,0:T(8,128)S(1)}) custom-call(s32[1]{0:T(128)} %bitcast.me_ref, bf16[48,768,256]{2,1,0:T(8,128)(2,1)} %bitcast.38, bf16[256,512]{1,0:T(8,128)(2,1)S(1)} %copy-done.3, bf16[256,512]{1,0:T(8,128)(2,1)S(1)} %bitcast.13, bf16[512,256]{1,0:T(8,128)(2,1)S(1)} %bitcast.19, ...), custom_call_target="tpu_custom_call" | custom-call | flops 49999998976 | bytes 1000 | tf_op jit(solution)/shard_map/backward/pallas_call | solution.py:294
  843.6 10.3 all-to-all-done.4.__1_.refs_4_
  853.9 3.8 all-to-all-start.5
  859.6 35.9 %all-to-all-done.5.refs_5_ = bf16[8,48,8,512]{3,2,1,0:T(8,128)(2,1)S(1)} async-done(((bf16[8,48,8,512]{3,2,1,0:T(8,128)(2,1)}), bf16[8,48,8,512]{3,2,1,0:T(8,128)(2,1)S(1)}, u32[]{:S(2)}, u32[]{:S(2)}) %all-to-all-start.5) | async-done | bytes 3145760 | tf_op jit(solution)/shard_map/all_to_all | solution.py:609
  895.5 1.6 copy-done.45
  897.1 25.8 %spectral.1 = (bf16[48,384,512]{2,1,0:T(8,128)(2,1)}, bf16[8,48,16,512]{3,2,1,0:T(8,128)(2,1)}, f32[8,128]{1,0:T(8,128)S(1)}) custom-call(bf16[48,384,384]{2,1,0:T(8,128)(2,1)} %get-tuple-element.78.table_ref, f32[384,1]{1,0:T(8,128)S(1)} %broadcast_in_dim.70.gain_ref, bf16[256,256]{1,0:T(8,128)(2,1)S(1)} %bitcast.20, f32[128,1]{1,0:T(8,128)S(1)} %slice.28.quad_ref, ...), custom_call_target="tpu_custom_call" | custom-call | flops 49999998976 | bytes 1000 | tf_op jit(solution)/shard_map/spectral/pallas_call | solution.py:361
  922.9 4.9 all-to-all-start.6
  928.0 15.6 %latitude.2 = (bf16[8,48,16,512]{3,2,1,0:T(8,128)(2,1)}, f32[8,128]{1,0:T(8,128)S(1)}) custom-call(bf16[48,384,384]{2,1,0:T(8,128)(2,1)} %get-tuple-element.78.table_ref, f32[128,1]{1,0:T(8,128)S(1)} %slice.29.quad_ref, bf16[48,384,512]{2,1,0:T(8,128)(2,1)} %get-tuple-element.135.coeff_ref, f32[8,128]{1,0:T(8,128)S(1)} %get-tuple-element.137._), custom_call_target="tpu_custom_call" | custom-call | flops 49999998976 | bytes 1000 | tf_op jit(solution)/shard_map/latitude/pallas_call | solution.py:399
  943.6 55.9 %all-to-all-done.6.wave_ref = bf16[8,48,16,512]{3,2,1,0:T(8,128)(2,1)} async-done(((bf16[8,48,16,512]{3,2,1,0:T(8,128)(2,1)}), bf16[8,48,16,512]{3,2,1,0:T(8,128)(2,1)}, u32[]{:S(2)}, u32[]{:S(2)}) %all-to-all-start.6) | async-done | bytes 6291488 | tf_op jit(solution)/shard_map/all_to_all | solution.py:620
  999.4 5.0 all-to-all-start.8
  1005.8 1.4 copy-done.24
  1007.2 14.8 %output.3 = (bf16[1,48,768,256]{3,2,1,0:T(8,128)(2,1)}, f32[8,128]{1,0:T(8,128)S(1)}) custom-call(s32[1]{0:T(128)} %bitcast.me_ref, bf16[8,48,16,512]{3,2,1,0:T(8,128)(2,1)} %all-to-all-done.6.wave_ref, bf16[768,768]{1,0:T(8,128)(2,1)S(1)} %copy-done.15, f32[8,128]{1,0:T(8,128)S(1)} %get-tuple-element.138._, bf16[2,8,192,256]{3,2,1,0:T(8,128)(2,1)S(1)} %copy-done.24, ...), custom_call_target="tpu_custom_call" | custom-call | flops 49999998976 | bytes 1000 | tf_op jit(solution)/shard_map/output/pallas_call | solution.py:480
  1022.0 15.6 %latitude.3 = (bf16[8,48,16,512]{3,2,1,0:T(8,128)(2,1)}, f32[8,128]{1,0:T(8,128)S(1)}) custom-call(bf16[48,384,384]{2,1,0:T(8,128)(2,1)} %get-tuple-element.78.table_ref, f32[128,1]{1,0:T(8,128)S(1)} %slice.27.quad_ref, bf16[48,384,512]{2,1,0:T(8,128)(2,1)} %get-tuple-element.135.coeff_ref, f32[8,128]{1,0:T(8,128)S(1)} %get-tuple-element.139._), custom_call_target="tpu_custom_call" | custom-call | flops 49999998976 | bytes 1000 | tf_op jit(solution)/shard_map/latitude/pallas_call | solution.py:399
  1037.5 38.5 %all-to-all-done.8.wave_ref = bf16[8,48,16,512]{3,2,1,0:T(8,128)(2,1)} async-done(((bf16[8,48,16,512]{3,2,1,0:T(8,128)(2,1)}), bf16[8,48,16,512]{3,2,1,0:T(8,128)(2,1)}, u32[]{:S(2)}, u32[]{:S(2)}) %all-to-all-start.8) | async-done | bytes 6291488 | tf_op jit(solution)/shard_map/all_to_all | solution.py:624
  1076.1 5.3 all-to-all-start.7
  1082.8 15.1 %output.4 = (bf16[1,48,768,256]{3,2,1,0:T(8,128)(2,1)}, f32[8,128]{1,0:T(8,128)S(1)}) custom-call(s32[1]{0:T(128)} %bitcast.me_ref, bf16[8,48,16,512]{3,2,1,0:T(8,128)(2,1)} %all-to-all-done.8.wave_ref, bf16[768,768]{1,0:T(8,128)(2,1)S(1)} %copy-done.16, f32[8,128]{1,0:T(8,128)S(1)} %get-tuple-element.142._, ...), custom_call_target="tpu_custom_call", output_to_operand_aliasing={{0}: (12, {})} | custom-call | flops 49999998976 | bytes 1000 | tf_op jit(solution)/shard_map/output/pallas_call | solution.py:480
  1097.9 55.0 %all-to-all-done.7.wave_ref = bf16[8,48,16,512]{3,2,1,0:T(8,128)(2,1)} async-done(((bf16[8,48,16,512]{3,2,1,0:T(8,128)(2,1)}), bf16[8,48,16,512]{3,2,1,0:T(8,128)(2,1)}, u32[]{:S(2)}, u32[]{:S(2)}) %all-to-all-start.7) | async-done | bytes 6291488 | tf_op jit(solution)/shard_map/all_to_all | solution.py:624
  1155.2 15.3 %output.5 = (bf16[1,48,768,256]{3,2,1,0:T(8,128)(2,1)}, f32[8,128]{1,0:T(8,128)}) custom-call(s32[1]{0:T(128)} %bitcast.me_ref, bf16[8,48,16,512]{3,2,1,0:T(8,128)(2,1)} %all-to-all-done.7.wave_ref, bf16[768,768]{1,0:T(8,128)(2,1)} %get-tuple-element.150.analysis_ref, f32[8,128]{1,0:T(8,128)S(1)} %get-tuple-element.144._, ...), custom_call_target="tpu_custom_call", output_to_operand_aliasing={{0}: (12, {})} | custom-call | flops 49999998976 | bytes 1000 | tf_op jit(solution)/shard_map/output/pallas_call | solution.py:480
  (157 shorter events, 30.1 us)
Async XLA Ops:
  1.9 17.4 %copy-start.1 = (bf16[512,256]{1,0:T(8,128)(2,1)S(1)}, bf16[512,256]{1,0:T(8,128)(2,1)}, u32[]{:S(2)}) copy-start(bf16[512,256]{1,0:T(8,128)(2,1)} %refs_4_.11) | copy-start | bytes 786436
  12.4 88.1 %collective-permute-start = (bf16[1,8,192,256]{3,2,1,0:T(8,128)(2,1)}, bf16[1,8,192,256]{3,2,1,0:T(8,128)(2,1)}, u32[]{:S(2)}, u32[]{:S(2)}) collective-permute-start(bf16[1,8,192,256]{3,2,1,0:T(8,128)(2,1)} %get-tuple-element.82), channel_id=1, source_target_pairs={{0,8},{8,16},{16,24},{24,0},{1,9},{9,17},{17,25},{25,1},{2,10},{10... | collective-permute-start | bytes 2359304 | tf_op jit(solution)/shard_map/ppermute | solution.py:507
  15.4 87.9 %collective-permute-start.1 = (bf16[1,8,192,256]{3,2,1,0:T(8,128)(2,1)}, bf16[1,8,192,256]{3,2,1,0:T(8,128)(2,1)}, u32[]{:S(2)}, u32[]{:S(2)}) collective-permute-start(bf16[1,8,192,256]{3,2,1,0:T(8,128)(2,1)} %get-tuple-element.83), channel_id=1, source_target_pairs={{0,16},{8,24},{16,0},{24,8},{1,17},{9,25},{17,1},{25,9},{2,18},{10... | collective-permute-start | bytes 2359304 | tf_op jit(solution)/shard_map/ppermute | solution.py:507
  18.0 86.0 %collective-permute-start.2 = (bf16[1,8,192,256]{3,2,1,0:T(8,128)(2,1)}, bf16[1,8,192,256]{3,2,1,0:T(8,128)(2,1)}, u32[]{:S(2)}, u32[]{:S(2)}) collective-permute-start(bf16[1,8,192,256]{3,2,1,0:T(8,128)(2,1)} %get-tuple-element.84), channel_id=1, source_target_pairs={{0,24},{8,0},{16,8},{24,16},{1,25},{9,1},{17,9},{25,17},{2,26},{10... | collective-permute-start | bytes 2359304 | tf_op jit(solution)/shard_map/ppermute | solution.py:507
  29.7 103.7 %collective-permute-start.3 = (bf16[1,8,192,256]{3,2,1,0:T(8,128)(2,1)}, bf16[1,8,192,256]{3,2,1,0:T(8,128)(2,1)}, u32[]{:S(2)}, u32[]{:S(2)}) collective-permute-start(bf16[1,8,192,256]{3,2,1,0:T(8,128)(2,1)} %get-tuple-element.87), channel_id=1, source_target_pairs={{0,8},{8,16},{16,24},{24,0},{1,9},{9,17},{17,25},{25,1},{2,10},{10... | collective-permute-start | bytes 2359304 | tf_op jit(solution)/shard_map/ppermute | solution.py:507
  30.4 139.9 %collective-permute-start.4 = (bf16[1,8,192,256]{3,2,1,0:T(8,128)(2,1)}, bf16[1,8,192,256]{3,2,1,0:T(8,128)(2,1)}, u32[]{:S(2)}, u32[]{:S(2)}) collective-permute-start(bf16[1,8,192,256]{3,2,1,0:T(8,128)(2,1)} %get-tuple-element.88), channel_id=1, source_target_pairs={{0,16},{8,24},{16,0},{24,8},{1,17},{9,25},{17,1},{25,9},{2,18},{10... | collective-permute-start | bytes 2359304 | tf_op jit(solution)/shard_map/ppermute | solution.py:507
  31.5 36.6 %copy-start.3 = (bf16[256,512]{1,0:T(8,128)(2,1)S(1)}, bf16[256,512]{1,0:T(8,128)(2,1)}, u32[]{:S(2)}) copy-start(bf16[256,512]{1,0:T(8,128)(2,1)} %up_ref.11) | copy-start | bytes 786436
  68.1 10.8 copy-start.46
  79.1 41.3 %copy-start.35 = (bf16[1,8,192,256]{3,2,1,0:T(8,128)(2,1)S(1)}, bf16[1,8,192,256]{3,2,1,0:T(8,128)(2,1)}, u32[]{:S(2)}) copy-start(bf16[1,8,192,256]{3,2,1,0:T(8,128)(2,1)} %copy-done.34) | copy-start | bytes 2359300
  100.5 459.2 %copy-start.17 = (bf16[768,768]{1,0:T(8,128)(2,1)}, bf16[768,768]{1,0:T(8,128)(2,1)S(1)}, u32[]{:S(2)}) copy-start(bf16[768,768]{1,0:T(8,128)(2,1)S(1)} %get-tuple-element.151.synth_ref) | copy-start | bytes 3538948
  100.5 69.8 %collective-permute-start.5 = (bf16[1,8,192,256]{3,2,1,0:T(8,128)(2,1)}, bf16[1,8,192,256]{3,2,1,0:T(8,128)(2,1)S(1)}, u32[]{:S(2)}, u32[]{:S(2)}) collective-permute-start(bf16[1,8,192,256]{3,2,1,0:T(8,128)(2,1)} %get-tuple-element.89), channel_id=1, source_target_pairs={{0,24},{8,0},{16,8},{24,16},{1,25},{9,1},{17,9},{25,17},{2,26},{10... | collective-permute-start | bytes 2359304 | tf_op jit(solution)/shard_map/ppermute | solution.py:507
  103.3 134.8 %collective-permute-start.6 = (bf16[1,8,192,256]{3,2,1,0:T(8,128)(2,1)S(1)}, bf16[1,8,192,256]{3,2,1,0:T(8,128)(2,1)S(1)}, u32[]{:S(2)}, u32[]{:S(2)}) collective-permute-start(bf16[1,8,192,256]{3,2,1,0:T(8,128)(2,1)S(1)} %get-tuple-element.92), channel_id=1, source_target_pairs={{0,8},{8,16},{16,24},{24,0},{1,9},{9,17},{17,25},{25,1},{2,10},{10... | collective-permute-start | bytes 2359304 | tf_op jit(solution)/shard_map/ppermute | solution.py:507
  103.9 134.2 %collective-permute-start.7 = (bf16[1,8,192,256]{3,2,1,0:T(8,128)(2,1)}, bf16[1,8,192,256]{3,2,1,0:T(8,128)(2,1)S(1)}, u32[]{:S(2)}, u32[]{:S(2)}) collective-permute-start(bf16[1,8,192,256]{3,2,1,0:T(8,128)(2,1)} %get-tuple-element.93), channel_id=1, source_target_pairs={{0,16},{8,24},{16,0},{24,8},{1,17},{9,25},{17,1},{25,9},{2,18},{10... | collective-permute-start | bytes 2359304 | tf_op jit(solution)/shard_map/ppermute | solution.py:507
  120.4 103.6 %copy-start.31 = (bf16[1,8,192,256]{3,2,1,0:T(8,128)(2,1)S(1)}, bf16[1,8,192,256]{3,2,1,0:T(8,128)(2,1)}, u32[]{:S(2)}) copy-start(bf16[1,8,192,256]{3,2,1,0:T(8,128)(2,1)} %copy-done.30) | copy-start | bytes 2359300
  133.5 342.0 %copy-start.22 = (bf16[2,8,192,256]{3,2,1,0:T(8,128)(2,1)}, bf16[2,8,192,256]{3,2,1,0:T(8,128)(2,1)S(1)}, u32[]{:S(2)}) copy-start(bf16[2,8,192,256]{3,2,1,0:T(8,128)(2,1)S(1)} %get-tuple-element.96.refs_0_.refs_3_) | copy-start | bytes 4718596
  133.5 124.9 %collective-permute-start.8 = (bf16[1,8,192,256]{3,2,1,0:T(8,128)(2,1)}, bf16[1,8,192,256]{3,2,1,0:T(8,128)(2,1)S(1)}, u32[]{:S(2)}, u32[]{:S(2)}) collective-permute-start(bf16[1,8,192,256]{3,2,1,0:T(8,128)(2,1)} %get-tuple-element.94), channel_id=1, source_target_pairs={{0,24},{8,0},{16,8},{24,16},{1,25},{9,1},{17,9},{25,17},{2,26},{10... | collective-permute-start | bytes 2359304 | tf_op jit(solution)/shard_map/ppermute | solution.py:507
  170.3 151.6 %collective-permute-start.10 = (bf16[2,8,192,256]{3,2,1,0:T(8,128)(2,1)}, bf16[2,8,192,256]{3,2,1,0:T(8,128)(2,1)S(1)}, u32[]{:S(2)}, u32[]{:S(2)}) collective-permute-start(bf16[2,8,192,256]{3,2,1,0:T(8,128)(2,1)} %get-tuple-element.98), channel_id=1, source_target_pairs={{0,16},{8,24},{16,0},{24,8},{1,17},{9,25},{17,1},{25,9},{2,18},{10... | collective-permute-start | bytes 4718600 | tf_op jit(solution)/shard_map/ppermute | solution.py:507
  170.3 219.0 %collective-permute-start.11 = (bf16[2,8,192,256]{3,2,1,0:T(8,128)(2,1)}, bf16[2,8,192,256]{3,2,1,0:T(8,128)(2,1)}, u32[]{:S(2)}, u32[]{:S(2)}) collective-permute-start(bf16[2,8,192,256]{3,2,1,0:T(8,128)(2,1)} %get-tuple-element.99), channel_id=1, source_target_pairs={{0,8},{8,16},{16,24},{24,0},{1,9},{9,17},{17,25},{25,1},{2,10},{10... | collective-permute-start | bytes 4718600 | tf_op jit(solution)/shard_map/ppermute | solution.py:507
  224.1 34.3 %copy-start.33 = (bf16[1,8,192,256]{3,2,1,0:T(8,128)(2,1)S(1)}, bf16[1,8,192,256]{3,2,1,0:T(8,128)(2,1)}, u32[]{:S(2)}) copy-start(bf16[1,8,192,256]{3,2,1,0:T(8,128)(2,1)} %copy-done.32) | copy-start | bytes 2359300
  238.2 153.9 %collective-permute-start.9 = (bf16[2,8,192,256]{3,2,1,0:T(8,128)(2,1)}, bf16[2,8,192,256]{3,2,1,0:T(8,128)(2,1)S(1)}, u32[]{:S(2)}, u32[]{:S(2)}) collective-permute-start(bf16[2,8,192,256]{3,2,1,0:T(8,128)(2,1)} %get-tuple-element.97), channel_id=1, source_target_pairs={{0,24},{8,0},{16,8},{24,16},{1,25},{9,1},{17,9},{25,17},{2,26},{10... | collective-permute-start | bytes 4718600 | tf_op jit(solution)/shard_map/ppermute | solution.py:507
  238.2 267.8 %collective-permute-start.12 = (bf16[2,8,192,256]{3,2,1,0:T(8,128)(2,1)}, bf16[2,8,192,256]{3,2,1,0:T(8,128)(2,1)}, u32[]{:S(2)}, u32[]{:S(2)}) collective-permute-start(bf16[2,8,192,256]{3,2,1,0:T(8,128)(2,1)} %get-tuple-element.103), channel_id=1, source_target_pairs={{0,24},{8,0},{16,8},{24,16},{1,25},{9,1},{17,9},{25,17},{2,26},{10... | collective-permute-start | bytes 4718600 | tf_op jit(solution)/shard_map/ppermute | solution.py:507
  258.4 299.6 %collective-permute-start.13 = (bf16[2,8,192,256]{3,2,1,0:T(8,128)(2,1)}, bf16[2,8,192,256]{3,2,1,0:T(8,128)(2,1)}, u32[]{:S(2)}, u32[]{:S(2)}) collective-permute-start(bf16[2,8,192,256]{3,2,1,0:T(8,128)(2,1)} %get-tuple-element.104), channel_id=1, source_target_pairs={{0,16},{8,24},{16,0},{24,8},{1,17},{9,25},{17,1},{25,9},{2,18},{10... | collective-permute-start | bytes 4718600 | tf_op jit(solution)/shard_map/ppermute | solution.py:507
  321.9 153.6 %copy-start.4 = (bf16[2,8,192,256]{3,2,1,0:T(8,128)(2,1)}, bf16[2,8,192,256]{3,2,1,0:T(8,128)(2,1)S(1)}, u32[]{:S(2)}) copy-start(bf16[2,8,192,256]{3,2,1,0:T(8,128)(2,1)S(1)} %collective-permute-done.10.refs_2_.refs_5_) | copy-start | bytes 4718596
  321.9 236.1 %collective-permute-start.14 = (bf16[2,8,192,256]{3,2,1,0:T(8,128)(2,1)}, bf16[2,8,192,256]{3,2,1,0:T(8,128)(2,1)}, u32[]{:S(2)}, u32[]{:S(2)}) collective-permute-start(bf16[2,8,192,256]{3,2,1,0:T(8,128)(2,1)} %get-tuple-element.105), channel_id=1, source_target_pairs={{0,8},{8,16},{16,24},{24,0},{1,9},{9,17},{17,25},{25,1},{2,10},{10... | collective-permute-start | bytes 4718600 | tf_op jit(solution)/shard_map/ppermute | solution.py:507
  389.3 199.5 %collective-permute-start.15 = (bf16[2,8,192,256]{3,2,1,0:T(8,128)(2,1)}, bf16[2,8,192,256]{3,2,1,0:T(8,128)(2,1)}, u32[]{:S(2)}, u32[]{:S(2)}) collective-permute-start(bf16[2,8,192,256]{3,2,1,0:T(8,128)(2,1)} %get-tuple-element.110), channel_id=1, source_target_pairs={{0,24},{8,0},{16,8},{24,16},{1,25},{9,1},{17,9},{25,17},{2,26},{10... | collective-permute-start | bytes 4718600 | tf_op jit(solution)/shard_map/ppermute | solution.py:507
  392.0 98.0 %copy-start.6 = (bf16[2,8,192,256]{3,2,1,0:T(8,128)(2,1)}, bf16[2,8,192,256]{3,2,1,0:T(8,128)(2,1)S(1)}, u32[]{:S(2)}) copy-start(bf16[2,8,192,256]{3,2,1,0:T(8,128)(2,1)S(1)} %collective-permute-done.9.refs_1_.refs_6_) | copy-start | bytes 4718596
  392.0 267.0 %collective-permute-start.16 = (bf16[2,8,192,256]{3,2,1,0:T(8,128)(2,1)}, bf16[2,8,192,256]{3,2,1,0:T(8,128)(2,1)}, u32[]{:S(2)}, u32[]{:S(2)}) collective-permute-start(bf16[2,8,192,256]{3,2,1,0:T(8,128)(2,1)} %get-tuple-element.111), channel_id=1, source_target_pairs={{0,16},{8,24},{16,0},{24,8},{1,17},{9,25},{17,1},{25,9},{2,18},{10... | collective-permute-start | bytes 4718600 | tf_op jit(solution)/shard_map/ppermute | solution.py:507
  490.1 94.2 %all-to-all-start = ((bf16[8,48,8,512]{3,2,1,0:T(8,128)(2,1)}), bf16[8,48,8,512]{3,2,1,0:T(8,128)(2,1)}, u32[]{:S(2)}, u32[]{:S(2)}) async-start(bf16[8,48,8,512]{3,2,1,0:T(8,128)(2,1)} %get-tuple-element.108), calls=%async_computation | async-start | bytes 6291456 | tf_op jit(solution)/shard_map/all_to_all | solution.py:609
  494.6 1.4 copy-start.23
  496.0 63.8 %copy-start.26 = (bf16[2,8,192,256]{3,2,1,0:T(8,128)(2,1)S(1)}, bf16[2,8,192,256]{3,2,1,0:T(8,128)(2,1)}, u32[]{:S(2)}) copy-start(bf16[2,8,192,256]{3,2,1,0:T(8,128)(2,1)} %copy-done.25) | copy-start | bytes 4718596
  505.9 153.3 %collective-permute-start.17 = (bf16[2,8,192,256]{3,2,1,0:T(8,128)(2,1)}, bf16[2,8,192,256]{3,2,1,0:T(8,128)(2,1)}, u32[]{:S(2)}, u32[]{:S(2)}) collective-permute-start(bf16[2,8,192,256]{3,2,1,0:T(8,128)(2,1)} %get-tuple-element.112), channel_id=1, source_target_pairs={{0,8},{8,16},{16,24},{24,0},{1,9},{9,17},{17,25},{25,1},{2,10},{10... | collective-permute-start | bytes 4718600 | tf_op jit(solution)/shard_map/ppermute | solution.py:507
  557.9 131.2 %collective-permute-start.18 = (bf16[1,8,192,256]{3,2,1,0:T(8,128)(2,1)}, bf16[1,8,192,256]{3,2,1,0:T(8,128)(2,1)}, u32[]{:S(2)}, u32[]{:S(2)}) collective-permute-start(bf16[1,8,192,256]{3,2,1,0:T(8,128)(2,1)} %get-tuple-element.117), channel_id=1, source_target_pairs={{0,24},{8,0},{16,8},{24,16},{1,25},{9,1},{17,9},{25,17},{2,26},{10... | collective-permute-start | bytes 2359304 | tf_op jit(solution)/shard_map/ppermute | solution.py:507
  558.0 168.5 %collective-permute-start.19 = (bf16[1,8,192,256]{3,2,1,0:T(8,128)(2,1)}, bf16[1,8,192,256]{3,2,1,0:T(8,128)(2,1)}, u32[]{:S(2)}, u32[]{:S(2)}) collective-permute-start(bf16[1,8,192,256]{3,2,1,0:T(8,128)(2,1)} %get-tuple-element.118), channel_id=1, source_target_pairs={{0,16},{8,24},{16,0},{24,8},{1,17},{9,25},{17,1},{25,9},{2,18},{10... | collective-permute-start | bytes 2359304 | tf_op jit(solution)/shard_map/ppermute | solution.py:507
  584.3 105.3 %all-to-all-start.1 = ((bf16[8,48,8,512]{3,2,1,0:T(8,128)(2,1)}), bf16[8,48,8,512]{3,2,1,0:T(8,128)(2,1)}, u32[]{:S(2)}, u32[]{:S(2)}) async-start(bf16[8,48,8,512]{3,2,1,0:T(8,128)(2,1)} %get-tuple-element.115), calls=%async_computation.1 | async-start | bytes 6291456 | tf_op jit(solution)/shard_map/all_to_all | solution.py:609
  588.7 137.8 %collective-permute-start.20 = (bf16[1,8,192,256]{3,2,1,0:T(8,128)(2,1)}, bf16[1,8,192,256]{3,2,1,0:T(8,128)(2,1)S(1)}, u32[]{:S(2)}, u32[]{:S(2)}) collective-permute-start(bf16[1,8,192,256]{3,2,1,0:T(8,128)(2,1)} %get-tuple-element.119), channel_id=1, source_target_pairs={{0,8},{8,16},{16,24},{24,0},{1,9},{9,17},{17,25},{25,1},{2,10},{10... | collective-permute-start | bytes 2359304 | tf_op jit(solution)/shard_map/ppermute | solution.py:507
  659.1 90.6 %collective-permute-start.21 = (bf16[1,8,192,256]{3,2,1,0:T(8,128)(2,1)}, bf16[1,8,192,256]{3,2,1,0:T(8,128)(2,1)}, u32[]{:S(2)}, u32[]{:S(2)}) collective-permute-start(bf16[1,8,192,256]{3,2,1,0:T(8,128)(2,1)} %get-tuple-element.123), channel_id=1, source_target_pairs={{0,24},{8,0},{16,8},{24,16},{1,25},{9,1},{17,9},{25,17},{2,26},{10... | collective-permute-start | bytes 2359304 | tf_op jit(solution)/shard_map/ppermute | solution.py:507
  659.2 134.6 %collective-permute-start.22 = (bf16[1,8,192,256]{3,2,1,0:T(8,128)(2,1)}, bf16[1,8,192,256]{3,2,1,0:T(8,128)(2,1)}, u32[]{:S(2)}, u32[]{:S(2)}) collective-permute-start(bf16[1,8,192,256]{3,2,1,0:T(8,128)(2,1)} %get-tuple-element.124), channel_id=1, source_target_pairs={{0,16},{8,24},{16,0},{24,8},{1,17},{9,25},{17,1},{25,9},{2,18},{10... | collective-permute-start | bytes 2359304 | tf_op jit(solution)/shard_map/ppermute | solution.py:507
  689.1 104.8 %collective-permute-start.23 = (bf16[1,8,192,256]{3,2,1,0:T(8,128)(2,1)}, bf16[1,8,192,256]{3,2,1,0:T(8,128)(2,1)S(1)}, u32[]{:S(2)}, u32[]{:S(2)}) collective-permute-start(bf16[1,8,192,256]{3,2,1,0:T(8,128)(2,1)} %get-tuple-element.125), channel_id=1, source_target_pairs={{0,8},{8,16},{16,24},{24,0},{1,9},{9,17},{17,25},{25,1},{2,10},{10... | collective-permute-start | bytes 2359304 | tf_op jit(solution)/shard_map/ppermute | solution.py:507
  689.5 55.6 %all-to-all-start.2 = ((bf16[8,48,8,512]{3,2,1,0:T(8,128)(2,1)}), bf16[8,48,8,512]{3,2,1,0:T(8,128)(2,1)}, u32[]{:S(2)}, u32[]{:S(2)}) async-start(bf16[8,48,8,512]{3,2,1,0:T(8,128)(2,1)} %get-tuple-element.121), calls=%async_computation.2 | async-start | bytes 6291456 | tf_op jit(solution)/shard_map/all_to_all | solution.py:609
  726.5 89.5 %collective-permute-start.24 = (bf16[1,8,192,256]{3,2,1,0:T(8,128)(2,1)}, bf16[1,8,192,256]{3,2,1,0:T(8,128)(2,1)}, u32[]{:S(2)}, u32[]{:S(2)}) collective-permute-start(bf16[1,8,192,256]{3,2,1,0:T(8,128)(2,1)} %copy-done.14), channel_id=1, source_target_pairs={{0,24},{8,0},{16,8},{24,16},{1,25},{9,1},{17,9},{25,17},{2,26},{10... | collective-permute-start | bytes 2359304 | tf_op jit(solution)/shard_map/ppermute | solution.py:507
  726.5 18.7 %copy-start.8 = (bf16[1,8,192,256]{3,2,1,0:T(8,128)(2,1)}, bf16[1,8,192,256]{3,2,1,0:T(8,128)(2,1)S(1)}, u32[]{:S(2)}) copy-start(bf16[1,8,192,256]{3,2,1,0:T(8,128)(2,1)S(1)} %collective-permute-done.20.refs_3_.refs_7_) | copy-start | bytes 2359300
  726.5 101.0 %collective-permute-start.25 = (bf16[1,8,192,256]{3,2,1,0:T(8,128)(2,1)}, bf16[1,8,192,256]{3,2,1,0:T(8,128)(2,1)}, u32[]{:S(2)}, u32[]{:S(2)}) collective-permute-start(bf16[1,8,192,256]{3,2,1,0:T(8,128)(2,1)} %copy-done.13), channel_id=1, source_target_pairs={{0,16},{8,24},{16,0},{24,8},{1,17},{9,25},{17,1},{25,9},{2,18},{10... | collective-permute-start | bytes 2359304 | tf_op jit(solution)/shard_map/ppermute | solution.py:507
  745.2 66.0 %all-to-all-start.3 = ((bf16[8,48,8,512]{3,2,1,0:T(8,128)(2,1)}), bf16[8,48,8,512]{3,2,1,0:T(8,128)(2,1)}, u32[]{:S(2)}, u32[]{:S(2)}) async-start(bf16[8,48,8,512]{3,2,1,0:T(8,128)(2,1)} %get-tuple-element.127), calls=%async_computation.3 | async-start | bytes 6291456 | tf_op jit(solution)/shard_map/all_to_all | solution.py:609
  749.6 77.9 %collective-permute-start.26 = (bf16[1,8,192,256]{3,2,1,0:T(8,128)(2,1)S(1)}, bf16[1,8,192,256]{3,2,1,0:T(8,128)(2,1)S(1)}, u32[]{:S(2)}, u32[]{:S(2)}) collective-permute-start(bf16[1,8,192,256]{3,2,1,0:T(8,128)(2,1)S(1)} %get-tuple-element.131), channel_id=1, source_target_pairs={{0,8},{8,16},{16,24},{24,0},{1,9},{9,17},{17,25},{25,1},{2,10},{10... | collective-permute-start | bytes 2359304 | tf_op jit(solution)/shard_map/ppermute | solution.py:507
  793.9 17.3 %copy-start.10 = (bf16[1,8,192,256]{3,2,1,0:T(8,128)(2,1)}, bf16[1,8,192,256]{3,2,1,0:T(8,128)(2,1)S(1)}, u32[]{:S(2)}) copy-start(bf16[1,8,192,256]{3,2,1,0:T(8,128)(2,1)S(1)} %collective-permute-done.23.refs_3_) | copy-start | bytes 2359300
  793.9 1.6 copy-start.20
  811.2 16.3 %copy-start.43 = (bf16[1,8,192,256]{3,2,1,0:T(8,128)(2,1)S(1)}, bf16[1,8,192,256]{3,2,1,0:T(8,128)(2,1)}, u32[]{:S(2)}) copy-start(bf16[1,8,192,256]{3,2,1,0:T(8,128)(2,1)} %copy-done.42) | copy-start | bytes 2359300
  811.2 42.7 %all-to-all-start.4 = ((bf16[8,48,8,512]{3,2,1,0:T(8,128)(2,1)}), bf16[8,48,8,512]{3,2,1,0:T(8,128)(2,1)}, u32[]{:S(2)}, u32[]{:S(2)}) async-start(bf16[8,48,8,512]{3,2,1,0:T(8,128)(2,1)} %get-tuple-element.133), calls=%async_computation.4 | async-start | bytes 6291456 | tf_op jit(solution)/shard_map/all_to_all | solution.py:609
  827.5 16.1 %copy-start.12 = (bf16[1,8,192,256]{3,2,1,0:T(8,128)(2,1)}, bf16[1,8,192,256]{3,2,1,0:T(8,128)(2,1)S(1)}, u32[]{:S(2)}) copy-start(bf16[1,8,192,256]{3,2,1,0:T(8,128)(2,1)S(1)} %collective-permute-done.26.refs_3_.refs_7_) | copy-start | bytes 2359300
  827.5 1.6 copy-start.21
  853.9 4.6 copy-start.48
  853.9 41.6 %all-to-all-start.5 = ((bf16[8,48,8,512]{3,2,1,0:T(8,128)(2,1)}), bf16[8,48,8,512]{3,2,1,0:T(8,128)(2,1)S(1)}, u32[]{:S(2)}, u32[]{:S(2)}) async-start(bf16[8,48,8,512]{3,2,1,0:T(8,128)(2,1)} %after.1), calls=%async_computation.5 | async-start | bytes 6291456 | tf_op jit(solution)/shard_map/all_to_all | solution.py:609
  895.5 1.6 copy-start.45
  922.9 4.9 copy-start.47
  922.9 76.5 %all-to-all-start.6 = ((bf16[8,48,16,512]{3,2,1,0:T(8,128)(2,1)}), bf16[8,48,16,512]{3,2,1,0:T(8,128)(2,1)}, u32[]{:S(2)}, u32[]{:S(2)}) async-start(bf16[8,48,16,512]{3,2,1,0:T(8,128)(2,1)} %get-tuple-element.136), calls=%async_computation.6 | async-start | bytes 12582912 | tf_op jit(solution)/shard_map/all_to_all | solution.py:620
  999.4 5.0 copy-start.5
  999.4 5.1 copy-start.7
  999.4 76.6 %all-to-all-start.8 = ((bf16[8,48,16,512]{3,2,1,0:T(8,128)(2,1)}), bf16[8,48,16,512]{3,2,1,0:T(8,128)(2,1)}, u32[]{:S(2)}, u32[]{:S(2)}) async-start(bf16[8,48,16,512]{3,2,1,0:T(8,128)(2,1)} %get-tuple-element.141), calls=%async_computation.8 | async-start | bytes 12582912 | tf_op jit(solution)/shard_map/all_to_all | solution.py:624
  1076.1 5.3 copy-start.9
  1076.1 5.3 copy-start.16
  1076.1 5.3 copy-start.38
  1076.1 76.9 %all-to-all-start.7 = ((bf16[8,48,16,512]{3,2,1,0:T(8,128)(2,1)}), bf16[8,48,16,512]{3,2,1,0:T(8,128)(2,1)}, u32[]{:S(2)}, u32[]{:S(2)}) async-start(bf16[8,48,16,512]{3,2,1,0:T(8,128)(2,1)} %get-tuple-element.140), calls=%async_computation.7 | async-start | bytes 12582912 | tf_op jit(solution)/shard_map/all_to_all | solution.py:624
  1081.4 1.4 copy-start.29
  1082.8 70.2 %copy-start.11 = (bf16[1,8,192,256]{3,2,1,0:T(8,128)(2,1)S(1)}, bf16[1,8,192,256]{3,2,1,0:T(8,128)(2,1)}, u32[]{:S(2)}) copy-start(bf16[1,8,192,256]{3,2,1,0:T(8,128)(2,1)} %copy-done.10) | copy-start | bytes 2359300
  (21 other events, 22.5 us)

commit v5 on v4

--- a/solution.py
+++ b/solution.py
@@ -181,7 +181,7 @@
 def exchange_kernel(members, forward, cotangent, me_ref, *refs):
     refs = list(refs)
     take = lambda count: [refs.pop(0) for _ in range(count)]
-    refs.pop(0)
+    take(2)
     forward_refs = take(4) if forward is not None else None
     if cotangent is not None:
         target_ref, weight_ref = take(2)
@@ -201,12 +201,12 @@
 
 
 def exchange_rows(
-    token, rows, members, me, forward, cotangent, saved, grid_input, up_weight, down_weight, target, weights, values
+    token, ahead, rows, members, me, forward, cotangent, saved, grid_input, up_weight, down_weight, target, weights, values
 ):
     _, lon, channels = saved.shape
     hidden = up_weight.shape[1]
     share = lon // members
-    in_specs, operands = [TOKEN_IN], [me, token]
+    in_specs, operands = [TOKEN_IN, TOKEN_IN], [me, token, ahead]
     if forward is not None:
         row_spec = pl.BlockSpec((1, lon, channels), lambda i, q: (forward + i, 0, 0))
         in_specs += [
@@ -529,6 +529,9 @@
     for part in range(parts):
         place = order.index(("exchange", min(part + 2, parts - 1))) + 1
         order.insert(place if part + 2 < parts else len(order), ("backward", part))
+    if parts > 2:
+        order.remove(("exchange", parts - 1))
+        order.insert(order.index(("backward", parts - 3)) + 1, ("exchange", parts - 1))
     return order
 
 
@@ -573,6 +576,7 @@
             cotangent = part if part >= 0 else None
             *pieces, token = exchange_rows(
                 token,
+                waves.get(part - 3, token) if part == parts - 1 else token,
                 rows,
                 members,
                 me,

time: 1180 us -> 1170 us (level)
    unnamed x102 -> x100, local copies, waits for them, and re-layouts: 31.6 us -> 26.5 us
  transfers between devices with their start and end apart: 36 -> 36, of which waited for: 12 -> 11; matrix products, arithmetic and copies ran while one was open for 2% -> 2% of each run, Pallas kernels for 23% -> 23%
where the time goes in v5:
time: 1170 us; the launch traced here: 1160 us
  waiting for transfers between devices  442 us (38%)
  starting transfers between devices  348 us (30%)
  Pallas kernels  322 us (28%)
  local copies, waits for them, and re-layouts  27.6 us (2%)
  other arithmetic  22.1 us (2%)
    ppermute x27, starting transfers between devices, shift(): moved.append(lax.ppermute(pieces[piece], 'member', pairs))  306 us
    ppermute x27, waiting for transfers between devices, shift(): moved.append(lax.ppermute(pieces[piece], 'member', pairs))  251 us
    pallas_call x9, Pallas kernels, exchange_rows(): pl.pallas_call(functools.partial(exchange_kernel, members, forward, cotan...  94.6 us
    all_to_all x2, waiting for transfers between devices, shards(): lat_waves[step] = lax.all_to_all(wave, 'lat', 0, 0, tiled=True)  92.2 us
    pallas_call x6, Pallas kernels, backward_rows(): pl.pallas_call(backward_kernel, grid_spec=pltpu.PrefetchScalarGridSpec(nu...  88.1 us
    all_to_all x1, waiting for transfers between devices, shards(): lat_waves = {0: lax.all_to_all(wave, 'lat', 0, 0, tiled=True)}  55.8 us
    pallas_call x3, Pallas kernels, output_rows(): pl.pallas_call(functools.partial(output_kernel, joined, members, 1.0 / lo...  45.4 us
    all_to_all x6, waiting for transfers between devices, shards(): waves[part] = lax.all_to_all(wave, 'lat', 0, 0, tiled=True)  43.6 us
  transfers between devices with their start and end apart: 36, of which 11 were waited for; matrix products, arithmetic and copies ran while one was open for 2% of the time, Pallas kernels for 23%

profile of v5, /device:TPU:0, one launch (start us, length us, event | category | flops | bytes accessed | tf_op | source)
XLA Modules:
  0.0 1162.4 jit_solution(8972639083220365867)
XLA Ops:
  1.9 9.6 exchange.9
  11.5 3.0 collective-permute-start
  14.5 2.6 collective-permute-start.1
  18.5 9.5 exchange.10
  30.7 36.6 %legendre.1 = (bf16[48,384,384]{2,1,0:T(8,128)(2,1)}, f32[8,128]{1,0:T(8,128)S(1)}) custom-call(f32[48,384]{1,0:T(8,128)S(1)} %multiply_add_fusion.start_ref, f32[1,384]{1,0:T(1,128)S(1)} %reshape.204.cosine_ref, f32[48,1]{1,0:T(8,128)S(1)} %add_convert_fusion.order_ref, f32[8,128]{1,0:T(8,128)S(1)} %get-tuple-element.77._), custom_call_target="tpu_custom_call" | custom-call | flops 49999998976 | bytes 1000 | tf_op jit(solution)/shard_map/legendre/pallas_call | solution.py:108
  67.3 9.6 exchange.11
  78.3 21.4 %select_convert_fusion = (bf16[768,768]{1,0:T(8,128)(2,1)}, bf16[768,768]{1,0:T(8,128)(2,1)S(1)}) fusion(s32[768]{0:T(1024)S(1)} %fusion.14, pred[768]{0:T(1024)(128)(4,1)S(1)} %fusion.20, f32[768]{0:T(1024)S(1)} %compare_select_fusion), kind=kLoop, calls=%fused_computation.6 | loop fusion | flops 14745600 | bytes 2366208 | tf_op jit(solution)/shard_map/convert_element_type | solution.py:54
  99.6 2.8 collective-permute-start.5
  103.1 16.5 %collective-permute-start.7 = (bf16[1,8,192,256]{3,2,1,0:T(8,128)(2,1)}, bf16[1,8,192,256]{3,2,1,0:T(8,128)(2,1)S(1)}, u32[]{:S(2)}, u32[]{:S(2)}) collective-permute-start(bf16[1,8,192,256]{3,2,1,0:T(8,128)(2,1)} %get-tuple-element.93), channel_id=1, source_target_pairs={{0,16},{8,24},{16,0},{24,8},{1,17},{9,25},{17,1},{25,9},{2,18},{10... | collective-permute-start | bytes 2359304 | tf_op jit(solution)/shard_map/ppermute | solution.py:507
  119.6 13.0 %exchange.12 = (bf16[2,8,192,256]{3,2,1,0:T(8,128)(2,1)S(1)}, bf16[2,8,192,256]{3,2,1,0:T(8,128)(2,1)}, bf16[2,8,192,256]{3,2,1,0:T(8,128)(2,1)}, bf16[2,8,192,256]{3,2,1,0:T(8,128)(2,1)}, f32[8,128]{1,0:T(8,128)S(1)}) custom-call(s32[1]{0:T(128)} %bitcast.me_ref, f32[8,128]{1,0:T(8,128)S(1)} %get-tuple-element.80.refs_0_.refs_1_, ...), custom_call_target="tpu_custom_call" | custom-call | flops 49999998976 | bytes 1000 | tf_op jit(solution)/shard_map/exchange/pallas_call | solution.py:228
  132.6 3.8 collective-permute-start.8
  136.4 33.0 %collective-permute-done.4.refs_10_ = bf16[1,8,192,256]{3,2,1,0:T(8,128)(2,1)} collective-permute-done((bf16[1,8,192,256]{3,2,1,0:T(8,128)(2,1)}, bf16[1,8,192,256]{3,2,1,0:T(8,128)(2,1)}, u32[]{:S(2)}, u32[]{:S(2)}) %collective-permute-start.4) | collective-permute-done | bytes 786464 | tf_op jit(solution)/shard_map/ppermute | solution.py:507
  169.4 53.8 %collective-permute-start.11 = (bf16[2,8,192,256]{3,2,1,0:T(8,128)(2,1)}, bf16[2,8,192,256]{3,2,1,0:T(8,128)(2,1)S(1)}, u32[]{:S(2)}, u32[]{:S(2)}) collective-permute-start(bf16[2,8,192,256]{3,2,1,0:T(8,128)(2,1)} %get-tuple-element.99), channel_id=1, source_target_pairs={{0,8},{8,16},{16,24},{24,0},{1,9},{9,17},{17,25},{25,1},{2,10},{10... | collective-permute-start | bytes 4718600 | tf_op jit(solution)/shard_map/ppermute | solution.py:507
  223.2 12.9 %exchange.13 = (bf16[2,8,192,256]{3,2,1,0:T(8,128)(2,1)S(1)}, bf16[2,8,192,256]{3,2,1,0:T(8,128)(2,1)}, bf16[2,8,192,256]{3,2,1,0:T(8,128)(2,1)}, bf16[2,8,192,256]{3,2,1,0:T(8,128)(2,1)}, f32[8,128]{1,0:T(8,128)S(1)}) custom-call(s32[1]{0:T(128)} %bitcast.me_ref, f32[8,128]{1,0:T(8,128)S(1)} %get-tuple-element.85.refs_0_.refs_1_, ...), custom_call_target="tpu_custom_call" | custom-call | flops 49999998976 | bytes 1000 | tf_op jit(solution)/shard_map/exchange/pallas_call | solution.py:228
  237.3 20.2 %collective-permute-start.12 = (bf16[2,8,192,256]{3,2,1,0:T(8,128)(2,1)}, bf16[2,8,192,256]{3,2,1,0:T(8,128)(2,1)}, u32[]{:S(2)}, u32[]{:S(2)}) collective-permute-start(bf16[2,8,192,256]{3,2,1,0:T(8,128)(2,1)} %get-tuple-element.103), channel_id=1, source_target_pairs={{0,24},{8,0},{16,8},{24,16},{1,25},{9,1},{17,9},{25,17},{2,26},{10... | collective-permute-start | bytes 4718600 | tf_op jit(solution)/shard_map/ppermute | solution.py:507
  257.5 12.7 %exchange.14 = (bf16[2,8,192,256]{3,2,1,0:T(8,128)(2,1)S(1)}, bf16[2,8,192,256]{3,2,1,0:T(8,128)(2,1)}, bf16[2,8,192,256]{3,2,1,0:T(8,128)(2,1)}, bf16[2,8,192,256]{3,2,1,0:T(8,128)(2,1)}, f32[8,128]{1,0:T(8,128)S(1)}) custom-call(s32[1]{0:T(128)} %bitcast.me_ref, f32[8,128]{1,0:T(8,128)S(1)} %get-tuple-element.90.refs_0_.refs_1_, ...), custom_call_target="tpu_custom_call" | custom-call | flops 49999998976 | bytes 1000 | tf_op jit(solution)/shard_map/exchange/pallas_call | solution.py:228
  271.3 49.7 %collective-permute-done.10.refs_2_.refs_6_ = bf16[2,8,192,256]{3,2,1,0:T(8,128)(2,1)S(1)} collective-permute-done((bf16[2,8,192,256]{3,2,1,0:T(8,128)(2,1)}, bf16[2,8,192,256]{3,2,1,0:T(8,128)(2,1)S(1)}, u32[]{:S(2)}, u32[]{:S(2)}) %collective-permute-start.10) | collective-permute-done | bytes 1572896 | tf_op jit(solution)/shard_map/ppermute | solution.py:507
  321.0 67.3 %collective-permute-start.14 = (bf16[2,8,192,256]{3,2,1,0:T(8,128)(2,1)}, bf16[2,8,192,256]{3,2,1,0:T(8,128)(2,1)}, u32[]{:S(2)}, u32[]{:S(2)}) collective-permute-start(bf16[2,8,192,256]{3,2,1,0:T(8,128)(2,1)} %get-tuple-element.105), channel_id=1, source_target_pairs={{0,8},{8,16},{16,24},{24,0},{1,9},{9,17},{17,25},{25,1},{2,10},{10... | collective-permute-start | bytes 4718600 | tf_op jit(solution)/shard_map/ppermute | solution.py:507
  388.4 2.8 collective-permute-start.15
  391.2 83.4 %collective-permute-start.16 = (bf16[2,8,192,256]{3,2,1,0:T(8,128)(2,1)}, bf16[2,8,192,256]{3,2,1,0:T(8,128)(2,1)}, u32[]{:S(2)}, u32[]{:S(2)}) collective-permute-start(bf16[2,8,192,256]{3,2,1,0:T(8,128)(2,1)} %get-tuple-element.111), channel_id=1, source_target_pairs={{0,16},{8,24},{16,0},{24,8},{1,17},{9,25},{17,1},{25,9},{2,18},{10... | collective-permute-start | bytes 4718600 | tf_op jit(solution)/shard_map/ppermute | solution.py:507
  474.6 14.7 %backward.6 = (bf16[8,48,8,512]{3,2,1,0:T(8,128)(2,1)}, f32[8,128]{1,0:T(8,128)S(1)}) custom-call(s32[1]{0:T(128)} %bitcast.me_ref, bf16[48,768,256]{2,1,0:T(8,128)(2,1)} %bitcast.33, bf16[256,512]{1,0:T(8,128)(2,1)S(1)} %copy-done.3, bf16[256,512]{1,0:T(8,128)(2,1)S(1)} %bitcast.8, bf16[512,256]{1,0:T(8,128)(2,1)S(1)} %bitcast.14, ...), custom_call_target="tpu_custom_call" | custom-call | flops 49999998976 | bytes 1000 | tf_op jit(solution)/shard_map/backward/pallas_call | solution.py:294
  489.2 4.5 all-to-all-start
  493.7 1.4 copy-done.22
  495.1 9.1 exchange.15
  504.3 2.0 collective-permute-start.17
  506.3 50.8 %collective-permute-done.13.refs_2_.refs_6_ = bf16[2,8,192,256]{3,2,1,0:T(8,128)(2,1)} collective-permute-done((bf16[2,8,192,256]{3,2,1,0:T(8,128)(2,1)}, bf16[2,8,192,256]{3,2,1,0:T(8,128)(2,1)}, u32[]{:S(2)}, u32[]{:S(2)}) %collective-permute-start.13) | collective-permute-done | bytes 1572896 | tf_op jit(solution)/shard_map/ppermute | solution.py:507
  557.1 1.8 collective-permute-start.19
  558.9 14.7 %backward.7 = (bf16[8,48,8,512]{3,2,1,0:T(8,128)(2,1)}, f32[8,128]{1,0:T(8,128)S(1)}) custom-call(s32[1]{0:T(128)} %bitcast.me_ref, bf16[48,768,256]{2,1,0:T(8,128)(2,1)} %bitcast.34, bf16[256,512]{1,0:T(8,128)(2,1)S(1)} %copy-done.3, bf16[256,512]{1,0:T(8,128)(2,1)S(1)} %bitcast.9, bf16[512,256]{1,0:T(8,128)(2,1)S(1)} %bitcast.15, ...), custom_call_target="tpu_custom_call" | custom-call | flops 49999998976 | bytes 1000 | tf_op jit(solution)/shard_map/backward/pallas_call | solution.py:294
  573.5 9.0 exchange.16
  583.4 4.5 all-to-all-start.1
  587.9 37.2 %collective-permute-start.20 = (bf16[1,8,192,256]{3,2,1,0:T(8,128)(2,1)}, bf16[1,8,192,256]{3,2,1,0:T(8,128)(2,1)S(1)}, u32[]{:S(2)}, u32[]{:S(2)}) collective-permute-start(bf16[1,8,192,256]{3,2,1,0:T(8,128)(2,1)} %get-tuple-element.118), channel_id=1, source_target_pairs={{0,8},{8,16},{16,24},{24,0},{1,9},{9,17},{17,25},{25,1},{2,10},{10... | collective-permute-start | bytes 2359304 | tf_op jit(solution)/shard_map/ppermute | solution.py:507
  625.1 33.1 %collective-permute-done.16.refs_2_.refs_6_ = bf16[2,8,192,256]{3,2,1,0:T(8,128)(2,1)} collective-permute-done((bf16[2,8,192,256]{3,2,1,0:T(8,128)(2,1)}, bf16[2,8,192,256]{3,2,1,0:T(8,128)(2,1)}, u32[]{:S(2)}, u32[]{:S(2)}) %collective-permute-start.16) | collective-permute-done | bytes 1572896 | tf_op jit(solution)/shard_map/ppermute | solution.py:507
  658.4 1.6 collective-permute-start.22
  660.0 1.4 copy-done.27
  661.4 14.7 %backward.8 = (bf16[8,48,8,512]{3,2,1,0:T(8,128)(2,1)}, f32[8,128]{1,0:T(8,128)S(1)}) custom-call(s32[1]{0:T(128)} %bitcast.me_ref, bf16[48,768,256]{2,1,0:T(8,128)(2,1)} %bitcast.35, bf16[256,512]{1,0:T(8,128)(2,1)S(1)} %copy-done.3, bf16[256,512]{1,0:T(8,128)(2,1)S(1)} %bitcast.10, bf16[512,256]{1,0:T(8,128)(2,1)S(1)} %bitcast.16, ...), custom_call_target="tpu_custom_call" | custom-call | flops 49999998976 | bytes 1000 | tf_op jit(solution)/shard_map/backward/pallas_call | solution.py:294
  676.5 4.4 all-to-all-start.2
  680.9 44.7 %collective-permute-done.19.refs_2_.refs_6_ = bf16[1,8,192,256]{3,2,1,0:T(8,128)(2,1)} collective-permute-done((bf16[1,8,192,256]{3,2,1,0:T(8,128)(2,1)}, bf16[1,8,192,256]{3,2,1,0:T(8,128)(2,1)}, u32[]{:S(2)}, u32[]{:S(2)}) %collective-permute-start.19) | collective-permute-done | bytes 786464 | tf_op jit(solution)/shard_map/ppermute | solution.py:507
  725.6 1.6 copy-done.18
  728.3 14.6 %backward.9 = (bf16[8,48,8,512]{3,2,1,0:T(8,128)(2,1)}, f32[8,128]{1,0:T(8,128)S(1)}) custom-call(s32[1]{0:T(128)} %bitcast.me_ref, bf16[48,768,256]{2,1,0:T(8,128)(2,1)} %bitcast.36, bf16[256,512]{1,0:T(8,128)(2,1)S(1)} %copy-done.3, bf16[256,512]{1,0:T(8,128)(2,1)S(1)} %bitcast.11, bf16[512,256]{1,0:T(8,128)(2,1)S(1)} %bitcast.17, ...), custom_call_target="tpu_custom_call" | custom-call | flops 49999998976 | bytes 1000 | tf_op jit(solution)/shard_map/backward/pallas_call | solution.py:294
  742.9 4.5 all-to-all-start.3
  748.8 9.1 exchange.17
  758.9 1.7 collective-permute-start.25
  760.7 2.0 collective-permute-start.26
  762.7 14.9 %backward.10 = (bf16[8,48,8,512]{3,2,1,0:T(8,128)(2,1)}, f32[8,128]{1,0:T(8,128)S(1)}) custom-call(s32[1]{0:T(128)} %bitcast.me_ref, bf16[48,768,256]{2,1,0:T(8,128)(2,1)} %bitcast.37, bf16[256,512]{1,0:T(8,128)(2,1)S(1)} %copy-done.3, bf16[256,512]{1,0:T(8,128)(2,1)S(1)} %bitcast.12, bf16[512,256]{1,0:T(8,128)(2,1)S(1)} %bitcast.18, ...), custom_call_target="tpu_custom_call" | custom-call | flops 49999998976 | bytes 1000 | tf_op jit(solution)/shard_map/backward/pallas_call | solution.py:294
  777.6 7.7 all-to-all-done.3.__.refs_3_
  785.3 4.8 all-to-all-start.4
  790.1 39.5 %collective-permute-done.25.refs_2_.refs_6_ = bf16[1,8,192,256]{3,2,1,0:T(8,128)(2,1)} collective-permute-done((bf16[1,8,192,256]{3,2,1,0:T(8,128)(2,1)}, bf16[1,8,192,256]{3,2,1,0:T(8,128)(2,1)}, u32[]{:S(2)}, u32[]{:S(2)}) %collective-permute-start.25) | collective-permute-done | bytes 786464 | tf_op jit(solution)/shard_map/ppermute | solution.py:507
  830.7 14.6 %backward.11 = (bf16[8,48,8,512]{3,2,1,0:T(8,128)(2,1)}, f32[8,128]{1,0:T(8,128)S(1)}) custom-call(s32[1]{0:T(128)} %bitcast.me_ref, bf16[48,768,256]{2,1,0:T(8,128)(2,1)} %bitcast.38, bf16[256,512]{1,0:T(8,128)(2,1)S(1)} %copy-done.3, bf16[256,512]{1,0:T(8,128)(2,1)S(1)} %bitcast.13, bf16[512,256]{1,0:T(8,128)(2,1)S(1)} %bitcast.19, ...), custom_call_target="tpu_custom_call" | custom-call | flops 49999998976 | bytes 1000 | tf_op jit(solution)/shard_map/backward/pallas_call | solution.py:294
  845.3 3.9 all-to-all-start.5
  851.1 36.0 %all-to-all-done.5.refs_5_ = bf16[8,48,8,512]{3,2,1,0:T(8,128)(2,1)S(1)} async-done(((bf16[8,48,8,512]{3,2,1,0:T(8,128)(2,1)}), bf16[8,48,8,512]{3,2,1,0:T(8,128)(2,1)S(1)}, u32[]{:S(2)}, u32[]{:S(2)}) %all-to-all-start.5) | async-done | bytes 3145760 | tf_op jit(solution)/shard_map/all_to_all | solution.py:613
  887.1 1.6 copy-done.43
  888.7 25.8 %spectral.1 = (bf16[48,384,512]{2,1,0:T(8,128)(2,1)}, bf16[8,48,16,512]{3,2,1,0:T(8,128)(2,1)}, f32[8,128]{1,0:T(8,128)S(1)}) custom-call(bf16[48,384,384]{2,1,0:T(8,128)(2,1)} %get-tuple-element.78.table_ref, f32[384,1]{1,0:T(8,128)S(1)} %broadcast_in_dim.70.gain_ref, bf16[256,256]{1,0:T(8,128)(2,1)S(1)} %bitcast.20, f32[128,1]{1,0:T(8,128)S(1)} %slice.28.quad_ref, ...), custom_call_target="tpu_custom_call" | custom-call | flops 49999998976 | bytes 1000 | tf_op jit(solution)/shard_map/spectral/pallas_call | solution.py:361
  914.5 4.9 all-to-all-start.6
  919.6 15.6 %latitude.2 = (bf16[8,48,16,512]{3,2,1,0:T(8,128)(2,1)}, f32[8,128]{1,0:T(8,128)S(1)}) custom-call(bf16[48,384,384]{2,1,0:T(8,128)(2,1)} %get-tuple-element.78.table_ref, f32[128,1]{1,0:T(8,128)S(1)} %slice.29.quad_ref, bf16[48,384,512]{2,1,0:T(8,128)(2,1)} %get-tuple-element.135.coeff_ref, f32[8,128]{1,0:T(8,128)S(1)} %get-tuple-element.137._), custom_call_target="tpu_custom_call" | custom-call | flops 49999998976 | bytes 1000 | tf_op jit(solution)/shard_map/latitude/pallas_call | solution.py:399
  935.2 55.8 %all-to-all-done.6.wave_ref = bf16[8,48,16,512]{3,2,1,0:T(8,128)(2,1)} async-done(((bf16[8,48,16,512]{3,2,1,0:T(8,128)(2,1)}), bf16[8,48,16,512]{3,2,1,0:T(8,128)(2,1)}, u32[]{:S(2)}, u32[]{:S(2)}) %all-to-all-start.6) | async-done | bytes 6291488 | tf_op jit(solution)/shard_map/all_to_all | solution.py:624
  991.0 5.0 all-to-all-start.8
  997.4 1.4 copy-done.23
  998.8 14.9 %output.3 = (bf16[1,48,768,256]{3,2,1,0:T(8,128)(2,1)}, f32[8,128]{1,0:T(8,128)S(1)}) custom-call(s32[1]{0:T(128)} %bitcast.me_ref, bf16[8,48,16,512]{3,2,1,0:T(8,128)(2,1)} %all-to-all-done.6.wave_ref, bf16[768,768]{1,0:T(8,128)(2,1)S(1)} %copy-done.14, f32[8,128]{1,0:T(8,128)S(1)} %get-tuple-element.138._, bf16[2,8,192,256]{3,2,1,0:T(8,128)(2,1)S(1)} %copy-done.23, ...), custom_call_target="tpu_custom_call" | custom-call | flops 49999998976 | bytes 1000 | tf_op jit(solution)/shard_map/output/pallas_call | solution.py:480
  1013.7 15.6 %latitude.3 = (bf16[8,48,16,512]{3,2,1,0:T(8,128)(2,1)}, f32[8,128]{1,0:T(8,128)S(1)}) custom-call(bf16[48,384,384]{2,1,0:T(8,128)(2,1)} %get-tuple-element.78.table_ref, f32[128,1]{1,0:T(8,128)S(1)} %slice.27.quad_ref, bf16[48,384,512]{2,1,0:T(8,128)(2,1)} %get-tuple-element.135.coeff_ref, f32[8,128]{1,0:T(8,128)S(1)} %get-tuple-element.139._), custom_call_target="tpu_custom_call" | custom-call | flops 49999998976 | bytes 1000 | tf_op jit(solution)/shard_map/latitude/pallas_call | solution.py:399
  1029.3 38.4 %all-to-all-done.8.wave_ref = bf16[8,48,16,512]{3,2,1,0:T(8,128)(2,1)} async-done(((bf16[8,48,16,512]{3,2,1,0:T(8,128)(2,1)}), bf16[8,48,16,512]{3,2,1,0:T(8,128)(2,1)}, u32[]{:S(2)}, u32[]{:S(2)}) %all-to-all-start.8) | async-done | bytes 6291488 | tf_op jit(solution)/shard_map/all_to_all | solution.py:628
  1067.7 5.1 all-to-all-start.7
  1075.4 15.3 %output.4 = (bf16[1,48,768,256]{3,2,1,0:T(8,128)(2,1)}, f32[8,128]{1,0:T(8,128)S(1)}) custom-call(s32[1]{0:T(128)} %bitcast.me_ref, bf16[8,48,16,512]{3,2,1,0:T(8,128)(2,1)} %all-to-all-done.8.wave_ref, bf16[768,768]{1,0:T(8,128)(2,1)S(1)} %copy-done.15, f32[8,128]{1,0:T(8,128)S(1)} %get-tuple-element.142._, ...), custom_call_target="tpu_custom_call", output_to_operand_aliasing={{0}: (12, {})} | custom-call | flops 49999998976 | bytes 1000 | tf_op jit(solution)/shard_map/output/pallas_call | solution.py:480
  1090.7 53.8 %all-to-all-done.7.wave_ref = bf16[8,48,16,512]{3,2,1,0:T(8,128)(2,1)} async-done(((bf16[8,48,16,512]{3,2,1,0:T(8,128)(2,1)}), bf16[8,48,16,512]{3,2,1,0:T(8,128)(2,1)}, u32[]{:S(2)}, u32[]{:S(2)}) %all-to-all-start.7) | async-done | bytes 6291488 | tf_op jit(solution)/shard_map/all_to_all | solution.py:628
  1146.7 15.2 %output.5 = (bf16[1,48,768,256]{3,2,1,0:T(8,128)(2,1)}, f32[8,128]{1,0:T(8,128)}) custom-call(s32[1]{0:T(128)} %bitcast.me_ref, bf16[8,48,16,512]{3,2,1,0:T(8,128)(2,1)} %all-to-all-done.7.wave_ref, bf16[768,768]{1,0:T(8,128)(2,1)} %get-tuple-element.150.analysis_ref, f32[8,128]{1,0:T(8,128)S(1)} %get-tuple-element.144._, ...), custom_call_target="tpu_custom_call", output_to_operand_aliasing={{0}: (12, {})} | custom-call | flops 49999998976 | bytes 1000 | tf_op jit(solution)/shard_map/output/pallas_call | solution.py:480
  (155 shorter events, 24.6 us)
Async XLA Ops:
  1.9 16.6 %copy-start.1 = (bf16[512,256]{1,0:T(8,128)(2,1)S(1)}, bf16[512,256]{1,0:T(8,128)(2,1)}, u32[]{:S(2)}) copy-start(bf16[512,256]{1,0:T(8,128)(2,1)} %refs_5_.11) | copy-start | bytes 786436
  11.5 88.1 %collective-permute-start = (bf16[1,8,192,256]{3,2,1,0:T(8,128)(2,1)}, bf16[1,8,192,256]{3,2,1,0:T(8,128)(2,1)}, u32[]{:S(2)}, u32[]{:S(2)}) collective-permute-start(bf16[1,8,192,256]{3,2,1,0:T(8,128)(2,1)} %get-tuple-element.82), channel_id=1, source_target_pairs={{0,8},{8,16},{16,24},{24,0},{1,9},{9,17},{17,25},{25,1},{2,10},{10... | collective-permute-start | bytes 2359304 | tf_op jit(solution)/shard_map/ppermute | solution.py:507
  14.5 87.9 %collective-permute-start.1 = (bf16[1,8,192,256]{3,2,1,0:T(8,128)(2,1)}, bf16[1,8,192,256]{3,2,1,0:T(8,128)(2,1)}, u32[]{:S(2)}, u32[]{:S(2)}) collective-permute-start(bf16[1,8,192,256]{3,2,1,0:T(8,128)(2,1)} %get-tuple-element.83), channel_id=1, source_target_pairs={{0,16},{8,24},{16,0},{24,8},{1,17},{9,25},{17,1},{25,9},{2,18},{10... | collective-permute-start | bytes 2359304 | tf_op jit(solution)/shard_map/ppermute | solution.py:507
  17.1 86.0 %collective-permute-start.2 = (bf16[1,8,192,256]{3,2,1,0:T(8,128)(2,1)}, bf16[1,8,192,256]{3,2,1,0:T(8,128)(2,1)}, u32[]{:S(2)}, u32[]{:S(2)}) collective-permute-start(bf16[1,8,192,256]{3,2,1,0:T(8,128)(2,1)} %get-tuple-element.84), channel_id=1, source_target_pairs={{0,24},{8,0},{16,8},{24,16},{1,25},{9,1},{17,9},{25,17},{2,26},{10... | collective-permute-start | bytes 2359304 | tf_op jit(solution)/shard_map/ppermute | solution.py:507
  28.9 103.7 %collective-permute-start.3 = (bf16[1,8,192,256]{3,2,1,0:T(8,128)(2,1)}, bf16[1,8,192,256]{3,2,1,0:T(8,128)(2,1)}, u32[]{:S(2)}, u32[]{:S(2)}) collective-permute-start(bf16[1,8,192,256]{3,2,1,0:T(8,128)(2,1)} %get-tuple-element.87), channel_id=1, source_target_pairs={{0,8},{8,16},{16,24},{24,0},{1,9},{9,17},{17,25},{25,1},{2,10},{10... | collective-permute-start | bytes 2359304 | tf_op jit(solution)/shard_map/ppermute | solution.py:507
  29.6 139.9 %collective-permute-start.4 = (bf16[1,8,192,256]{3,2,1,0:T(8,128)(2,1)}, bf16[1,8,192,256]{3,2,1,0:T(8,128)(2,1)}, u32[]{:S(2)}, u32[]{:S(2)}) collective-permute-start(bf16[1,8,192,256]{3,2,1,0:T(8,128)(2,1)} %get-tuple-element.88), channel_id=1, source_target_pairs={{0,16},{8,24},{16,0},{24,8},{1,17},{9,25},{17,1},{25,9},{2,18},{10... | collective-permute-start | bytes 2359304 | tf_op jit(solution)/shard_map/ppermute | solution.py:507
  30.7 36.6 %copy-start.3 = (bf16[256,512]{1,0:T(8,128)(2,1)S(1)}, bf16[256,512]{1,0:T(8,128)(2,1)}, u32[]{:S(2)}) copy-start(bf16[256,512]{1,0:T(8,128)(2,1)} %up_ref.11) | copy-start | bytes 786436
  67.3 10.8 copy-start.44
  99.6 374.9 %copy-start.16 = (bf16[768,768]{1,0:T(8,128)(2,1)}, bf16[768,768]{1,0:T(8,128)(2,1)S(1)}, u32[]{:S(2)}) copy-start(bf16[768,768]{1,0:T(8,128)(2,1)S(1)} %get-tuple-element.151.synth_ref) | copy-start | bytes 3538948
  99.6 69.8 %collective-permute-start.5 = (bf16[1,8,192,256]{3,2,1,0:T(8,128)(2,1)}, bf16[1,8,192,256]{3,2,1,0:T(8,128)(2,1)S(1)}, u32[]{:S(2)}, u32[]{:S(2)}) collective-permute-start(bf16[1,8,192,256]{3,2,1,0:T(8,128)(2,1)} %get-tuple-element.89), channel_id=1, source_target_pairs={{0,24},{8,0},{16,8},{24,16},{1,25},{9,1},{17,9},{25,17},{2,26},{10... | collective-permute-start | bytes 2359304 | tf_op jit(solution)/shard_map/ppermute | solution.py:507
  102.5 134.8 %collective-permute-start.6 = (bf16[1,8,192,256]{3,2,1,0:T(8,128)(2,1)}, bf16[1,8,192,256]{3,2,1,0:T(8,128)(2,1)S(1)}, u32[]{:S(2)}, u32[]{:S(2)}) collective-permute-start(bf16[1,8,192,256]{3,2,1,0:T(8,128)(2,1)} %get-tuple-element.92), channel_id=1, source_target_pairs={{0,8},{8,16},{16,24},{24,0},{1,9},{9,17},{17,25},{25,1},{2,10},{10... | collective-permute-start | bytes 2359304 | tf_op jit(solution)/shard_map/ppermute | solution.py:507
  103.1 134.2 %collective-permute-start.7 = (bf16[1,8,192,256]{3,2,1,0:T(8,128)(2,1)}, bf16[1,8,192,256]{3,2,1,0:T(8,128)(2,1)S(1)}, u32[]{:S(2)}, u32[]{:S(2)}) collective-permute-start(bf16[1,8,192,256]{3,2,1,0:T(8,128)(2,1)} %get-tuple-element.93), channel_id=1, source_target_pairs={{0,16},{8,24},{16,0},{24,8},{1,17},{9,25},{17,1},{25,9},{2,18},{10... | collective-permute-start | bytes 2359304 | tf_op jit(solution)/shard_map/ppermute | solution.py:507
  119.6 103.6 %copy-start.31 = (bf16[1,8,192,256]{3,2,1,0:T(8,128)(2,1)S(1)}, bf16[1,8,192,256]{3,2,1,0:T(8,128)(2,1)}, u32[]{:S(2)}) copy-start(bf16[1,8,192,256]{3,2,1,0:T(8,128)(2,1)} %copy-done.30) | copy-start | bytes 2359300
  132.6 341.9 %copy-start.21 = (bf16[2,8,192,256]{3,2,1,0:T(8,128)(2,1)}, bf16[2,8,192,256]{3,2,1,0:T(8,128)(2,1)S(1)}, u32[]{:S(2)}) copy-start(bf16[2,8,192,256]{3,2,1,0:T(8,128)(2,1)S(1)} %get-tuple-element.96.refs_0_.refs_4_) | copy-start | bytes 4718596
  132.6 124.9 %collective-permute-start.8 = (bf16[1,8,192,256]{3,2,1,0:T(8,128)(2,1)}, bf16[1,8,192,256]{3,2,1,0:T(8,128)(2,1)S(1)}, u32[]{:S(2)}, u32[]{:S(2)}) collective-permute-start(bf16[1,8,192,256]{3,2,1,0:T(8,128)(2,1)} %get-tuple-element.94), channel_id=1, source_target_pairs={{0,24},{8,0},{16,8},{24,16},{1,25},{9,1},{17,9},{25,17},{2,26},{10... | collective-permute-start | bytes 2359304 | tf_op jit(solution)/shard_map/ppermute | solution.py:507
  169.4 151.6 %collective-permute-start.10 = (bf16[2,8,192,256]{3,2,1,0:T(8,128)(2,1)}, bf16[2,8,192,256]{3,2,1,0:T(8,128)(2,1)S(1)}, u32[]{:S(2)}, u32[]{:S(2)}) collective-permute-start(bf16[2,8,192,256]{3,2,1,0:T(8,128)(2,1)} %get-tuple-element.98), channel_id=1, source_target_pairs={{0,16},{8,24},{16,0},{24,8},{1,17},{9,25},{17,1},{25,9},{2,18},{10... | collective-permute-start | bytes 4718600 | tf_op jit(solution)/shard_map/ppermute | solution.py:507
  169.4 219.0 %collective-permute-start.11 = (bf16[2,8,192,256]{3,2,1,0:T(8,128)(2,1)}, bf16[2,8,192,256]{3,2,1,0:T(8,128)(2,1)S(1)}, u32[]{:S(2)}, u32[]{:S(2)}) collective-permute-start(bf16[2,8,192,256]{3,2,1,0:T(8,128)(2,1)} %get-tuple-element.99), channel_id=1, source_target_pairs={{0,8},{8,16},{16,24},{24,0},{1,9},{9,17},{17,25},{25,1},{2,10},{10... | collective-permute-start | bytes 4718600 | tf_op jit(solution)/shard_map/ppermute | solution.py:507
  223.2 34.3 %copy-start.33 = (bf16[1,8,192,256]{3,2,1,0:T(8,128)(2,1)S(1)}, bf16[1,8,192,256]{3,2,1,0:T(8,128)(2,1)}, u32[]{:S(2)}) copy-start(bf16[1,8,192,256]{3,2,1,0:T(8,128)(2,1)} %copy-done.32) | copy-start | bytes 2359300
  237.3 153.9 %collective-permute-start.9 = (bf16[2,8,192,256]{3,2,1,0:T(8,128)(2,1)}, bf16[2,8,192,256]{3,2,1,0:T(8,128)(2,1)S(1)}, u32[]{:S(2)}, u32[]{:S(2)}) collective-permute-start(bf16[2,8,192,256]{3,2,1,0:T(8,128)(2,1)} %get-tuple-element.97), channel_id=1, source_target_pairs={{0,24},{8,0},{16,8},{24,16},{1,25},{9,1},{17,9},{25,17},{2,26},{10... | collective-permute-start | bytes 4718600 | tf_op jit(solution)/shard_map/ppermute | solution.py:507
  237.3 267.0 %collective-permute-start.12 = (bf16[2,8,192,256]{3,2,1,0:T(8,128)(2,1)}, bf16[2,8,192,256]{3,2,1,0:T(8,128)(2,1)}, u32[]{:S(2)}, u32[]{:S(2)}) collective-permute-start(bf16[2,8,192,256]{3,2,1,0:T(8,128)(2,1)} %get-tuple-element.103), channel_id=1, source_target_pairs={{0,24},{8,0},{16,8},{24,16},{1,25},{9,1},{17,9},{25,17},{2,26},{10... | collective-permute-start | bytes 4718600 | tf_op jit(solution)/shard_map/ppermute | solution.py:507
  257.5 299.6 %collective-permute-start.13 = (bf16[2,8,192,256]{3,2,1,0:T(8,128)(2,1)}, bf16[2,8,192,256]{3,2,1,0:T(8,128)(2,1)}, u32[]{:S(2)}, u32[]{:S(2)}) collective-permute-start(bf16[2,8,192,256]{3,2,1,0:T(8,128)(2,1)} %get-tuple-element.104), channel_id=1, source_target_pairs={{0,16},{8,24},{16,0},{24,8},{1,17},{9,25},{17,1},{25,9},{2,18},{10... | collective-permute-start | bytes 4718600 | tf_op jit(solution)/shard_map/ppermute | solution.py:507
  321.0 153.5 %copy-start.4 = (bf16[2,8,192,256]{3,2,1,0:T(8,128)(2,1)}, bf16[2,8,192,256]{3,2,1,0:T(8,128)(2,1)S(1)}, u32[]{:S(2)}) copy-start(bf16[2,8,192,256]{3,2,1,0:T(8,128)(2,1)S(1)} %collective-permute-done.10.refs_2_.refs_6_) | copy-start | bytes 4718596
  321.0 236.1 %collective-permute-start.14 = (bf16[2,8,192,256]{3,2,1,0:T(8,128)(2,1)}, bf16[2,8,192,256]{3,2,1,0:T(8,128)(2,1)}, u32[]{:S(2)}, u32[]{:S(2)}) collective-permute-start(bf16[2,8,192,256]{3,2,1,0:T(8,128)(2,1)} %get-tuple-element.105), channel_id=1, source_target_pairs={{0,8},{8,16},{16,24},{24,0},{1,9},{9,17},{17,25},{25,1},{2,10},{10... | collective-permute-start | bytes 4718600 | tf_op jit(solution)/shard_map/ppermute | solution.py:507
  388.4 86.2 %copy-start.47 = (bf16[2,8,192,256]{3,2,1,0:T(8,128)(2,1)}, bf16[2,8,192,256]{3,2,1,0:T(8,128)(2,1)S(1)}, u32[]{:S(2)}) copy-start(bf16[2,8,192,256]{3,2,1,0:T(8,128)(2,1)S(1)} %collective-permute-done.11.refs_3_.refs_5_) | copy-start | bytes 4718596
  388.4 199.5 %collective-permute-start.15 = (bf16[2,8,192,256]{3,2,1,0:T(8,128)(2,1)}, bf16[2,8,192,256]{3,2,1,0:T(8,128)(2,1)}, u32[]{:S(2)}, u32[]{:S(2)}) collective-permute-start(bf16[2,8,192,256]{3,2,1,0:T(8,128)(2,1)} %get-tuple-element.110), channel_id=1, source_target_pairs={{0,24},{8,0},{16,8},{24,16},{1,25},{9,1},{17,9},{25,17},{2,26},{10... | collective-permute-start | bytes 4718600 | tf_op jit(solution)/shard_map/ppermute | solution.py:507
  391.2 98.0 %copy-start.6 = (bf16[2,8,192,256]{3,2,1,0:T(8,128)(2,1)}, bf16[2,8,192,256]{3,2,1,0:T(8,128)(2,1)S(1)}, u32[]{:S(2)}) copy-start(bf16[2,8,192,256]{3,2,1,0:T(8,128)(2,1)S(1)} %collective-permute-done.9.refs_1_.refs_7_) | copy-start | bytes 4718596
  391.2 267.0 %collective-permute-start.16 = (bf16[2,8,192,256]{3,2,1,0:T(8,128)(2,1)}, bf16[2,8,192,256]{3,2,1,0:T(8,128)(2,1)}, u32[]{:S(2)}, u32[]{:S(2)}) collective-permute-start(bf16[2,8,192,256]{3,2,1,0:T(8,128)(2,1)} %get-tuple-element.111), channel_id=1, source_target_pairs={{0,16},{8,24},{16,0},{24,8},{1,17},{9,25},{17,1},{25,9},{2,18},{10... | collective-permute-start | bytes 4718600 | tf_op jit(solution)/shard_map/ppermute | solution.py:507
  489.2 94.2 %all-to-all-start = ((bf16[8,48,8,512]{3,2,1,0:T(8,128)(2,1)}), bf16[8,48,8,512]{3,2,1,0:T(8,128)(2,1)}, u32[]{:S(2)}, u32[]{:S(2)}) async-start(bf16[8,48,8,512]{3,2,1,0:T(8,128)(2,1)} %get-tuple-element.108), calls=%async_computation | async-start | bytes 6291456 | tf_op jit(solution)/shard_map/all_to_all | solution.py:613
  495.1 63.8 %copy-start.17 = (bf16[768,768]{1,0:T(8,128)(2,1)S(1)}, bf16[768,768]{1,0:T(8,128)(2,1)}, u32[]{:S(2)}) copy-start(bf16[768,768]{1,0:T(8,128)(2,1)} %copy-done.16) | copy-start | bytes 3538948
  495.1 63.8 %copy-start.25 = (bf16[2,8,192,256]{3,2,1,0:T(8,128)(2,1)S(1)}, bf16[2,8,192,256]{3,2,1,0:T(8,128)(2,1)}, u32[]{:S(2)}) copy-start(bf16[2,8,192,256]{3,2,1,0:T(8,128)(2,1)} %copy-done.24) | copy-start | bytes 4718596
  504.3 69.3 %copy-start.34 = (bf16[1,8,192,256]{3,2,1,0:T(8,128)(2,1)}, bf16[1,8,192,256]{3,2,1,0:T(8,128)(2,1)S(1)}, u32[]{:S(2)}) copy-start(bf16[1,8,192,256]{3,2,1,0:T(8,128)(2,1)S(1)} %get-tuple-element.115.refs_0_.refs_4_) | copy-start | bytes 2359300
  504.3 154.1 %collective-permute-start.17 = (bf16[2,8,192,256]{3,2,1,0:T(8,128)(2,1)}, bf16[2,8,192,256]{3,2,1,0:T(8,128)(2,1)}, u32[]{:S(2)}, u32[]{:S(2)}) collective-permute-start(bf16[2,8,192,256]{3,2,1,0:T(8,128)(2,1)} %get-tuple-element.112), channel_id=1, source_target_pairs={{0,8},{8,16},{16,24},{24,0},{1,9},{9,17},{17,25},{25,1},{2,10},{10... | collective-permute-start | bytes 4718600 | tf_op jit(solution)/shard_map/ppermute | solution.py:507
  557.1 119.0 %collective-permute-start.18 = (bf16[1,8,192,256]{3,2,1,0:T(8,128)(2,1)}, bf16[1,8,192,256]{3,2,1,0:T(8,128)(2,1)}, u32[]{:S(2)}, u32[]{:S(2)}) collective-permute-start(bf16[1,8,192,256]{3,2,1,0:T(8,128)(2,1)} %get-tuple-element.116), channel_id=1, source_target_pairs={{0,24},{8,0},{16,8},{24,16},{1,25},{9,1},{17,9},{25,17},{2,26},{10... | collective-permute-start | bytes 2359304 | tf_op jit(solution)/shard_map/ppermute | solution.py:507
  557.1 168.5 %collective-permute-start.19 = (bf16[1,8,192,256]{3,2,1,0:T(8,128)(2,1)}, bf16[1,8,192,256]{3,2,1,0:T(8,128)(2,1)}, u32[]{:S(2)}, u32[]{:S(2)}) collective-permute-start(bf16[1,8,192,256]{3,2,1,0:T(8,128)(2,1)} %get-tuple-element.117), channel_id=1, source_target_pairs={{0,16},{8,24},{16,0},{24,8},{1,17},{9,25},{17,1},{25,9},{2,18},{10... | collective-permute-start | bytes 2359304 | tf_op jit(solution)/shard_map/ppermute | solution.py:507
  583.4 93.0 %all-to-all-start.1 = ((bf16[8,48,8,512]{3,2,1,0:T(8,128)(2,1)}), bf16[8,48,8,512]{3,2,1,0:T(8,128)(2,1)}, u32[]{:S(2)}, u32[]{:S(2)}) async-start(bf16[8,48,8,512]{3,2,1,0:T(8,128)(2,1)} %get-tuple-element.114), calls=%async_computation.1 | async-start | bytes 6291456 | tf_op jit(solution)/shard_map/all_to_all | solution.py:613
  587.9 137.7 %collective-permute-start.20 = (bf16[1,8,192,256]{3,2,1,0:T(8,128)(2,1)}, bf16[1,8,192,256]{3,2,1,0:T(8,128)(2,1)S(1)}, u32[]{:S(2)}, u32[]{:S(2)}) collective-permute-start(bf16[1,8,192,256]{3,2,1,0:T(8,128)(2,1)} %get-tuple-element.118), channel_id=1, source_target_pairs={{0,8},{8,16},{16,24},{24,0},{1,9},{9,17},{17,25},{25,1},{2,10},{10... | collective-permute-start | bytes 2359304 | tf_op jit(solution)/shard_map/ppermute | solution.py:507
  658.2 102.5 %collective-permute-start.21 = (bf16[1,8,192,256]{3,2,1,0:T(8,128)(2,1)}, bf16[1,8,192,256]{3,2,1,0:T(8,128)(2,1)}, u32[]{:S(2)}, u32[]{:S(2)}) collective-permute-start(bf16[1,8,192,256]{3,2,1,0:T(8,128)(2,1)} %get-tuple-element.123), channel_id=1, source_target_pairs={{0,24},{8,0},{16,8},{24,16},{1,25},{9,1},{17,9},{25,17},{2,26},{10... | collective-permute-start | bytes 2359304 | tf_op jit(solution)/shard_map/ppermute | solution.py:507
  658.4 104.3 %collective-permute-start.22 = (bf16[1,8,192,256]{3,2,1,0:T(8,128)(2,1)}, bf16[1,8,192,256]{3,2,1,0:T(8,128)(2,1)}, u32[]{:S(2)}, u32[]{:S(2)}) collective-permute-start(bf16[1,8,192,256]{3,2,1,0:T(8,128)(2,1)} %get-tuple-element.124), channel_id=1, source_target_pairs={{0,16},{8,24},{16,0},{24,8},{1,17},{9,25},{17,1},{25,9},{2,18},{10... | collective-permute-start | bytes 2359304 | tf_op jit(solution)/shard_map/ppermute | solution.py:507
  676.1 86.6 %collective-permute-start.23 = (bf16[1,8,192,256]{3,2,1,0:T(8,128)(2,1)}, bf16[1,8,192,256]{3,2,1,0:T(8,128)(2,1)S(1)}, u32[]{:S(2)}, u32[]{:S(2)}) collective-permute-start(bf16[1,8,192,256]{3,2,1,0:T(8,128)(2,1)} %get-tuple-element.125), channel_id=1, source_target_pairs={{0,8},{8,16},{16,24},{24,0},{1,9},{9,17},{17,25},{25,1},{2,10},{10... | collective-permute-start | bytes 2359304 | tf_op jit(solution)/shard_map/ppermute | solution.py:507
  676.5 66.5 %all-to-all-start.2 = ((bf16[8,48,8,512]{3,2,1,0:T(8,128)(2,1)}), bf16[8,48,8,512]{3,2,1,0:T(8,128)(2,1)}, u32[]{:S(2)}, u32[]{:S(2)}) async-start(bf16[8,48,8,512]{3,2,1,0:T(8,128)(2,1)} %get-tuple-element.120), calls=%async_computation.2 | async-start | bytes 6291456 | tf_op jit(solution)/shard_map/all_to_all | solution.py:613
  725.6 17.3 %copy-start.8 = (bf16[1,8,192,256]{3,2,1,0:T(8,128)(2,1)}, bf16[1,8,192,256]{3,2,1,0:T(8,128)(2,1)S(1)}, u32[]{:S(2)}) copy-start(bf16[1,8,192,256]{3,2,1,0:T(8,128)(2,1)S(1)} %collective-permute-done.20.refs_3_.refs_7_) | copy-start | bytes 2359300
  742.9 42.4 %all-to-all-start.3 = ((bf16[8,48,8,512]{3,2,1,0:T(8,128)(2,1)}), bf16[8,48,8,512]{3,2,1,0:T(8,128)(2,1)}, u32[]{:S(2)}, u32[]{:S(2)}) async-start(bf16[8,48,8,512]{3,2,1,0:T(8,128)(2,1)} %get-tuple-element.127), calls=%async_computation.3 | async-start | bytes 6291456 | tf_op jit(solution)/shard_map/all_to_all | solution.py:613
  748.8 13.9 %copy-start.19 = (bf16[768,768]{1,0:T(8,128)(2,1)S(1)}, bf16[768,768]{1,0:T(8,128)(2,1)}, u32[]{:S(2)}) copy-start(bf16[768,768]{1,0:T(8,128)(2,1)} %copy-done.16) | copy-start | bytes 3538948
  748.8 13.9 %copy-start.38 = (bf16[1,8,192,256]{3,2,1,0:T(8,128)(2,1)S(1)}, bf16[1,8,192,256]{3,2,1,0:T(8,128)(2,1)}, u32[]{:S(2)}) copy-start(bf16[1,8,192,256]{3,2,1,0:T(8,128)(2,1)} %copy-done.37) | copy-start | bytes 2359300
  758.9 31.2 %collective-permute-start.24 = (bf16[1,8,192,256]{3,2,1,0:T(8,128)(2,1)}, bf16[1,8,192,256]{3,2,1,0:T(8,128)(2,1)S(1)}, u32[]{:S(2)}, u32[]{:S(2)}) collective-permute-start(bf16[1,8,192,256]{3,2,1,0:T(8,128)(2,1)} %get-tuple-element.129), channel_id=1, source_target_pairs={{0,24},{8,0},{16,8},{24,16},{1,25},{9,1},{17,9},{25,17},{2,26},{10... | collective-permute-start | bytes 2359304 | tf_op jit(solution)/shard_map/ppermute | solution.py:507
  758.9 70.7 %collective-permute-start.25 = (bf16[1,8,192,256]{3,2,1,0:T(8,128)(2,1)}, bf16[1,8,192,256]{3,2,1,0:T(8,128)(2,1)}, u32[]{:S(2)}, u32[]{:S(2)}) collective-permute-start(bf16[1,8,192,256]{3,2,1,0:T(8,128)(2,1)} %get-tuple-element.130), channel_id=1, source_target_pairs={{0,16},{8,24},{16,0},{24,8},{1,17},{9,25},{17,1},{25,9},{2,18},{10... | collective-permute-start | bytes 2359304 | tf_op jit(solution)/shard_map/ppermute | solution.py:507
  760.7 68.9 %collective-permute-start.26 = (bf16[1,8,192,256]{3,2,1,0:T(8,128)(2,1)}, bf16[1,8,192,256]{3,2,1,0:T(8,128)(2,1)}, u32[]{:S(2)}, u32[]{:S(2)}) collective-permute-start(bf16[1,8,192,256]{3,2,1,0:T(8,128)(2,1)} %get-tuple-element.131), channel_id=1, source_target_pairs={{0,8},{8,16},{16,24},{24,0},{1,9},{9,17},{17,25},{25,1},{2,10},{10... | collective-permute-start | bytes 2359304 | tf_op jit(solution)/shard_map/ppermute | solution.py:507
  762.7 14.9 %copy-start.10 = (bf16[1,8,192,256]{3,2,1,0:T(8,128)(2,1)}, bf16[1,8,192,256]{3,2,1,0:T(8,128)(2,1)S(1)}, u32[]{:S(2)}) copy-start(bf16[1,8,192,256]{3,2,1,0:T(8,128)(2,1)S(1)} %collective-permute-done.23.refs_3_) | copy-start | bytes 2359300
  785.3 44.3 %copy-start.20 = (bf16[768,768]{1,0:T(8,128)(2,1)S(1)}, bf16[768,768]{1,0:T(8,128)(2,1)}, u32[]{:S(2)}) copy-start(bf16[768,768]{1,0:T(8,128)(2,1)} %copy-done.16) | copy-start | bytes 3538948
  785.3 60.0 %all-to-all-start.4 = ((bf16[8,48,8,512]{3,2,1,0:T(8,128)(2,1)}), bf16[8,48,8,512]{3,2,1,0:T(8,128)(2,1)}, u32[]{:S(2)}, u32[]{:S(2)}) async-start(bf16[8,48,8,512]{3,2,1,0:T(8,128)(2,1)} %get-tuple-element.133), calls=%async_computation.4 | async-start | bytes 6291456 | tf_op jit(solution)/shard_map/all_to_all | solution.py:613
  790.1 55.2 %copy-start.12 = (bf16[1,8,192,256]{3,2,1,0:T(8,128)(2,1)}, bf16[1,8,192,256]{3,2,1,0:T(8,128)(2,1)S(1)}, u32[]{:S(2)}) copy-start(bf16[1,8,192,256]{3,2,1,0:T(8,128)(2,1)S(1)} %collective-permute-done.24.refs_1_.refs_5_) | copy-start | bytes 2359300
  845.3 4.7 copy-start.46
  845.3 41.8 %all-to-all-start.5 = ((bf16[8,48,8,512]{3,2,1,0:T(8,128)(2,1)}), bf16[8,48,8,512]{3,2,1,0:T(8,128)(2,1)S(1)}, u32[]{:S(2)}, u32[]{:S(2)}) async-start(bf16[8,48,8,512]{3,2,1,0:T(8,128)(2,1)} %after.1), calls=%async_computation.5 | async-start | bytes 6291456 | tf_op jit(solution)/shard_map/all_to_all | solution.py:613
  887.1 1.6 copy-start.43
  914.5 4.9 copy-start.45
  914.5 76.5 %all-to-all-start.6 = ((bf16[8,48,16,512]{3,2,1,0:T(8,128)(2,1)}), bf16[8,48,16,512]{3,2,1,0:T(8,128)(2,1)}, u32[]{:S(2)}, u32[]{:S(2)}) async-start(bf16[8,48,16,512]{3,2,1,0:T(8,128)(2,1)} %get-tuple-element.136), calls=%async_computation.6 | async-start | bytes 12582912 | tf_op jit(solution)/shard_map/all_to_all | solution.py:624
  991.0 5.0 copy-start.5
  991.0 5.1 copy-start.7
  991.0 76.6 %all-to-all-start.8 = ((bf16[8,48,16,512]{3,2,1,0:T(8,128)(2,1)}), bf16[8,48,16,512]{3,2,1,0:T(8,128)(2,1)}, u32[]{:S(2)}, u32[]{:S(2)}) async-start(bf16[8,48,16,512]{3,2,1,0:T(8,128)(2,1)} %get-tuple-element.141), calls=%async_computation.8 | async-start | bytes 12582912 | tf_op jit(solution)/shard_map/all_to_all | solution.py:628
  1067.7 5.1 copy-start.9
  1067.7 5.2 copy-start.15
  1067.7 76.7 %all-to-all-start.7 = ((bf16[8,48,16,512]{3,2,1,0:T(8,128)(2,1)}), bf16[8,48,16,512]{3,2,1,0:T(8,128)(2,1)}, u32[]{:S(2)}, u32[]{:S(2)}) async-start(bf16[8,48,16,512]{3,2,1,0:T(8,128)(2,1)} %get-tuple-element.140), calls=%async_computation.7 | async-start | bytes 12582912 | tf_op jit(solution)/shard_map/all_to_all | solution.py:628
  1075.4 69.0 %copy-start.11 = (bf16[1,8,192,256]{3,2,1,0:T(8,128)(2,1)S(1)}, bf16[1,8,192,256]{3,2,1,0:T(8,128)(2,1)}, u32[]{:S(2)}) copy-start(bf16[1,8,192,256]{3,2,1,0:T(8,128)(2,1)} %copy-done.10) | copy-start | bytes 2359300
  1075.4 69.0 %copy-start.13 = (bf16[1,8,192,256]{3,2,1,0:T(8,128)(2,1)S(1)}, bf16[1,8,192,256]{3,2,1,0:T(8,128)(2,1)}, u32[]{:S(2)}) copy-start(bf16[1,8,192,256]{3,2,1,0:T(8,128)(2,1)} %copy-done.12) | copy-start | bytes 2359300
  (20 other events, 23.4 us)
